TPU v7x, 512 devices: a whole 4x4x16 slice. The times are simulated.
512 devices in a mesh: gx: 16 (over z), gy: 8 (over y, core), gz: 4 (over x).
Axes of the slice: x: 4, y: 4, z: 16, core: 2. Of those that a mesh axis runs over, the one named last changes fastest.
Arguments:
- pressure_source: float32 [128, 128, 512], P('gx', 'gy', 'gz'), may hold values from -40 to 40
- conductivity: float32 [128, 128, 512], P('gx', 'gy', 'gz'), may hold values from 0.25 to 4
Outputs:
- pressure: float32 [128, 128, 512], P('gx', 'gy', 'gz')
All inputs are finite; a program needn't handle non-finite values.
Results may differ from a plain program's by a relative error of at most 0.0001.
Values sent between devices are 32-bit elements; how exact they have to be, the bound alone decides.
A program may use at most 64 MiB of HBM per device.

v0:
```python
import jax
import jax.numpy as jnp
from jax import lax
from jax.sharding import PartitionSpec as P

LEVELS = 4
DEGREE = 3


center_value = 1.125
radius_value = 0.875


def padded_2(cells, sides, width):
    for axis, dim in sides:
        count = lax.axis_size(axis)
        head = lax.slice_in_dim(cells, 0, width, axis=dim)
        tail = lax.slice_in_dim(cells, cells.shape[dim] - width, cells.shape[dim], axis=dim)
        cells = jnp.concatenate(
            [
                lax.ppermute(tail, axis, [(i, (i + 1) % count) for i in range(count)]),
                cells,
                lax.ppermute(head, axis, [((i + 1) % count, i) for i in range(count)]),
            ],
            axis=dim,
        )
    return cells


def pad_bricks(field_in):
    return padded_2(field_in, (("gx", 0), ("gy", 1), ("gz", 2)), 1)


def harmonic(one_side, other_side):
    return 2.0 * one_side * other_side / (one_side + other_side)


def fine_faces(padded):
    middle = padded[1:-1, 1:-1, 1:-1]
    return jnp.stack(
        [
            harmonic(middle, padded[:-2, 1:-1, 1:-1]),
            harmonic(middle, padded[1:-1, :-2, 1:-1]),
            harmonic(middle, padded[1:-1, 1:-1, :-2]),
            harmonic(middle, padded[2:, 1:-1, 1:-1]),
            harmonic(middle, padded[1:-1, 2:, 1:-1]),
            harmonic(middle, padded[1:-1, 1:-1, 2:]),
        ]
    )


def apply_operator(padded, face_terms):
    middle = padded[1:-1, 1:-1, 1:-1]
    result = face_terms[0] * (middle - padded[:-2, 1:-1, 1:-1]) + face_terms[3] * (
        middle - padded[2:, 1:-1, 1:-1]
    )
    result = (
        result
        + face_terms[1] * (middle - padded[1:-1, :-2, 1:-1])
        + face_terms[4] * (middle - padded[1:-1, 2:, 1:-1])
    )
    result = (
        result
        + face_terms[2] * (middle - padded[1:-1, 1:-1, :-2])
        + face_terms[5] * (middle - padded[1:-1, 1:-1, 2:])
    )
    return result


def inverse_diagonal(face_terms):
    return 1.0 / (
        face_terms[0]
        + face_terms[3]
        + (face_terms[1] + face_terms[4])
        + (face_terms[2] + face_terms[5])
    )


def coarsen_faces(face_terms):
    size_x = face_terms.shape[1] // 2
    size_y = face_terms.shape[2] // 2
    size_z = face_terms.shape[3] // 2
    blocks = face_terms.reshape(6, size_x, 2, size_y, 2, size_z, 2)
    return 0.125 * jnp.stack(
        [
            blocks[0][:, 0].sum(axis=(2, 4)),
            blocks[1][:, :, :, 0].sum(axis=(1, 4)),
            blocks[2][..., 0].sum(axis=(1, 3)),
            blocks[3][:, 1].sum(axis=(2, 4)),
            blocks[4][:, :, :, 1].sum(axis=(1, 4)),
            blocks[5][..., 1].sum(axis=(1, 3)),
        ]
    )


def restrict(field_in):
    size_x, size_y, size_z = field_in.shape
    blocks = field_in.reshape(size_x // 2, 2, size_y // 2, 2, size_z // 2, 2)
    return blocks.sum(axis=(1, 3, 5)) * 0.125


def prolong(field_in):
    size_x, size_y, size_z = field_in.shape
    spread = jnp.broadcast_to(
        field_in[:, None, :, None, :, None], (size_x, 2, size_y, 2, size_z, 2)
    )
    return spread.reshape(2 * size_x, 2 * size_y, 2 * size_z)


def chebyshev(right_side, start, residual, face_terms, inverse, pad_field):
    ratio = center_value / radius_value
    rho_old = 1.0 / ratio
    direction = inverse * residual / center_value
    estimate = direction if start is None else start + direction
    for step_index in range(DEGREE - 1):
        residual = right_side - apply_operator(pad_field(estimate), face_terms)
        rho_new = 1.0 / (2.0 * ratio - rho_old)
        direction = (
            rho_new * rho_old * direction + 2.0 * rho_new / radius_value * inverse * residual
        )
        estimate = estimate + direction
        rho_old = rho_new
    return estimate


def shards(pressure_source, conductivity):

    def pad_for():
        return pad_bricks

    face_terms = fine_faces(pad_bricks(conductivity))
    right_side = pressure_source
    saved = []
    for level_index in range(LEVELS - 1):
        pad_field = pad_for()
        inverse = inverse_diagonal(face_terms)
        estimate = chebyshev(right_side, None, right_side, face_terms, inverse, pad_field)
        residual = right_side - apply_operator(pad_field(estimate), face_terms)
        saved.append((right_side, face_terms, inverse, estimate, residual))
        regroup_face_terms = coarsen_faces(face_terms)
        right_side = restrict(residual)
        face_terms = regroup_face_terms
    correction = chebyshev(
        right_side, None, right_side, face_terms, inverse_diagonal(face_terms), pad_for()
    )
    for level_index in range(LEVELS - 2, -1, -1):
        right_side, face_terms, inverse, estimate, residual = saved[level_index]
        estimate = estimate + prolong(correction)
        residual = right_side - apply_operator(pad_for()(estimate), face_terms)
        correction = chebyshev(right_side, estimate, residual, face_terms, inverse, pad_for())
    return correction


def solution(mesh):
    placed = (P("gx", "gy", "gz"), P("gx", "gy", "gz"))
    return jax.shard_map(
        shards, mesh=mesh, in_specs=placed, out_specs=P("gx", "gy", "gz"), check_vma=False
    )
```

profile of v0, /device:TPU:1, one launch (start us, length us, event | category | flops | bytes accessed | tf_op | source)
XLA Modules:
  0.0 556.4 jit_solution(16178875244825844580)
XLA Ops:
  0.7 4.4 collective-permute-start
  5.1 9.5 %collective-permute-start.1 = (f32[1,16,128]{2,1,0:T(8,128)S(1)}, f32[1,16,128]{2,1,0:T(8,128)S(1)}, u32[]{:S(2)}, u32[]{:S(2)}) collective-permute-start(f32[1,16,128]{2,1,0:T(8,128)S(1)} %get-tuple-element.83), channel_id=1, source_target_pairs={{32,0},{64,32},{96,64},{128,96},{160,128},{192,160},{224,192},{256... | collective-permute-start | bytes 24584 | tf_op jit(solution)/shard_map/ppermute | solution.py:23
  19.5 4.4 collective-permute-start.5
  25.9 4.9 collective-permute-done.4
  31.9 5.1 collective-permute-start.7
  38.9 5.5 squeeze.72
  46.4 5.5 squeeze.73
  53.9 5.5 squeeze.74
  62.0 5.5 squeeze.75
  69.4 5.5 squeeze.76
  76.9 5.5 squeeze.77
  82.4 3.7 slice_reduce_fusion
  88.1 4.8 collective-permute-start.9
  96.1 3.5 collective-permute-start.10
  103.1 4.9 collective-permute-start.13
  110.0 3.5 collective-permute-done.12
  113.6 5.7 %collective-permute-start.15 = (f32[10,1,128]{2,1,0:T(1,128)S(1)}, f32[10,1,128]{2,1,0:T(1,128)S(1)}, u32[]{:S(2)}, u32[]{:S(2)}) collective-permute-start(f32[10,1,128]{2,1,0:T(1,128)S(1)} %get-tuple-element.65), channel_id=1, source_target_pairs={{4,0},{8,4},{12,8},{16,12},{20,16},{24,20},{28,24},{0,28},{5,1},{9... | collective-permute-start | bytes 15368 | tf_op jit(solution)/shard_map/ppermute | solution.py:23
  122.5 3.4 collective-permute-start.16
  131.5 3.4 collective-permute-start.18
  137.2 5.4 collective-permute-start.21
  145.8 3.4 collective-permute-start.22
  152.8 5.5 reshape.359
  162.8 3.4 collective-permute-start.24
  168.4 5.6 %collective-permute-start.27 = (f32[6,1,64]{2,1,0:T(1,128)S(1)}, f32[6,1,64]{2,1,0:T(1,128)S(1)}, u32[]{:S(2)}, u32[]{:S(2)}) collective-permute-start(f32[6,1,64]{2,1,0:T(1,128)S(1)} %get-tuple-element.113), channel_id=1, source_target_pairs={{4,0},{8,4},{12,8},{16,12},{20,16},{24,20},{28,24},{0,28},{5,1},{9... | collective-permute-start | bytes 4616 | tf_op jit(solution)/shard_map/ppermute | solution.py:23
  192.6 6.0 %collective-permute-start.33 = (f32[6,1,64]{2,1,0:T(1,128)S(1)}, f32[6,1,64]{2,1,0:T(1,128)S(1)}, u32[]{:S(2)}, u32[]{:S(2)}) collective-permute-start(f32[6,1,64]{2,1,0:T(1,128)S(1)} %get-tuple-element.111), channel_id=1, source_target_pairs={{4,0},{8,4},{12,8},{16,12},{20,16},{24,20},{28,24},{0,28},{5,1},{9... | collective-permute-start | bytes 4616 | tf_op jit(solution)/shard_map/ppermute | solution.py:23
  201.7 3.4 collective-permute-start.34
  215.9 5.7 %collective-permute-start.39 = (f32[6,1,64]{2,1,0:T(1,128)S(1)}, f32[6,1,64]{2,1,0:T(1,128)S(1)}, u32[]{:S(2)}, u32[]{:S(2)}) collective-permute-start(f32[6,1,64]{2,1,0:T(1,128)S(1)} %get-tuple-element.109), channel_id=1, source_target_pairs={{4,0},{8,4},{12,8},{16,12},{20,16},{24,20},{28,24},{0,28},{5,1},{9... | collective-permute-start | bytes 4616 | tf_op jit(solution)/shard_map/ppermute | solution.py:23
  224.8 3.4 collective-permute-start.40
  233.5 3.4 collective-permute-start.42
  239.1 5.4 collective-permute-start.45
  247.6 3.4 collective-permute-start.46
  255.4 3.4 collective-permute-start.48
  260.9 5.6 %collective-permute-start.51 = (f32[4,1,32]{2,1,0:T(1,128)S(1)}, f32[4,1,32]{2,1,0:T(1,128)S(1)}, u32[]{:S(2)}, u32[]{:S(2)}) collective-permute-start(f32[4,1,32]{2,1,0:T(1,128)S(1)} %get-tuple-element.147), channel_id=1, source_target_pairs={{4,0},{8,4},{12,8},{16,12},{20,16},{24,20},{28,24},{0,28},{5,1},{9... | collective-permute-start | bytes 1544 | tf_op jit(solution)/shard_map/ppermute | solution.py:23
  284.0 6.0 %collective-permute-start.57 = (f32[4,1,32]{2,1,0:T(1,128)S(1)}, f32[4,1,32]{2,1,0:T(1,128)S(1)}, u32[]{:S(2)}, u32[]{:S(2)}) collective-permute-start(f32[4,1,32]{2,1,0:T(1,128)S(1)} %get-tuple-element.145), channel_id=1, source_target_pairs={{4,0},{8,4},{12,8},{16,12},{20,16},{24,20},{28,24},{0,28},{5,1},{9... | collective-permute-start | bytes 1544 | tf_op jit(solution)/shard_map/ppermute | solution.py:23
  293.1 3.4 collective-permute-start.58
  307.1 5.7 %collective-permute-start.63 = (f32[3,1,16]{2,1,0:T(1,128)S(1)}, f32[3,1,16]{2,1,0:T(1,128)S(1)}, u32[]{:S(2)}, u32[]{:S(2)}) collective-permute-start(f32[3,1,16]{2,1,0:T(1,128)S(1)} %get-tuple-element.169), channel_id=1, source_target_pairs={{4,0},{8,4},{12,8},{16,12},{20,16},{24,20},{28,24},{0,28},{5,1},{9... | collective-permute-start | bytes 584 | tf_op jit(solution)/shard_map/ppermute | solution.py:23
  315.9 3.4 collective-permute-start.64
  323.5 3.4 collective-permute-start.66
  329.0 5.4 collective-permute-start.69
  337.6 3.4 collective-permute-start.70
  345.4 3.4 collective-permute-start.72
  350.9 5.6 %collective-permute-start.75 = (f32[4,1,32]{2,1,0:T(1,128)S(1)}, f32[4,1,32]{2,1,0:T(1,128)S(1)}, u32[]{:S(2)}, u32[]{:S(2)}) collective-permute-start(f32[4,1,32]{2,1,0:T(1,128)S(1)} %get-tuple-element.143), channel_id=1, source_target_pairs={{4,0},{8,4},{12,8},{16,12},{20,16},{24,20},{28,24},{0,28},{5,1},{9... | collective-permute-start | bytes 1544 | tf_op jit(solution)/shard_map/ppermute | solution.py:23
  367.9 3.4 collective-permute-start.78
  373.5 5.7 %collective-permute-start.81 = (f32[4,1,32]{2,1,0:T(1,128)S(1)}, f32[4,1,32]{2,1,0:T(1,128)S(1)}, u32[]{:S(2)}, u32[]{:S(2)}) collective-permute-start(f32[4,1,32]{2,1,0:T(1,128)S(1)} %get-tuple-element.141), channel_id=1, source_target_pairs={{4,0},{8,4},{12,8},{16,12},{20,16},{24,20},{28,24},{0,28},{5,1},{9... | collective-permute-start | bytes 1544 | tf_op jit(solution)/shard_map/ppermute | solution.py:23
  382.3 3.4 collective-permute-start.82
  390.1 3.4 collective-permute-start.84
  395.6 5.4 collective-permute-start.87
  404.2 3.4 collective-permute-start.88
  412.3 3.4 collective-permute-start.90
  417.9 5.4 collective-permute-start.93
  426.5 3.4 collective-permute-start.94
  434.6 3.4 collective-permute-start.96
  440.1 5.6 %collective-permute-start.99 = (f32[6,1,64]{2,1,0:T(1,128)S(1)}, f32[6,1,64]{2,1,0:T(1,128)S(1)}, u32[]{:S(2)}, u32[]{:S(2)}) collective-permute-start(f32[6,1,64]{2,1,0:T(1,128)S(1)} %get-tuple-element.99), channel_id=1, source_target_pairs={{4,0},{8,4},{12,8},{16,12},{20,16},{24,20},{28,24},{0,28},{5,1},{9... | collective-permute-start | bytes 4616 | tf_op jit(solution)/shard_map/ppermute | solution.py:23
  457.5 3.4 collective-permute-start.102
  463.1 5.7 %collective-permute-start.105 = (f32[6,1,64]{2,1,0:T(1,128)S(1)}, f32[6,1,64]{2,1,0:T(1,128)S(1)}, u32[]{:S(2)}, u32[]{:S(2)}) collective-permute-start(f32[6,1,64]{2,1,0:T(1,128)S(1)} %get-tuple-element.97), channel_id=1, source_target_pairs={{4,0},{8,4},{12,8},{16,12},{20,16},{24,20},{28,24},{0,28},{5,1},{9... | collective-permute-start | bytes 4616 | tf_op jit(solution)/shard_map/ppermute | solution.py:23
  472.0 3.6 collective-permute-start.106
  480.7 4.0 reshape.362
  486.7 3.4 collective-permute-start.108
  492.3 5.5 collective-permute-start.111
  509.9 3.4 collective-permute-start.114
  515.6 5.4 collective-permute-start.117
  524.2 3.4 collective-permute-start.118
  539.2 5.9 %collective-permute-start.123 = (f32[10,1,128]{2,1,0:T(1,128)S(1)}, f32[10,1,128]{2,1,0:T(1,128)S(1)}, u32[]{:S(2)}, u32[]{:S(2)}) collective-permute-start(f32[10,1,128]{2,1,0:T(1,128)S(1)} %get-tuple-element.57), channel_id=1, source_target_pairs={{4,0},{8,4},{12,8},{16,12},{20,16},{24,20},{28,24},{0,28},{5,1},{9... | collective-permute-start | bytes 15368 | tf_op jit(solution)/shard_map/ppermute | solution.py:23
  552.0 3.6 collective-permute-done.124
  (376 shorter events, 265.5 us)
Async XLA Ops:
  0.7 13.9 %collective-permute-start = (f32[1,16,128]{2,1,0:T(8,128)S(1)}, f32[1,16,128]{2,1,0:T(8,128)S(1)}, u32[]{:S(2)}, u32[]{:S(2)}) collective-permute-start(f32[1,16,128]{2,1,0:T(8,128)S(1)} %get-tuple-element.82), channel_id=1, source_target_pairs={{0,32},{32,64},{64,96},{96,128},{128,160},{160,192},{192,224},{224... | collective-permute-start | bytes 24584 | tf_op jit(solution)/shard_map/ppermute | solution.py:21
  5.1 10.4 %collective-permute-start.1 = (f32[1,16,128]{2,1,0:T(8,128)S(1)}, f32[1,16,128]{2,1,0:T(8,128)S(1)}, u32[]{:S(2)}, u32[]{:S(2)}) collective-permute-start(f32[1,16,128]{2,1,0:T(8,128)S(1)} %get-tuple-element.83), channel_id=1, source_target_pairs={{32,0},{64,32},{96,64},{128,96},{160,128},{192,160},{224,192},{256... | collective-permute-start | bytes 24584 | tf_op jit(solution)/shard_map/ppermute | solution.py:23
  19.5 6.3 %collective-permute-start.5 = (f32[10,18,1]{2,1,0:T(8,128)S(1)}, f32[10,18,1]{2,1,0:T(8,128)S(1)}, u32[]{:S(2)}, u32[]{:S(2)}) collective-permute-start(f32[10,18,1]{2,1,0:T(8,128)S(1)} %get-tuple-element.49), channel_id=1, source_target_pairs={{1,0},{2,1},{3,2},{0,3},{5,4},{6,5},{7,6},{4,7},{9,8},{10,9},{11,1... | collective-permute-start | bytes 2168 | tf_op jit(solution)/shard_map/ppermute | solution.py:23
  23.9 6.8 %collective-permute-start.4 = (f32[10,18,1]{2,1,0:T(8,128)S(1)}, f32[10,18,1]{2,1,0:T(8,128)S(1)}, u32[]{:S(2)}, u32[]{:S(2)}) collective-permute-start(f32[10,18,1]{2,1,0:T(8,128)S(1)} %get-tuple-element.48), channel_id=1, source_target_pairs={{0,1},{1,2},{2,3},{3,0},{4,5},{5,6},{6,7},{7,4},{8,9},{9,10},{10,1... | collective-permute-start | bytes 2168 | tf_op jit(solution)/shard_map/ppermute | solution.py:21
  31.9 56.2 %collective-permute-start.7 = (f32[1,16,128]{2,1,0:T(8,128)S(1)}, f32[1,16,128]{2,1,0:T(8,128)S(1)}, u32[]{:S(2)}, u32[]{:S(2)}) collective-permute-start(f32[1,16,128]{2,1,0:T(8,128)S(1)} %get-tuple-element.81), channel_id=1, source_target_pairs={{32,0},{64,32},{96,64},{128,96},{160,128},{192,160},{224,192},{256... | collective-permute-start | bytes 24584 | tf_op jit(solution)/shard_map/ppermute | solution.py:23
  37.0 51.1 %collective-permute-start.6 = (f32[1,16,128]{2,1,0:T(8,128)S(1)}, f32[1,16,128]{2,1,0:T(8,128)S(1)}, u32[]{:S(2)}, u32[]{:S(2)}) collective-permute-start(f32[1,16,128]{2,1,0:T(8,128)S(1)} %get-tuple-element.80), channel_id=1, source_target_pairs={{0,32},{32,64},{64,96},{96,128},{128,160},{160,192},{192,224},{224... | collective-permute-start | bytes 24584 | tf_op jit(solution)/shard_map/ppermute | solution.py:21
  88.1 5.6 %collective-permute-start.9 = (f32[10,1,128]{2,1,0:T(1,128)S(1)}, f32[10,1,128]{2,1,0:T(1,128)S(1)}, u32[]{:S(2)}, u32[]{:S(2)}) collective-permute-start(f32[10,1,128]{2,1,0:T(1,128)S(1)} %get-tuple-element.67), channel_id=1, source_target_pairs={{4,0},{8,4},{12,8},{16,12},{20,16},{24,20},{28,24},{0,28},{5,1},{9... | collective-permute-start | bytes 15368 | tf_op jit(solution)/shard_map/ppermute | solution.py:23
  94.2 6.0 %collective-permute-start.11 = (f32[10,18,1]{2,1,0:T(8,128)S(1)}, f32[10,18,1]{2,1,0:T(8,128)S(1)}, u32[]{:S(2)}, u32[]{:S(2)}) collective-permute-start(f32[10,18,1]{2,1,0:T(8,128)S(1)} %get-tuple-element.47), channel_id=1, source_target_pairs={{1,0},{2,1},{3,2},{0,3},{5,4},{6,5},{7,6},{4,7},{9,8},{10,9},{11,1... | collective-permute-start | bytes 2168 | tf_op jit(solution)/shard_map/ppermute | solution.py:23
  96.1 6.8 %collective-permute-start.10 = (f32[10,18,1]{2,1,0:T(8,128)S(1)}, f32[10,18,1]{2,1,0:T(8,128)S(1)}, u32[]{:S(2)}, u32[]{:S(2)}) collective-permute-start(f32[10,18,1]{2,1,0:T(8,128)S(1)} %get-tuple-element.46), channel_id=1, source_target_pairs={{0,1},{1,2},{2,3},{3,0},{4,5},{5,6},{6,7},{7,4},{8,9},{9,10},{10,1... | collective-permute-start | bytes 2168 | tf_op jit(solution)/shard_map/ppermute | solution.py:21
  103.1 6.9 %collective-permute-start.13 = (f32[1,16,128]{2,1,0:T(8,128)S(1)}, f32[1,16,128]{2,1,0:T(8,128)S(1)}, u32[]{:S(2)}, u32[]{:S(2)}) collective-permute-start(f32[1,16,128]{2,1,0:T(8,128)S(1)} %get-tuple-element.79), channel_id=1, source_target_pairs={{32,0},{64,32},{96,64},{128,96},{160,128},{192,160},{224,192},{256... | collective-permute-start | bytes 24584 | tf_op jit(solution)/shard_map/ppermute | solution.py:23
  108.0 5.6 %collective-permute-start.12 = (f32[1,16,128]{2,1,0:T(8,128)S(1)}, f32[1,16,128]{2,1,0:T(8,128)S(1)}, u32[]{:S(2)}, u32[]{:S(2)}) collective-permute-start(f32[1,16,128]{2,1,0:T(8,128)S(1)} %get-tuple-element.78), channel_id=1, source_target_pairs={{0,32},{32,64},{64,96},{96,128},{128,160},{160,192},{192,224},{224... | collective-permute-start | bytes 24584 | tf_op jit(solution)/shard_map/ppermute | solution.py:21
  113.6 6.5 %collective-permute-start.15 = (f32[10,1,128]{2,1,0:T(1,128)S(1)}, f32[10,1,128]{2,1,0:T(1,128)S(1)}, u32[]{:S(2)}, u32[]{:S(2)}) collective-permute-start(f32[10,1,128]{2,1,0:T(1,128)S(1)} %get-tuple-element.65), channel_id=1, source_target_pairs={{4,0},{8,4},{12,8},{16,12},{20,16},{24,20},{28,24},{0,28},{5,1},{9... | collective-permute-start | bytes 15368 | tf_op jit(solution)/shard_map/ppermute | solution.py:23
  120.6 5.6 %collective-permute-start.17 = (f32[10,18,1]{2,1,0:T(8,128)S(1)}, f32[10,18,1]{2,1,0:T(8,128)S(1)}, u32[]{:S(2)}, u32[]{:S(2)}) collective-permute-start(f32[10,18,1]{2,1,0:T(8,128)S(1)} %get-tuple-element.45), channel_id=1, source_target_pairs={{1,0},{2,1},{3,2},{0,3},{5,4},{6,5},{7,6},{4,7},{9,8},{10,9},{11,1... | collective-permute-start | bytes 2168 | tf_op jit(solution)/shard_map/ppermute | solution.py:23
  122.5 6.8 %collective-permute-start.16 = (f32[10,18,1]{2,1,0:T(8,128)S(1)}, f32[10,18,1]{2,1,0:T(8,128)S(1)}, u32[]{:S(2)}, u32[]{:S(2)}) collective-permute-start(f32[10,18,1]{2,1,0:T(8,128)S(1)} %get-tuple-element.44), channel_id=1, source_target_pairs={{0,1},{1,2},{2,3},{3,0},{4,5},{5,6},{6,7},{7,4},{8,9},{9,10},{10,1... | collective-permute-start | bytes 2168 | tf_op jit(solution)/shard_map/ppermute | solution.py:21
  129.6 5.9 %collective-permute-start.19 = (f32[1,16,128]{2,1,0:T(8,128)S(1)}, f32[1,16,128]{2,1,0:T(8,128)S(1)}, u32[]{:S(2)}, u32[]{:S(2)}) collective-permute-start(f32[1,16,128]{2,1,0:T(8,128)S(1)} %get-tuple-element.77), channel_id=1, source_target_pairs={{32,0},{64,32},{96,64},{128,96},{160,128},{192,160},{224,192},{256... | collective-permute-start | bytes 24584 | tf_op jit(solution)/shard_map/ppermute | solution.py:23
  131.5 5.6 %collective-permute-start.18 = (f32[1,16,128]{2,1,0:T(8,128)S(1)}, f32[1,16,128]{2,1,0:T(8,128)S(1)}, u32[]{:S(2)}, u32[]{:S(2)}) collective-permute-start(f32[1,16,128]{2,1,0:T(8,128)S(1)} %get-tuple-element.76), channel_id=1, source_target_pairs={{0,32},{32,64},{64,96},{96,128},{128,160},{160,192},{192,224},{224... | collective-permute-start | bytes 24584 | tf_op jit(solution)/shard_map/ppermute | solution.py:21
  137.2 6.2 %collective-permute-start.21 = (f32[10,1,128]{2,1,0:T(1,128)S(1)}, f32[10,1,128]{2,1,0:T(1,128)S(1)}, u32[]{:S(2)}, u32[]{:S(2)}) collective-permute-start(f32[10,1,128]{2,1,0:T(1,128)S(1)} %get-tuple-element.63), channel_id=1, source_target_pairs={{4,0},{8,4},{12,8},{16,12},{20,16},{24,20},{28,24},{0,28},{5,1},{9... | collective-permute-start | bytes 15368 | tf_op jit(solution)/shard_map/ppermute | solution.py:23
  143.9 5.6 %collective-permute-start.23 = (f32[10,18,1]{2,1,0:T(8,128)S(1)}, f32[10,18,1]{2,1,0:T(8,128)S(1)}, u32[]{:S(2)}, u32[]{:S(2)}) collective-permute-start(f32[10,18,1]{2,1,0:T(8,128)S(1)} %get-tuple-element.43), channel_id=1, source_target_pairs={{1,0},{2,1},{3,2},{0,3},{5,4},{6,5},{7,6},{4,7},{9,8},{10,9},{11,1... | collective-permute-start | bytes 2168 | tf_op jit(solution)/shard_map/ppermute | solution.py:23
  145.8 6.8 %collective-permute-start.22 = (f32[10,18,1]{2,1,0:T(8,128)S(1)}, f32[10,18,1]{2,1,0:T(8,128)S(1)}, u32[]{:S(2)}, u32[]{:S(2)}) collective-permute-start(f32[10,18,1]{2,1,0:T(8,128)S(1)} %get-tuple-element.42), channel_id=1, source_target_pairs={{0,1},{1,2},{2,3},{3,0},{4,5},{5,6},{6,7},{7,4},{8,9},{9,10},{10,1... | collective-permute-start | bytes 2168 | tf_op jit(solution)/shard_map/ppermute | solution.py:21
  162.8 5.6 collective-permute-start.24
  168.4 6.4 %collective-permute-start.27 = (f32[6,1,64]{2,1,0:T(1,128)S(1)}, f32[6,1,64]{2,1,0:T(1,128)S(1)}, u32[]{:S(2)}, u32[]{:S(2)}) collective-permute-start(f32[6,1,64]{2,1,0:T(1,128)S(1)} %get-tuple-element.113), channel_id=1, source_target_pairs={{4,0},{8,4},{12,8},{16,12},{20,16},{24,20},{28,24},{0,28},{5,1},{9... | collective-permute-start | bytes 4616 | tf_op jit(solution)/shard_map/ppermute | solution.py:23
  177.7 6.0 %collective-permute-start.28 = (f32[6,10,1]{2,1,0:T(8,128)S(1)}, f32[6,10,1]{2,1,0:T(8,128)S(1)}, u32[]{:S(2)}, u32[]{:S(2)}) collective-permute-start(f32[6,10,1]{2,1,0:T(8,128)S(1)} %get-tuple-element.94), channel_id=1, source_target_pairs={{0,1},{1,2},{2,3},{3,0},{4,5},{5,6},{6,7},{7,4},{8,9},{9,10},{10,1... | collective-permute-start | bytes 728 | tf_op jit(solution)/shard_map/ppermute | solution.py:21
  187.0 5.6 collective-permute-start.30
  192.6 6.8 %collective-permute-start.33 = (f32[6,1,64]{2,1,0:T(1,128)S(1)}, f32[6,1,64]{2,1,0:T(1,128)S(1)}, u32[]{:S(2)}, u32[]{:S(2)}) collective-permute-start(f32[6,1,64]{2,1,0:T(1,128)S(1)} %get-tuple-element.111), channel_id=1, source_target_pairs={{4,0},{8,4},{12,8},{16,12},{20,16},{24,20},{28,24},{0,28},{5,1},{9... | collective-permute-start | bytes 4616 | tf_op jit(solution)/shard_map/ppermute | solution.py:23
  201.7 6.0 %collective-permute-start.34 = (f32[6,10,1]{2,1,0:T(8,128)S(1)}, f32[6,10,1]{2,1,0:T(8,128)S(1)}, u32[]{:S(2)}, u32[]{:S(2)}) collective-permute-start(f32[6,10,1]{2,1,0:T(8,128)S(1)} %get-tuple-element.92), channel_id=1, source_target_pairs={{0,1},{1,2},{2,3},{3,0},{4,5},{5,6},{6,7},{7,4},{8,9},{9,10},{10,1... | collective-permute-start | bytes 728 | tf_op jit(solution)/shard_map/ppermute | solution.py:21
  210.3 5.6 collective-permute-start.36
  215.9 6.5 %collective-permute-start.39 = (f32[6,1,64]{2,1,0:T(1,128)S(1)}, f32[6,1,64]{2,1,0:T(1,128)S(1)}, u32[]{:S(2)}, u32[]{:S(2)}) collective-permute-start(f32[6,1,64]{2,1,0:T(1,128)S(1)} %get-tuple-element.109), channel_id=1, source_target_pairs={{4,0},{8,4},{12,8},{16,12},{20,16},{24,20},{28,24},{0,28},{5,1},{9... | collective-permute-start | bytes 4616 | tf_op jit(solution)/shard_map/ppermute | solution.py:23
  224.8 6.0 %collective-permute-start.40 = (f32[6,10,1]{2,1,0:T(8,128)S(1)}, f32[6,10,1]{2,1,0:T(8,128)S(1)}, u32[]{:S(2)}, u32[]{:S(2)}) collective-permute-start(f32[6,10,1]{2,1,0:T(8,128)S(1)} %get-tuple-element.90), channel_id=1, source_target_pairs={{0,1},{1,2},{2,3},{3,0},{4,5},{5,6},{6,7},{7,4},{8,9},{9,10},{10,1... | collective-permute-start | bytes 728 | tf_op jit(solution)/shard_map/ppermute | solution.py:21
  239.1 6.2 %collective-permute-start.45 = (f32[4,1,32]{2,1,0:T(1,128)S(1)}, f32[4,1,32]{2,1,0:T(1,128)S(1)}, u32[]{:S(2)}, u32[]{:S(2)}) collective-permute-start(f32[4,1,32]{2,1,0:T(1,128)S(1)} %get-tuple-element.149), channel_id=1, source_target_pairs={{4,0},{8,4},{12,8},{16,12},{20,16},{24,20},{28,24},{0,28},{5,1},{9... | collective-permute-start | bytes 1544 | tf_op jit(solution)/shard_map/ppermute | solution.py:23
  247.6 5.7 %collective-permute-start.46 = (f32[4,6,1]{2,1,0:T(8,128)S(1)}, f32[4,6,1]{2,1,0:T(8,128)S(1)}, u32[]{:S(2)}, u32[]{:S(2)}) collective-permute-start(f32[4,6,1]{2,1,0:T(8,128)S(1)} %get-tuple-element.130), channel_id=1, source_target_pairs={{0,1},{1,2},{2,3},{3,0},{4,5},{5,6},{6,7},{7,4},{8,9},{9,10},{10,1... | collective-permute-start | bytes 296 | tf_op jit(solution)/shard_map/ppermute | solution.py:21
  260.9 6.4 %collective-permute-start.51 = (f32[4,1,32]{2,1,0:T(1,128)S(1)}, f32[4,1,32]{2,1,0:T(1,128)S(1)}, u32[]{:S(2)}, u32[]{:S(2)}) collective-permute-start(f32[4,1,32]{2,1,0:T(1,128)S(1)} %get-tuple-element.147), channel_id=1, source_target_pairs={{4,0},{8,4},{12,8},{16,12},{20,16},{24,20},{28,24},{0,28},{5,1},{9... | collective-permute-start | bytes 1544 | tf_op jit(solution)/shard_map/ppermute | solution.py:23
  270.2 5.7 %collective-permute-start.52 = (f32[4,6,1]{2,1,0:T(8,128)S(1)}, f32[4,6,1]{2,1,0:T(8,128)S(1)}, u32[]{:S(2)}, u32[]{:S(2)}) collective-permute-start(f32[4,6,1]{2,1,0:T(8,128)S(1)} %get-tuple-element.128), channel_id=1, source_target_pairs={{0,1},{1,2},{2,3},{3,0},{4,5},{5,6},{6,7},{7,4},{8,9},{9,10},{10,1... | collective-permute-start | bytes 296 | tf_op jit(solution)/shard_map/ppermute | solution.py:21
  284.0 6.8 %collective-permute-start.57 = (f32[4,1,32]{2,1,0:T(1,128)S(1)}, f32[4,1,32]{2,1,0:T(1,128)S(1)}, u32[]{:S(2)}, u32[]{:S(2)}) collective-permute-start(f32[4,1,32]{2,1,0:T(1,128)S(1)} %get-tuple-element.145), channel_id=1, source_target_pairs={{4,0},{8,4},{12,8},{16,12},{20,16},{24,20},{28,24},{0,28},{5,1},{9... | collective-permute-start | bytes 1544 | tf_op jit(solution)/shard_map/ppermute | solution.py:23
  293.1 5.7 %collective-permute-start.58 = (f32[4,6,1]{2,1,0:T(8,128)S(1)}, f32[4,6,1]{2,1,0:T(8,128)S(1)}, u32[]{:S(2)}, u32[]{:S(2)}) collective-permute-start(f32[4,6,1]{2,1,0:T(8,128)S(1)} %get-tuple-element.126), channel_id=1, source_target_pairs={{0,1},{1,2},{2,3},{3,0},{4,5},{5,6},{6,7},{7,4},{8,9},{9,10},{10,1... | collective-permute-start | bytes 296 | tf_op jit(solution)/shard_map/ppermute | solution.py:21
  307.1 6.5 %collective-permute-start.63 = (f32[3,1,16]{2,1,0:T(1,128)S(1)}, f32[3,1,16]{2,1,0:T(1,128)S(1)}, u32[]{:S(2)}, u32[]{:S(2)}) collective-permute-start(f32[3,1,16]{2,1,0:T(1,128)S(1)} %get-tuple-element.169), channel_id=1, source_target_pairs={{4,0},{8,4},{12,8},{16,12},{20,16},{24,20},{28,24},{0,28},{5,1},{9... | collective-permute-start | bytes 584 | tf_op jit(solution)/shard_map/ppermute | solution.py:23
  315.9 5.6 %collective-permute-start.64 = (f32[3,4,1]{2,1,0:T(4,128)S(1)}, f32[3,4,1]{2,1,0:T(4,128)S(1)}, u32[]{:S(2)}, u32[]{:S(2)}) collective-permute-start(f32[3,4,1]{2,1,0:T(4,128)S(1)} %get-tuple-element.152), channel_id=1, source_target_pairs={{0,1},{1,2},{2,3},{3,0},{4,5},{5,6},{6,7},{7,4},{8,9},{9,10},{10,1... | collective-permute-start | bytes 152 | tf_op jit(solution)/shard_map/ppermute | solution.py:21
  329.0 6.2 %collective-permute-start.69 = (f32[3,1,16]{2,1,0:T(1,128)S(1)}, f32[3,1,16]{2,1,0:T(1,128)S(1)}, u32[]{:S(2)}, u32[]{:S(2)}) collective-permute-start(f32[3,1,16]{2,1,0:T(1,128)S(1)} %get-tuple-element.167), channel_id=1, source_target_pairs={{4,0},{8,4},{12,8},{16,12},{20,16},{24,20},{28,24},{0,28},{5,1},{9... | collective-permute-start | bytes 584 | tf_op jit(solution)/shard_map/ppermute | solution.py:23
  337.6 5.6 %collective-permute-start.70 = (f32[3,4,1]{2,1,0:T(4,128)S(1)}, f32[3,4,1]{2,1,0:T(4,128)S(1)}, u32[]{:S(2)}, u32[]{:S(2)}) collective-permute-start(f32[3,4,1]{2,1,0:T(4,128)S(1)} %get-tuple-element.150), channel_id=1, source_target_pairs={{0,1},{1,2},{2,3},{3,0},{4,5},{5,6},{6,7},{7,4},{8,9},{9,10},{10,1... | collective-permute-start | bytes 152 | tf_op jit(solution)/shard_map/ppermute | solution.py:21
  350.9 6.4 %collective-permute-start.75 = (f32[4,1,32]{2,1,0:T(1,128)S(1)}, f32[4,1,32]{2,1,0:T(1,128)S(1)}, u32[]{:S(2)}, u32[]{:S(2)}) collective-permute-start(f32[4,1,32]{2,1,0:T(1,128)S(1)} %get-tuple-element.143), channel_id=1, source_target_pairs={{4,0},{8,4},{12,8},{16,12},{20,16},{24,20},{28,24},{0,28},{5,1},{9... | collective-permute-start | bytes 1544 | tf_op jit(solution)/shard_map/ppermute | solution.py:23
  360.2 5.7 %collective-permute-start.76 = (f32[4,6,1]{2,1,0:T(8,128)S(1)}, f32[4,6,1]{2,1,0:T(8,128)S(1)}, u32[]{:S(2)}, u32[]{:S(2)}) collective-permute-start(f32[4,6,1]{2,1,0:T(8,128)S(1)} %get-tuple-element.124), channel_id=1, source_target_pairs={{0,1},{1,2},{2,3},{3,0},{4,5},{5,6},{6,7},{7,4},{8,9},{9,10},{10,1... | collective-permute-start | bytes 296 | tf_op jit(solution)/shard_map/ppermute | solution.py:21
  373.5 6.5 %collective-permute-start.81 = (f32[4,1,32]{2,1,0:T(1,128)S(1)}, f32[4,1,32]{2,1,0:T(1,128)S(1)}, u32[]{:S(2)}, u32[]{:S(2)}) collective-permute-start(f32[4,1,32]{2,1,0:T(1,128)S(1)} %get-tuple-element.141), channel_id=1, source_target_pairs={{4,0},{8,4},{12,8},{16,12},{20,16},{24,20},{28,24},{0,28},{5,1},{9... | collective-permute-start | bytes 1544 | tf_op jit(solution)/shard_map/ppermute | solution.py:23
  382.3 5.7 %collective-permute-start.82 = (f32[4,6,1]{2,1,0:T(8,128)S(1)}, f32[4,6,1]{2,1,0:T(8,128)S(1)}, u32[]{:S(2)}, u32[]{:S(2)}) collective-permute-start(f32[4,6,1]{2,1,0:T(8,128)S(1)} %get-tuple-element.122), channel_id=1, source_target_pairs={{0,1},{1,2},{2,3},{3,0},{4,5},{5,6},{6,7},{7,4},{8,9},{9,10},{10,1... | collective-permute-start | bytes 296 | tf_op jit(solution)/shard_map/ppermute | solution.py:21
  395.6 6.2 %collective-permute-start.87 = (f32[4,1,32]{2,1,0:T(1,128)S(1)}, f32[4,1,32]{2,1,0:T(1,128)S(1)}, u32[]{:S(2)}, u32[]{:S(2)}) collective-permute-start(f32[4,1,32]{2,1,0:T(1,128)S(1)} %get-tuple-element.139), channel_id=1, source_target_pairs={{4,0},{8,4},{12,8},{16,12},{20,16},{24,20},{28,24},{0,28},{5,1},{9... | collective-permute-start | bytes 1544 | tf_op jit(solution)/shard_map/ppermute | solution.py:23
  404.2 5.7 %collective-permute-start.88 = (f32[4,6,1]{2,1,0:T(8,128)S(1)}, f32[4,6,1]{2,1,0:T(8,128)S(1)}, u32[]{:S(2)}, u32[]{:S(2)}) collective-permute-start(f32[4,6,1]{2,1,0:T(8,128)S(1)} %get-tuple-element.120), channel_id=1, source_target_pairs={{0,1},{1,2},{2,3},{3,0},{4,5},{5,6},{6,7},{7,4},{8,9},{9,10},{10,1... | collective-permute-start | bytes 296 | tf_op jit(solution)/shard_map/ppermute | solution.py:21
  412.3 5.6 collective-permute-start.90
  417.9 6.2 %collective-permute-start.93 = (f32[6,1,64]{2,1,0:T(1,128)S(1)}, f32[6,1,64]{2,1,0:T(1,128)S(1)}, u32[]{:S(2)}, u32[]{:S(2)}) collective-permute-start(f32[6,1,64]{2,1,0:T(1,128)S(1)} %get-tuple-element.101), channel_id=1, source_target_pairs={{4,0},{8,4},{12,8},{16,12},{20,16},{24,20},{28,24},{0,28},{5,1},{9... | collective-permute-start | bytes 4616 | tf_op jit(solution)/shard_map/ppermute | solution.py:23
  426.5 6.0 %collective-permute-start.94 = (f32[6,10,1]{2,1,0:T(8,128)S(1)}, f32[6,10,1]{2,1,0:T(8,128)S(1)}, u32[]{:S(2)}, u32[]{:S(2)}) collective-permute-start(f32[6,10,1]{2,1,0:T(8,128)S(1)} %get-tuple-element.88), channel_id=1, source_target_pairs={{0,1},{1,2},{2,3},{3,0},{4,5},{5,6},{6,7},{7,4},{8,9},{9,10},{10,1... | collective-permute-start | bytes 728 | tf_op jit(solution)/shard_map/ppermute | solution.py:21
  434.6 5.6 collective-permute-start.96
  440.1 6.4 %collective-permute-start.99 = (f32[6,1,64]{2,1,0:T(1,128)S(1)}, f32[6,1,64]{2,1,0:T(1,128)S(1)}, u32[]{:S(2)}, u32[]{:S(2)}) collective-permute-start(f32[6,1,64]{2,1,0:T(1,128)S(1)} %get-tuple-element.99), channel_id=1, source_target_pairs={{4,0},{8,4},{12,8},{16,12},{20,16},{24,20},{28,24},{0,28},{5,1},{9... | collective-permute-start | bytes 4616 | tf_op jit(solution)/shard_map/ppermute | solution.py:23
  449.4 6.0 %collective-permute-start.100 = (f32[6,10,1]{2,1,0:T(8,128)S(1)}, f32[6,10,1]{2,1,0:T(8,128)S(1)}, u32[]{:S(2)}, u32[]{:S(2)}) collective-permute-start(f32[6,10,1]{2,1,0:T(8,128)S(1)} %get-tuple-element.86), channel_id=1, source_target_pairs={{0,1},{1,2},{2,3},{3,0},{4,5},{5,6},{6,7},{7,4},{8,9},{9,10},{10,1... | collective-permute-start | bytes 728 | tf_op jit(solution)/shard_map/ppermute | solution.py:21
  463.1 6.5 %collective-permute-start.105 = (f32[6,1,64]{2,1,0:T(1,128)S(1)}, f32[6,1,64]{2,1,0:T(1,128)S(1)}, u32[]{:S(2)}, u32[]{:S(2)}) collective-permute-start(f32[6,1,64]{2,1,0:T(1,128)S(1)} %get-tuple-element.97), channel_id=1, source_target_pairs={{4,0},{8,4},{12,8},{16,12},{20,16},{24,20},{28,24},{0,28},{5,1},{9... | collective-permute-start | bytes 4616 | tf_op jit(solution)/shard_map/ppermute | solution.py:23
  472.0 6.0 %collective-permute-start.106 = (f32[6,10,1]{2,1,0:T(8,128)S(1)}, f32[6,10,1]{2,1,0:T(8,128)S(1)}, u32[]{:S(2)}, u32[]{:S(2)}) collective-permute-start(f32[6,10,1]{2,1,0:T(8,128)S(1)} %get-tuple-element.84), channel_id=1, source_target_pairs={{0,1},{1,2},{2,3},{3,0},{4,5},{5,6},{6,7},{7,4},{8,9},{9,10},{10,1... | collective-permute-start | bytes 728 | tf_op jit(solution)/shard_map/ppermute | solution.py:21
  486.7 5.6 %collective-permute-start.108 = (f32[1,16,128]{2,1,0:T(8,128)S(1)}, f32[1,16,128]{2,1,0:T(8,128)S(1)}, u32[]{:S(2)}, u32[]{:S(2)}) collective-permute-start(f32[1,16,128]{2,1,0:T(8,128)S(1)} %get-tuple-element.74), channel_id=1, source_target_pairs={{0,32},{32,64},{64,96},{96,128},{128,160},{160,192},{192,224},{224... | collective-permute-start | bytes 24584 | tf_op jit(solution)/shard_map/ppermute | solution.py:21
  492.3 6.3 %collective-permute-start.111 = (f32[10,1,128]{2,1,0:T(1,128)S(1)}, f32[10,1,128]{2,1,0:T(1,128)S(1)}, u32[]{:S(2)}, u32[]{:S(2)}) collective-permute-start(f32[10,1,128]{2,1,0:T(1,128)S(1)} %get-tuple-element.61), channel_id=1, source_target_pairs={{4,0},{8,4},{12,8},{16,12},{20,16},{24,20},{28,24},{0,28},{5,1},{9... | collective-permute-start | bytes 15368 | tf_op jit(solution)/shard_map/ppermute | solution.py:23
  499.1 5.6 %collective-permute-start.113 = (f32[10,18,1]{2,1,0:T(8,128)S(1)}, f32[10,18,1]{2,1,0:T(8,128)S(1)}, u32[]{:S(2)}, u32[]{:S(2)}) collective-permute-start(f32[10,18,1]{2,1,0:T(8,128)S(1)} %get-tuple-element.41), channel_id=1, source_target_pairs={{1,0},{2,1},{3,2},{0,3},{5,4},{6,5},{7,6},{4,7},{9,8},{10,9},{11,1... | collective-permute-start | bytes 2168 | tf_op jit(solution)/shard_map/ppermute | solution.py:23
  501.0 6.8 %collective-permute-start.112 = (f32[10,18,1]{2,1,0:T(8,128)S(1)}, f32[10,18,1]{2,1,0:T(8,128)S(1)}, u32[]{:S(2)}, u32[]{:S(2)}) collective-permute-start(f32[10,18,1]{2,1,0:T(8,128)S(1)} %get-tuple-element.40), channel_id=1, source_target_pairs={{0,1},{1,2},{2,3},{3,0},{4,5},{5,6},{6,7},{7,4},{8,9},{9,10},{10,1... | collective-permute-start | bytes 2168 | tf_op jit(solution)/shard_map/ppermute | solution.py:21
  509.9 5.6 %collective-permute-start.114 = (f32[1,16,128]{2,1,0:T(8,128)S(1)}, f32[1,16,128]{2,1,0:T(8,128)S(1)}, u32[]{:S(2)}, u32[]{:S(2)}) collective-permute-start(f32[1,16,128]{2,1,0:T(8,128)S(1)} %get-tuple-element.72), channel_id=1, source_target_pairs={{0,32},{32,64},{64,96},{96,128},{128,160},{160,192},{192,224},{224... | collective-permute-start | bytes 24584 | tf_op jit(solution)/shard_map/ppermute | solution.py:21
  515.6 6.2 %collective-permute-start.117 = (f32[10,1,128]{2,1,0:T(1,128)S(1)}, f32[10,1,128]{2,1,0:T(1,128)S(1)}, u32[]{:S(2)}, u32[]{:S(2)}) collective-permute-start(f32[10,1,128]{2,1,0:T(1,128)S(1)} %get-tuple-element.59), channel_id=1, source_target_pairs={{4,0},{8,4},{12,8},{16,12},{20,16},{24,20},{28,24},{0,28},{5,1},{9... | collective-permute-start | bytes 15368 | tf_op jit(solution)/shard_map/ppermute | solution.py:23
  522.3 5.6 %collective-permute-start.119 = (f32[10,18,1]{2,1,0:T(8,128)S(1)}, f32[10,18,1]{2,1,0:T(8,128)S(1)}, u32[]{:S(2)}, u32[]{:S(2)}) collective-permute-start(f32[10,18,1]{2,1,0:T(8,128)S(1)} %get-tuple-element.39), channel_id=1, source_target_pairs={{1,0},{2,1},{3,2},{0,3},{5,4},{6,5},{7,6},{4,7},{9,8},{10,9},{11,1... | collective-permute-start | bytes 2168 | tf_op jit(solution)/shard_map/ppermute | solution.py:23
  524.2 6.8 %collective-permute-start.118 = (f32[10,18,1]{2,1,0:T(8,128)S(1)}, f32[10,18,1]{2,1,0:T(8,128)S(1)}, u32[]{:S(2)}, u32[]{:S(2)}) collective-permute-start(f32[10,18,1]{2,1,0:T(8,128)S(1)} %get-tuple-element.38), channel_id=1, source_target_pairs={{0,1},{1,2},{2,3},{3,0},{4,5},{5,6},{6,7},{7,4},{8,9},{9,10},{10,1... | collective-permute-start | bytes 2168 | tf_op jit(solution)/shard_map/ppermute | solution.py:21
  533.5 5.6 %collective-permute-start.120 = (f32[1,16,128]{2,1,0:T(8,128)S(1)}, f32[1,16,128]{2,1,0:T(8,128)S(1)}, u32[]{:S(2)}, u32[]{:S(2)}) collective-permute-start(f32[1,16,128]{2,1,0:T(8,128)S(1)} %get-tuple-element.70), channel_id=1, source_target_pairs={{0,32},{32,64},{64,96},{96,128},{128,160},{160,192},{192,224},{224... | collective-permute-start | bytes 24584 | tf_op jit(solution)/shard_map/ppermute | solution.py:21
  539.2 6.7 %collective-permute-start.123 = (f32[10,1,128]{2,1,0:T(1,128)S(1)}, f32[10,1,128]{2,1,0:T(1,128)S(1)}, u32[]{:S(2)}, u32[]{:S(2)}) collective-permute-start(f32[10,1,128]{2,1,0:T(1,128)S(1)} %get-tuple-element.57), channel_id=1, source_target_pairs={{4,0},{8,4},{12,8},{16,12},{20,16},{24,20},{28,24},{0,28},{5,1},{9... | collective-permute-start | bytes 15368 | tf_op jit(solution)/shard_map/ppermute | solution.py:23
  546.3 5.6 %collective-permute-start.125 = (f32[10,18,1]{2,1,0:T(8,128)S(1)}, f32[10,18,1]{2,1,0:T(8,128)S(1)}, u32[]{:S(2)}, u32[]{:S(2)}) collective-permute-start(f32[10,18,1]{2,1,0:T(8,128)S(1)} %get-tuple-element.37), channel_id=1, source_target_pairs={{1,0},{2,1},{3,2},{0,3},{5,4},{6,5},{7,6},{4,7},{9,8},{10,9},{11,1... | collective-permute-start | bytes 2168 | tf_op jit(solution)/shard_map/ppermute | solution.py:23
  548.8 6.8 %collective-permute-start.124 = (f32[10,18,1]{2,1,0:T(8,128)S(1)}, f32[10,18,1]{2,1,0:T(8,128)S(1)}, u32[]{:S(2)}, u32[]{:S(2)}) collective-permute-start(f32[10,18,1]{2,1,0:T(8,128)S(1)} %get-tuple-element.36), channel_id=1, source_target_pairs={{0,1},{1,2},{2,3},{3,0},{4,5},{5,6},{6,7},{7,4},{8,9},{9,10},{10,1... | collective-permute-start | bytes 2168 | tf_op jit(solution)/shard_map/ppermute | solution.py:21
  (63 other events, 265.2 us)
where the time goes:
time: 561 us; the launch traced here: 556 us
  starting transfers between devices  349 us (62%)
  waiting for transfers between devices  129 us (23%)
  local copies, waits for them, and re-layouts  53.7 us (10%)
  other arithmetic  22.8 us (4%)
    ppermute x63, starting transfers between devices, padded_2(): lax.ppermute(head, axis, [((i + 1) % count, i) for i in range(count)])  215 us
    ppermute x63, starting transfers between devices, padded_2(): lax.ppermute(tail, axis, [(i, (i + 1) % count) for i in range(count)])  134 us
    ppermute x63, waiting for transfers between devices, padded_2(): lax.ppermute(tail, axis, [(i, (i + 1) % count) for i in range(count)])  111 us
    ppermute x63, waiting for transfers between devices, padded_2(): lax.ppermute(head, axis, [((i + 1) % count, i) for i in range(count)])  17.7 us
  transfers between devices with their start and end apart: 126, of which 86 were waited for; matrix products, arithmetic and copies ran while one was open for 10% of the time, Pallas kernels for 0%

commit v1 on v0

v1 whole, which is shorter than its diff:
```python
import functools

import jax
import jax.numpy as jnp
from jax import lax
from jax.experimental import pallas as pl
from jax.experimental.pallas import tpu as pltpu
from jax.sharding import PartitionSpec as P

MESH = pl.DeviceIdType.MESH
F32 = jnp.float32

CENTER = 1.125
RADIUS = 0.875
RATIO = CENTER / RADIUS
RHO0 = 1.0 / RATIO
RHO1 = 1.0 / (2.0 * RATIO - RHO0)
RHO2 = 1.0 / (2.0 * RATIO - RHO1)
STEPS = ((RHO1 * RHO0, 2.0 * RHO1 / RADIUS), (RHO2 * RHO1, 2.0 * RHO2 / RADIUS))


def roll(value, shift, axis):
    return pltpu.roll(value, shift % value.shape[axis], axis)


def lane_of(shape):
    return lax.broadcasted_iota(jnp.int32, shape, len(shape) - 1)


def select_matrix(target):
    row = lax.broadcasted_iota(jnp.int32, (128, 128), 0)
    column = lax.broadcasted_iota(jnp.int32, (128, 128), 1)
    return jnp.where(row == target(column), 1.0, 0.0).astype(F32)


def dot(a, b):
    return jnp.dot(a, b, precision=lax.Precision.HIGHEST, preferred_element_type=F32)


def harmonic(one_side, other_side):
    return 2.0 * one_side * other_side / (one_side + other_side)


def chunks(low, high, size):
    return [(start, min(start + size, high)) for start in range(low, high, size)]


def operator_0(field, faces, low, high):
    face_x, face_y, face_z = faces
    result = []
    cells = []
    for t in range(2):
        v = field[low - 1 : high + 1, t]
        flux = face_x[low : high + 1, t] * (v[1:] - v[:-1])
        c = v[1:-1]
        g = flux[:-1] - flux[1:]
        flux = face_y[low:high, t] * (c - roll(c, 1, 1))
        g = g + (flux - roll(flux, -1, 1))
        cells.append(c)
        result.append(g)
    even = face_z[low:high, 0] * (cells[0] - roll(cells[1], 1, 2))
    odd = face_z[low:high, 1] * (cells[1] - cells[0])
    return [result[0] + (even - odd), result[1] + (odd - roll(even, -1, 2))]


def operator_1(field, faces, low, high):
    v = field[low - 1 : high + 1]
    flux = faces[low : high + 1, 0] * (v[1:] - v[:-1])
    c = v[1:-1]
    g = flux[:-1] - flux[1:]
    flux = faces[low:high, 1] * (c - roll(c, 1, 1))
    g = g + (flux - roll(flux, -1, 1))
    flux = faces[low:high, 2] * (c - roll(c, 1, 2))
    return g + (flux - roll(flux, -1, 2))


def rows(ref, low, high):
    pieces = []
    at = low
    while at < high:
        start = at % 16
        stop = min(16, start + high - at)
        pieces.append(ref[start:stop])
        at += stop - start
    return pieces[0] if len(pieces) == 1 else jnp.concatenate(pieces, axis=0)


def put_rows(ref, low, high, value):
    at = low
    while at < high:
        start = at % 16
        stop = min(16, start + high - at)
        ref[start:stop] = value[at - low : at - low + stop - start]
        at += stop - start


def operator_2(field, faces, low, high):
    face_x, face_y, face_z = faces
    v = rows(field, low - 1, high + 1)
    half = lane_of(v[:-1].shape) < 64
    turned = roll(v, 64, 2)
    flux = rows(face_x, low, high + 1) * (v[1:] - jnp.where(half, turned[:-1], turned[1:]))
    turned = roll(flux, 64, 2)
    g = flux[:-1] - jnp.where(half[1:], turned[:-1], turned[1:])
    c = v[1:-1]
    flux = rows(face_y, low, high) * (c - roll(c, 1, 1))
    g = g + (flux - roll(flux, -1, 1))
    flux = rows(face_z, low, high) * (c - roll(c, 1, 2))
    return g + (flux - roll(flux, -1, 2))


def operator_3(field, faces, low, high):
    face_x, face_y, face_z = faces
    v = rows(field, low - 1, high + 1)
    flux = rows(face_x, low, high + 1) * (v[1:] - v[:-1])
    g = flux[:-1] - flux[1:]
    c = v[1:-1]
    flux = rows(face_y, low, high) * (c - roll(c, 1, 1))
    g = g + (flux - roll(flux, -1, 1))
    flux = rows(face_z, low, high) * (c - roll(c, 2, 2))
    return g + (flux - roll(flux, -2, 2))


def kernel(
    sizes,
    source_hbm,
    cond_hbm,
    out_ref,
    staged,
    own,
    z_send,
    z_recv,
    win,
    y_send,
    y_recv,
    fx,
    fy,
    fz,
    inv,
    xa,
    xb,
    dd,
    tmp0,
    f1,
    b1,
    inv1,
    x1a,
    x1b,
    d1,
    tmp1,
    dup1,
    g2f,
    g2b,
    f2,
    b2,
    inv2,
    x2a,
    x2b,
    d2,
    tmp2,
    f3,
    b3,
    inv3,
    x3a,
    x3b,
    d3,
    dup2,
    dup21,
    in_sem,
    z_sems,
    x_sems,
    y_sems,
    f1x_sems,
    f1y_sems,
    b1x_sems,
    b1y_sems,
    gfx_sems,
    gfy_sems,
    gbx_sems,
    gby_sems,
):
    count_x, count_y, count_z = sizes
    me_x, me_y, me_z = lax.axis_index("gx"), lax.axis_index("gy"), lax.axis_index("gz")

    def at_x(step):
        return {"gx": lax.rem(me_x + (step + count_x), count_x)}

    def at_y(step):
        return {"gy": lax.rem(me_y + (step + count_y), count_y)}

    def at_z(step):
        return {"gz": lax.rem(me_z + (step + count_z), count_z)}

    loads = [
        pltpu.make_async_copy(cond_hbm, staged.at[0], in_sem.at[0]),
        pltpu.make_async_copy(source_hbm, staged.at[1], in_sem.at[1]),
    ]
    for load in loads:
        load.start()

    barrier = pltpu.get_barrier_semaphore()
    partners = [at_z(1), at_z(-1)]
    partners += [at_x(step) for step in range(1, count_x)]
    partners += [at_y(step) for step in range(1, count_y)]
    for partner in partners:
        pl.semaphore_signal(barrier, inc=1, device_id=partner, device_id_type=MESH)

    pending = []

    def send(source, target, sems, slot, device):
        copy = pltpu.make_async_remote_copy(
            src_ref=source,
            dst_ref=target,
            send_sem=sems.at[0, slot],
            recv_sem=sems.at[1, slot],
            device_id=device,
            device_id_type=MESH,
        )
        copy.start()
        pending.append(copy)
        return copy

    keep = select_matrix(lambda l: jnp.where(l < 64, 2 * l, 2 * (l - 64) + 1))
    down_a = select_matrix(
        lambda l: jnp.where(l < 64, -1, jnp.where(l < 96, 2 * (l - 64), 2 * (l - 96) + 1))
    )
    down_b = select_matrix(
        lambda l: jnp.where(l >= 64, -1, jnp.where(l < 32, 2 * l, 2 * (l - 32) + 1))
    )
    up_a = select_matrix(
        lambda l: jnp.where(l < 64, -1, jnp.where(l >= 96, 64 + 2 * (l - 96), 64 + 2 * (l - 64) + 1))
    )
    up_b = select_matrix(
        lambda l: jnp.where(l >= 64, -1, jnp.where(l >= 32, 64 + 2 * (l - 32), 64 + 2 * l + 1))
    )
    z_copies = []
    for f in range(2):
        loads[f].wait()
        cells = staged[f].reshape(128, 128)
        z_send[f, 0] = (dot(cells[:64], down_a) + dot(cells[64:], down_b)).reshape(4, 16, 128)
        z_send[f, 1] = (dot(cells[:64], up_a) + dot(cells[64:], up_b)).reshape(4, 16, 128)
        if f == 0:
            pl.semaphore_wait(barrier, len(partners))
        z_copies.append(
            [
                send(z_send.at[f, way], z_recv.at[f, way], z_sems, 2 * f + way, at_z((-1, 1)[way]))
                for way in range(2)
            ]
        )
        own[f] = dot(cells, keep).reshape(8, 16, 128)

    def send_x(f):
        return [
            send(
                win.at[f, 4:8, :, 0:16, :],
                win.at[f, 12:16, :, 0:16, :],
                x_sems,
                2 * f,
                at_x(-1),
            ),
            send(
                win.at[f, 8:12, :, 0:16, :],
                win.at[f, 0:4, :, 0:16, :],
                x_sems,
                2 * f + 1,
                at_x(1),
            ),
        ]

    def send_y(f):
        y_send[f, 0] = win[f, :, :, 0:4, :]
        y_send[f, 1] = win[f, :, :, 12:16, :]
        return [
            send(y_send.at[f, way], y_recv.at[f, way], y_sems, 2 * f + way, at_y((-1, 1)[way]))
            for way in range(2)
        ]

    def place_y(f, copies):
        for copy in copies:
            copy.wait_recv()
        win[f, :, :, 16:20, :] = y_recv[f, 0]
        win[f, :, :, 20:24, :] = y_recv[f, 1]

    x_copies = []
    for f in range(2):
        for copy in z_copies[f]:
            copy.wait_recv()
        lane = lane_of((4, 16, 128))
        for part in range(2):
            mine = own[f, 4 * part : 4 * part + 4]
            above, below = z_recv[f, 0], z_recv[f, 1]
            for t in range(2):
                turn_above = ((0, 96), (64, 32))[part][t]
                turn_below = ((0, 32), (64, 96))[part][t]
                halo = jnp.where(
                    lane < 96,
                    roll(above, turn_above, 2) if turn_above else above,
                    roll(below, turn_below, 2) if turn_below else below,
                )
                win[f, 4 + 4 * part : 8 + 4 * part, t, 0:16, :] = jnp.where(
                    lane < 64, roll(mine, 64, 2) if t else mine, halo
                )
        x_copies.append(send_x(f))
    y_copies = []
    for f in range(2):
        for copy in x_copies[f]:
            copy.wait_recv()
        y_copies.append(send_y(f))
    place_y(0, y_copies[0])

    cond, source, best = win.at[0], win.at[1], win.at[2]
    faces0 = (fx, fy, fz)
    for low, high in chunks(1, 16, 4):
        for t in range(2):
            k = cond[low - 1 : high, t]
            fx[low:high, t] = harmonic(k[1:], k[:-1])
    for low, high in chunks(1, 15, 4):
        k0, k1 = cond[low:high, 0], cond[low:high, 1]
        fy[low:high, 0] = harmonic(k0, roll(k0, 1, 1))
        fy[low:high, 1] = harmonic(k1, roll(k1, 1, 1))
        fz[low:high, 0] = harmonic(k0, roll(k1, 1, 2))
        fz[low:high, 1] = harmonic(k1, k0)

    for i in range(4):
        tmp0[0, i] = fx[4 + 2 * i, 0, 0:16, :] + fx[4 + 2 * i, 1, 0:16, :]
        tmp0[1, i] = (fy[4 + 2 * i, 0, 0:16, :] + fy[4 + 2 * i, 1, 0:16, :]) + (
            fy[5 + 2 * i, 0, 0:16, :] + fy[5 + 2 * i, 1, 0:16, :]
        )
        tmp0[2, i] = fz[4 + 2 * i, 0, 0:16, :] + fz[5 + 2 * i, 0, 0:16, :]
    first, second = pl.ds(0, 8, stride=2), pl.ds(1, 8, stride=2)
    f1[8:12, 0, 8:16, :] = 0.125 * (tmp0[0, :, first, :] + tmp0[0, :, second, :])
    f1[8:12, 1, 8:16, :] = 0.125 * tmp0[1, :, first, :]
    f1[8:12, 2, 8:16, :] = 0.125 * (tmp0[2, :, first, :] + tmp0[2, :, second, :])
    f1x_copies = [
        send(
            f1.at[8:12, :, 8:16, :],
            f1.at[8 - 4 * step : 12 - 4 * step, :, 8:16, :],
            f1x_sems,
            slot,
            at_x(step),
        )
        for slot, step in enumerate((-1, 1, -2, 2))
    ]

    row = lax.broadcasted_iota(jnp.int32, (128, 128), 0)
    column = lax.broadcasted_iota(jnp.int32, (128, 128), 1)
    pack = [
        jnp.where((row // 2 + 16) % 64 + 64 * p == column, 1.0, 0.0).astype(F32) for p in range(2)
    ]
    pack_even = [
        jnp.where((row % 2 == 0) & ((row // 2 + 16) % 64 + 64 * p == column), 1.0, 0.0).astype(F32)
        for p in range(2)
    ]
    first4, second4 = pl.ds(0, 4, stride=2), pl.ds(1, 4, stride=2)
    tmp1[0] = dot(f1[8, 0, 8:16, :], pack[0]) + dot(f1[10, 0, 8:16, :], pack[1])
    tmp1[1] = dot(f1[8, 1, 8:16, :] + f1[9, 1, 8:16, :], pack[0]) + dot(
        f1[10, 1, 8:16, :] + f1[11, 1, 8:16, :], pack[1]
    )
    tmp1[2] = dot(f1[8, 2, 8:16, :] + f1[9, 2, 8:16, :], pack_even[0]) + dot(
        f1[10, 2, 8:16, :] + f1[11, 2, 8:16, :], pack_even[1]
    )
    g2f[1, 2, 0] = 0.125 * (tmp1[0, first4, :] + tmp1[0, second4, :])
    g2f[1, 2, 1] = 0.125 * tmp1[1, first4, :]
    g2f[1, 2, 2] = 0.125 * (tmp1[2, first4, :] + tmp1[2, second4, :])

    def gather_x(ref, sems):
        return [
            send(ref.at[1, 2], ref.at[1, (2 - step) % count_x], sems, step - 1, at_x(step))
            for step in range(1, count_x)
        ]

    def gather_y(ref, sems):
        return [
            send(ref.at[1], ref.at[(1 - step) % count_y], sems, step - 1, at_y(step))
            for step in range(1, count_y)
        ]

    gfx_copies = gather_x(g2f, gfx_sems)

    for low, high in chunks(1, 15, 2):
        x_sum = [fx[low:high, t] + fx[low + 1 : high + 1, t] for t in range(2)]
        y_sum = [fy[low:high, t] + roll(fy[low:high, t], -1, 1) for t in range(2)]
        z0, z1 = fz[low:high, 0], fz[low:high, 1]
        inv[low:high, 0] = 1.0 / ((x_sum[0] + y_sum[0]) + (z0 + z1))
        inv[low:high, 1] = 1.0 / ((x_sum[1] + y_sum[1]) + (z1 + roll(z0, -1, 2)))

    place_y(1, y_copies[1])
    for low, high in chunks(1, 15, 4):
        for t in range(2):
            d = inv[low:high, t] * source[low:high, t] * (1.0 / CENTER)
            dd[low:high, t] = d
            xa[low:high, t] = d

    def step_0(old, new, low, high, step, target=None):
        keep_old, keep_new = STEPS[step]
        for lo, hi in chunks(low, high, 2):
            applied = operator_0(old, faces0, lo, hi)
            for t in range(2):
                r = source[lo:hi, t] - applied[t]
                d = keep_old * dd[lo:hi, t] + keep_new * (inv[lo:hi, t] * r)
                if target is None:
                    dd[lo:hi, t] = d
                    new[lo:hi, t] = old[lo:hi, t] + d
                else:
                    target(lo, hi, t, old[lo:hi, t] + d)

    step_0(xa, xb, 2, 14, 0)

    for copy in f1x_copies:
        copy.wait_recv()
    f1y_copies = [
        send(
            f1.at[:, :, 8:16, :],
            f1.at[:, :, 8 - 8 * step : 16 - 8 * step, :],
            f1y_sems,
            slot,
            at_y(step),
        )
        for slot, step in enumerate((-1, 1))
    ]
    step_0(xb, xa, 3, 13, 1)
    best[4:12, :, 0:16, :] = xa[4:12, :, 0:16, :]
    for i in range(4):
        applied = operator_0(xa, faces0, 4 + 2 * i, 6 + 2 * i)
        r = (source[4 + 2 * i : 6 + 2 * i, 0, 0:16, :] - applied[0][:, :16]) + (
            source[4 + 2 * i : 6 + 2 * i, 1, 0:16, :] - applied[1][:, :16]
        )
        tmp0[0, i] = r[0] + r[1]
    b1[8:12, 8:16, :] = 0.125 * (tmp0[0, :, first, :] + tmp0[0, :, second, :])
    b1x_copies = [
        send(
            b1.at[8:12, 8:16, :],
            b1.at[8 - 4 * step : 12 - 4 * step, 8:16, :],
            b1x_sems,
            slot,
            at_x(step),
        )
        for slot, step in enumerate((-1, 1, -2, 2))
    ]
    x_copies.append(send_x(2))
    for copy in gfx_copies:
        copy.wait_recv()
    gfy_copies = gather_y(g2f, gfy_sems)

    for copy in f1y_copies:
        copy.wait_recv()
    for low, high in chunks(1, 19, 6):
        x_sum = f1[low:high, 0] + f1[low + 1 : high + 1, 0]
        y_term, z_term = f1[low:high, 1], f1[low:high, 2]
        y_sum = y_term + roll(y_term, -1, 1)
        inv1[low:high] = 1.0 / ((x_sum + y_sum) + (z_term + roll(z_term, -1, 2)))

    for copy in b1x_copies:
        copy.wait_recv()
    b1y_copies = [
        send(
            b1.at[:, 8:16, :],
            b1.at[:, 8 - 8 * step : 16 - 8 * step, :],
            b1y_sems,
            slot,
            at_y(step),
        )
        for slot, step in enumerate((-1, 1))
    ]
    for copy in x_copies[2]:
        copy.wait_recv()
    y_copies.append(send_y(2))
    for copy in b1y_copies:
        copy.wait_recv()

    for low, high in chunks(1, 19, 6):
        d = inv1[low:high] * b1[low:high] * (1.0 / CENTER)
        d1[low:high] = d
        x1a[low:high] = d

    def step_1(old, new, low, high, step):
        keep_old, keep_new = STEPS[step]
        for lo, hi in chunks(low, high, 4):
            r = b1[lo:hi] - operator_1(old, f1, lo, hi)
            d = keep_old * d1[lo:hi] + keep_new * (inv1[lo:hi] * r)
            d1[lo:hi] = d
            new[lo:hi] = old[lo:hi] + d

    step_1(x1a, x1b, 2, 18, 0)
    step_1(x1b, x1a, 3, 17, 1)
    r = (b1[8:12] - operator_1(x1a, f1, 8, 12))[:, 8:16]
    tmp1[0] = dot(r[0] + r[1], pack[0]) + dot(r[2] + r[3], pack[1])
    g2b[1, 2] = 0.125 * (tmp1[0, first4, :] + tmp1[0, second4, :])
    gbx_copies = gather_x(g2b, gbx_sems)

    for copy in gfy_copies:
        copy.wait_recv()
    for f in range(3):
        for s in range(count_y):
            f2[f, :, 4 * s : 4 * s + 4, :] = g2f[s, :, f]
    faces2 = (f2.at[0], f2.at[1], f2.at[2])
    for low, high in chunks(0, 16, 4):
        terms = rows(faces2[0], low, high + 1)
        turned = roll(terms, 64, 2)
        half = lane_of(terms[1:].shape) < 64
        x_sum = terms[:-1] + jnp.where(half, turned[:-1], turned[1:])
        y_term, z_term = f2[1, low:high], f2[2, low:high]
        y_sum = y_term + roll(y_term, -1, 1)
        inv2[low:high] = 1.0 / ((x_sum + y_sum) + (z_term + roll(z_term, -1, 2)))

        x_low = f2[0, low:high]
        x_low = jnp.where(half, x_low, roll(x_low, 64, 2))
        tmp2[0, low:high] = x_low + roll(x_low, -1, 2)
        y_both = y_term + roll(y_term, 64, 2)
        tmp2[1, low:high] = y_both + roll(y_both, -1, 2)
        tmp2[2, low:high] = z_term + roll(z_term, 64, 2)
    first16, second16 = pl.ds(0, 16, stride=2), pl.ds(1, 16, stride=2)
    f3[0] = 0.125 * (tmp2[0, :, first16, :] + tmp2[0, :, second16, :])
    f3[1] = 0.125 * tmp2[1, :, first16, :]
    f3[2] = 0.125 * (tmp2[2, :, first16, :] + tmp2[2, :, second16, :])
    faces3 = (f3.at[0], f3.at[1], f3.at[2])
    for low, high in chunks(0, 16, 8):
        terms = rows(faces3[0], low, high + 1)
        y_term, z_term = f3[1, low:high], f3[2, low:high]
        inv3[low:high] = 1.0 / (
            (terms[:-1] + terms[1:] + (y_term + roll(y_term, -1, 1)))
            + (z_term + roll(z_term, -2, 2))
        )

    for copy in gbx_copies:
        copy.wait_recv()
    gby_copies = gather_y(g2b, gby_sems)
    place_y(2, y_copies[2])
    for copy in gby_copies:
        copy.wait_recv()
    for s in range(count_y):
        b2[:, 4 * s : 4 * s + 4, :] = g2b[s]

    for low, high in chunks(0, 16, 4):
        d = inv2[low:high] * b2[low:high] * (1.0 / CENTER)
        d2[low:high] = d
        x2a[low:high] = d

    def step_2(old, new, low, high, step):
        keep_old, keep_new = STEPS[step]
        for lo, hi in chunks(low, high, 2):
            r = rows(b2, lo, hi) - operator_2(old, faces2, lo, hi)
            d = keep_old * rows(d2, lo, hi) + keep_new * (rows(inv2, lo, hi) * r)
            put_rows(d2, lo, hi, d)
            put_rows(new, lo, hi, rows(old, lo, hi) + d)

    step_2(x2a, x2b, 0, 16, 0)
    step_2(x2b, x2a, 0, 16, 1)
    for low, high in chunks(0, 16, 2):
        r = b2[low:high] - operator_2(x2a, faces2, low, high)
        r = r + roll(r, 64, 2)
        tmp2[0, low:high] = r + roll(r, -1, 2)
    b3[...] = 0.125 * (tmp2[0, :, first16, :] + tmp2[0, :, second16, :])

    d = inv3[...] * b3[...] * (1.0 / CENTER)
    d3[...] = d
    x3a[...] = d

    def step_3(old, new, low, high, step):
        keep_old, keep_new = STEPS[step]
        for lo, hi in chunks(low, high, 4):
            r = rows(b3, lo, hi) - operator_3(old, faces3, lo, hi)
            d = keep_old * rows(d3, lo, hi) + keep_new * (rows(inv3, lo, hi) * r)
            put_rows(d3, lo, hi, d)
            put_rows(new, lo, hi, rows(old, lo, hi) + d)

    step_3(x3a, x3b, 0, 16, 0)
    step_3(x3b, x3a, 0, 16, 1)

    e = x3a[...]
    e = jnp.where(lane_of(e.shape) % 2 == 0, e, roll(e, 1, 2))
    dup2[:, first16, :] = e
    dup2[:, second16, :] = e
    for low, high in chunks(-3, 8, 4):
        put_rows(x2b, low, high, rows(x2a, low, high) + rows(dup2, low, high))
    for low, high in chunks(-2, 7, 2):
        r = rows(b2, low, high) - operator_2(x2b, faces2, low, high)
        d = rows(inv2, low, high) * r * (1.0 / CENTER)
        put_rows(d2, low, high, d)
        put_rows(x2a, low, high, rows(x2b, low, high) + d)
    step_2(x2a, x2b, -1, 6, 0)
    step_2(x2b, x2a, 0, 5, 1)

    spread = [
        jnp.where((column // 2 + 16) % 64 + 64 * p == row, 1.0, 0.0).astype(F32) for p in range(2)
    ]
    e = x2a[0:5, 0:16, :].reshape(80, 128)
    for p in range(2):
        value = dot(e, spread[p]).reshape(5, 16, 128)
        dup21[p, :, first16, :] = value
        dup21[p, :, second16, :] = value
    for i in range(3, 17):
        x1b[i] = x1a[i] + dup21[(i // 2) % 2, i // 4, 0:24, :]
    for low, high in chunks(4, 16, 4):
        r = b1[low:high] - operator_1(x1b, f1, low, high)
        d = inv1[low:high] * r * (1.0 / CENTER)
        d1[low:high] = d
        x1a[low:high] = x1b[low:high] + d
    step_1(x1a, x1b, 5, 15, 0)
    step_1(x1b, x1a, 6, 14, 1)

    e = x1a[6:14]
    dup1[:, pl.ds(0, 24, stride=2), :] = e
    dup1[:, pl.ds(1, 24, stride=2), :] = e
    lower = lax.broadcasted_iota(jnp.int32, (8, 128), 0) < 4
    for i in range(1, 15):
        j = i // 2
        brick = dup1[j, 16:32, :]
        edge = jnp.where(lower, dup1[j, 32:40, :], dup1[j, 8:16, :])
        for t in range(2):
            xb[i, t, 0:16, :] = best[i, t, 0:16, :] + brick
            xb[i, t, 16:24, :] = best[i, t, 16:24, :] + edge
    for lo, hi in chunks(2, 14, 2):
        applied = operator_0(xb, faces0, lo, hi)
        for t in range(2):
            r = source[lo:hi, t] - applied[t]
            d = inv[lo:hi, t] * r * (1.0 / CENTER)
            dd[lo:hi, t] = d
            xa[lo:hi, t] = xb[lo:hi, t] + d
    step_0(xa, xb, 3, 13, 0)

    def to_own(lo, hi, t, value):
        own[t, lo - 4 : hi - 4] = value[:, 0:16, :]

    step_0(xb, None, 4, 12, 1, to_own)
    join = [
        jnp.where((column == 2 * row + t) & (row < 64), 1.0, 0.0).astype(F32) for t in range(2)
    ]
    result = dot(own[0].reshape(128, 128), join[0]) + dot(own[1].reshape(128, 128), join[1])
    out_ref[...] = result.reshape(8, 16, 128)

    for copy in pending:
        copy.wait_send()


def solution(mesh):
    sizes = (mesh.shape["gx"], mesh.shape["gy"], mesh.shape["gz"])
    count_x, count_y, _ = sizes
    vmem = lambda *shape: pltpu.VMEM(shape, F32)
    sems = lambda count: pltpu.SemaphoreType.DMA((2, count))
    fine = (16, 2, 24, 128)
    level1 = (20, 24, 128)
    level2 = (16, 32, 128)
    level3 = (16, 16, 128)
    scratch = [
        vmem(2, 8, 16, 128),
        vmem(2, 8, 16, 128),
        vmem(2, 2, 4, 16, 128),
        vmem(2, 2, 4, 16, 128),
        vmem(3, *fine),
        vmem(3, 2, 16, 2, 4, 128),
        vmem(3, 2, 16, 2, 4, 128),
        vmem(*fine),
        vmem(*fine),
        vmem(*fine),
        vmem(*fine),
        vmem(*fine),
        vmem(*fine),
        vmem(*fine),
        vmem(3, 4, 16, 128),
        vmem(20, 3, 24, 128),
        vmem(*level1),
        vmem(*level1),
        vmem(*level1),
        vmem(*level1),
        vmem(*level1),
        vmem(3, 8, 128),
        vmem(8, 48, 128),
        vmem(count_y, count_x, 3, 4, 128),
        vmem(count_y, count_x, 4, 128),
        vmem(3, *level2),
        vmem(*level2),
        vmem(*level2),
        vmem(*level2),
        vmem(*level2),
        vmem(*level2),
        vmem(3, *level2),
        vmem(3, *level3),
        vmem(*level3),
        vmem(*level3),
        vmem(*level3),
        vmem(*level3),
        vmem(*level3),
        vmem(*level2),
        vmem(2, 5, 32, 128),
        pltpu.SemaphoreType.DMA((2,)),
        sems(4),
        sems(6),
        sems(6),
        sems(4),
        sems(2),
        sems(4),
        sems(2),
        sems(count_x - 1),
        sems(count_y - 1),
        sems(count_x - 1),
        sems(count_y - 1),
    ]

    def shards(pressure_source, conductivity):
        return pl.pallas_call(
            functools.partial(kernel, sizes),
            out_shape=jax.ShapeDtypeStruct((8, 16, 128), F32),
            in_specs=[pl.BlockSpec(memory_space=pl.ANY)] * 2,
            out_specs=pl.BlockSpec(memory_space=pltpu.VMEM),
            scratch_shapes=scratch,
            compiler_params=pltpu.CompilerParams(
                collective_id=0, has_side_effects=True, vmem_limit_bytes=48 * 1024 * 1024
            ),
        )(pressure_source, conductivity)

    placed = (P("gx", "gy", "gz"), P("gx", "gy", "gz"))
    return jax.shard_map(
        shards, mesh=mesh, in_specs=placed, out_specs=P("gx", "gy", "gz"), check_vma=False
    )
```

time: 561 us -> 71.3 us (0.13)
  starting transfers between devices: 349 us -> 0 us
  waiting for transfers between devices: 129 us -> 0 us
  Pallas kernels: 0 us -> 68.8 us
  local copies, waits for them, and re-layouts: 53.7 us -> 2.31 us
  other arithmetic: 22.8 us -> 0 us
    ppermute x126 -> x0, starting transfers between devices: 349 us -> none  [the longest x63 215 us: padded_2(): lax.ppermute(head, axis, [((i + 1) % count, i) for i in range(count)])]
    ppermute x126 -> x0, waiting for transfers between devices: 129 us -> none  [the longest x63 111 us: padded_2(): lax.ppermute(tail, axis, [(i, (i + 1) % count) for i in range(count)])]
    pallas_call x0 -> x1, Pallas kernels: none -> 68.8 us  [shards(): pl.pallas_call(functools.partial(kernel, sizes), out_shape=jax.ShapeDtype...]
    squeeze x18 -> x0, local copies, waits for them, and re-layouts: 36.9 us -> none  [the longest x3 6.15 us: coarsen_faces(): blocks[2][..., 0].sum(axis=(1, 3))]
    reduce_sum x22 -> x0, other arithmetic: 18.3 us -> none  [the longest x3 4.11 us: coarsen_faces(): blocks[5][..., 1].sum(axis=(1, 3))]
    reshape x4 -> x0, local copies, waits for them, and re-layouts: 10.3 us -> none  [the longest x2 6.06 us: restrict(): blocks = field_in.reshape(size_x // 2, 2, size_y // 2, 2, size_z // 2, 2)]
  transfers between devices with their start and end apart: 126 -> 0, of which waited for: 86 -> 0; matrix products, arithmetic and copies ran while one was open for 10% -> 0% of each run, Pallas kernels for 0% -> 0%
where the time goes in v1:
time: 71.3 us; the launch traced here: 71.1 us
  Pallas kernels  68.8 us (96%)
  local copies, waits for them, and re-layouts  2.31 us (3%)
    pallas_call x1, Pallas kernels, shards(): pl.pallas_call(functools.partial(kernel, sizes), out_shape=jax.ShapeDtype...  68.8 us
    unnamed x5, local copies, waits for them, and re-layouts  2.31 us

profile of v1, /device:TPU:1, one launch (start us, length us, event | category | flops | bytes accessed | tf_op | source)
XLA Modules:
  0.0 71.1 jit_solution(8591543957088128036)
XLA Ops:
  0.0 0.0 copy-start
  0.0 0.8 %copy-done = f32[8,16,128]{2,1,0:T(8,128)S(1)} copy-done((f32[8,16,128]{2,1,0:T(8,128)S(1)}, f32[8,16,128]{2,1,0:T(8,128)}, u32[]{:S(2)}) %copy-start) | copy-done | bytes 65560
  0.8 0.0 copy-start.1
  0.8 0.8 %copy-done.1 = f32[8,16,128]{2,1,0:T(8,128)S(1)} copy-done((f32[8,16,128]{2,1,0:T(8,128)S(1)}, f32[8,16,128]{2,1,0:T(8,128)}, u32[]{:S(2)}) %copy-start.1) | copy-done | bytes 65560
  1.7 68.8 %shard_map.28 = f32[8,16,128]{2,1,0:T(8,128)S(1)} custom-call(f32[8,16,128]{2,1,0:T(8,128)S(1)} %copy-done, f32[8,16,128]{2,1,0:T(8,128)S(1)} %copy-done.1), custom_call_target="tpu_custom_call" | custom-call | tf_op jit(solution)/shard_map/pallas_call | solution.py:701
  70.5 0.6 copy.4
Async XLA Ops:
  0.0 0.8 %copy-start = (f32[8,16,128]{2,1,0:T(8,128)S(1)}, f32[8,16,128]{2,1,0:T(8,128)}, u32[]{:S(2)}) copy-start(f32[8,16,128]{2,1,0:T(8,128)} %source_hbm.1) | copy-start | bytes 196612
  0.8 0.8 %copy-start.1 = (f32[8,16,128]{2,1,0:T(8,128)S(1)}, f32[8,16,128]{2,1,0:T(8,128)}, u32[]{:S(2)}) copy-start(f32[8,16,128]{2,1,0:T(8,128)} %cond_hbm.1) | copy-start | bytes 196612

commit v2 on v1

--- a/solution.py
+++ b/solution.py
@@ -41,83 +41,86 @@
     return 2.0 * one_side * other_side / (one_side + other_side)
 
 
-def chunks(low, high, size):
-    return [(start, min(start + size, high)) for start in range(low, high, size)]
-
-
-def operator_0(field, faces, low, high):
+def each(low, high, size, body):
+    assert (high - low) % size == 0
+    count = (high - low) // size
+    if count == 1:
+        body(low)
+        return
+
+    def one(i, carry):
+        body(low + i * size)
+        return carry
+
+    lax.fori_loop(0, count, one, 0)
+
+
+def operator_0(field, faces, low, size):
     face_x, face_y, face_z = faces
+    here = pl.ds(low, size)
     result = []
     cells = []
     for t in range(2):
-        v = field[low - 1 : high + 1, t]
-        flux = face_x[low : high + 1, t] * (v[1:] - v[:-1])
+        v = field[pl.ds(low - 1, size + 2), t]
+        flux = face_x[pl.ds(low, size + 1), t] * (v[1:] - v[:-1])
         c = v[1:-1]
         g = flux[:-1] - flux[1:]
-        flux = face_y[low:high, t] * (c - roll(c, 1, 1))
+        flux = face_y[here, t] * (c - roll(c, 1, 1))
         g = g + (flux - roll(flux, -1, 1))
         cells.append(c)
         result.append(g)
-    even = face_z[low:high, 0] * (cells[0] - roll(cells[1], 1, 2))
-    odd = face_z[low:high, 1] * (cells[1] - cells[0])
+    even = face_z[here, 0] * (cells[0] - roll(cells[1], 1, 2))
+    odd = face_z[here, 1] * (cells[1] - cells[0])
     return [result[0] + (even - odd), result[1] + (odd - roll(even, -1, 2))]
 
 
-def operator_1(field, faces, low, high):
-    v = field[low - 1 : high + 1]
-    flux = faces[low : high + 1, 0] * (v[1:] - v[:-1])
+def operator_1(field, faces, low, size):
+    here = pl.ds(low, size)
+    v = field[pl.ds(low - 1, size + 2)]
+    flux = faces[pl.ds(low, size + 1), 0] * (v[1:] - v[:-1])
     c = v[1:-1]
     g = flux[:-1] - flux[1:]
-    flux = faces[low:high, 1] * (c - roll(c, 1, 1))
+    flux = faces[here, 1] * (c - roll(c, 1, 1))
     g = g + (flux - roll(flux, -1, 1))
-    flux = faces[low:high, 2] * (c - roll(c, 1, 2))
+    flux = faces[here, 2] * (c - roll(c, 1, 2))
     return g + (flux - roll(flux, -1, 2))
 
 
-def rows(ref, low, high):
-    pieces = []
-    at = low
-    while at < high:
-        start = at % 16
-        stop = min(16, start + high - at)
-        pieces.append(ref[start:stop])
-        at += stop - start
-    return pieces[0] if len(pieces) == 1 else jnp.concatenate(pieces, axis=0)
-
-
-def put_rows(ref, low, high, value):
-    at = low
-    while at < high:
-        start = at % 16
-        stop = min(16, start + high - at)
-        ref[start:stop] = value[at - low : at - low + stop - start]
-        at += stop - start
-
-
-def operator_2(field, faces, low, high):
+def rows(ref, low, size):
+    return jnp.concatenate(
+        [ref[pl.ds(lax.rem(low + (k + 16), 16), 1)] for k in range(size)], axis=0
+    )
+
+
+def put_rows(ref, low, value):
+    for k in range(value.shape[0]):
+        ref[pl.ds(lax.rem(low + (k + 16), 16), 1)] = value[k : k + 1]
+
+
+def operator_2(field, faces, low, size):
     face_x, face_y, face_z = faces
-    v = rows(field, low - 1, high + 1)
+    v = rows(field, low - 1, size + 2)
     half = lane_of(v[:-1].shape) < 64
     turned = roll(v, 64, 2)
-    flux = rows(face_x, low, high + 1) * (v[1:] - jnp.where(half, turned[:-1], turned[1:]))
+    flux = rows(face_x, low, size + 1) * (v[1:] - jnp.where(half, turned[:-1], turned[1:]))
     turned = roll(flux, 64, 2)
     g = flux[:-1] - jnp.where(half[1:], turned[:-1], turned[1:])
     c = v[1:-1]
-    flux = rows(face_y, low, high) * (c - roll(c, 1, 1))
+    flux = rows(face_y, low, size) * (c - roll(c, 1, 1))
     g = g + (flux - roll(flux, -1, 1))
-    flux = rows(face_z, low, high) * (c - roll(c, 1, 2))
+    flux = rows(face_z, low, size) * (c - roll(c, 1, 2))
     return g + (flux - roll(flux, -1, 2))
 
 
-def operator_3(field, faces, low, high):
+def operator_3(field, faces, low, size):
     face_x, face_y, face_z = faces
-    v = rows(field, low - 1, high + 1)
-    flux = rows(face_x, low, high + 1) * (v[1:] - v[:-1])
+    v = rows(field, low - 1, size + 2)
+    flux = rows(face_x, low, size + 1) * (v[1:] - v[:-1])
     g = flux[:-1] - flux[1:]
     c = v[1:-1]
-    flux = rows(face_y, low, high) * (c - roll(c, 1, 1))
+    flux = rows(face_y, low, size) * (c - roll(c, 1, 1))
     g = g + (flux - roll(flux, -1, 1))
-    flux = rows(face_z, low, high) * (c - roll(c, 2, 2))
+    flux = rows(face_z, low, size) * (c - roll(c, 2, 2))
     return g + (flux - roll(flux, -2, 2))
 
 
@@ -310,16 +313,19 @@
 
     cond, source, best = win.at[0], win.at[1], win.at[2]
     faces0 = (fx, fy, fz)
-    for low, high in chunks(1, 16, 4):
-        for t in range(2):
-            k = cond[low - 1 : high, t]
-            fx[low:high, t] = harmonic(k[1:], k[:-1])
-    for low, high in chunks(1, 15, 4):
-        k0, k1 = cond[low:high, 0], cond[low:high, 1]
-        fy[low:high, 0] = harmonic(k0, roll(k0, 1, 1))
-        fy[low:high, 1] = harmonic(k1, roll(k1, 1, 1))
-        fz[low:high, 0] = harmonic(k0, roll(k1, 1, 2))
-        fz[low:high, 1] = harmonic(k1, k0)
+
+    def fine_faces(low):
+        here = pl.ds(low, 2)
+        k0, k1 = cond[here, 0], cond[here, 1]
+        fx[here, 0] = harmonic(k0, cond[pl.ds(low - 1, 2), 0])
+        fx[here, 1] = harmonic(k1, cond[pl.ds(low - 1, 2), 1])
+        fy[here, 0] = harmonic(k0, roll(k0, 1, 1))
+        fy[here, 1] = harmonic(k1, roll(k1, 1, 1))
+        fz[here, 0] = harmonic(k0, roll(k1, 1, 2))
+        fz[here, 1] = harmonic(k1, k0)
+
+    each(1, 15, 2, fine_faces)
+    fx[15] = harmonic(cond[15], cond[14])
 
     for i in range(4):
         tmp0[0, i] = fx[4 + 2 * i, 0, 0:16, :] + fx[4 + 2 * i, 1, 0:16, :]
@@ -375,36 +381,71 @@
             for step in range(1, count_y)
         ]
 
+    sibling = {"gy": me_y + 1 - 2 * lax.rem(me_y, 2)}
+    shift = lax.rem(me_y, 2) * 2 + (count_y - 1)
+
+    def hand_on(ref, sems, place):
+        return send(
+            ref.at[place],
+            ref.at[lax.rem(place + shift, count_y)],
+            sems,
+            count_y + place,
+            sibling,
+        )
+
+    def gather_y_shared(ref, sems):
+        places = [(1 - step) % count_y for step in range(2, count_y, 2)]
+        far = {
+            place: send(ref.at[1], ref.at[place], sems, place, at_y(1 - place + count_y))
+            for place in places
+        }
+        return far, [hand_on(ref, sems, 1)]
+
+    def hand_on_all(ref, sems, far, handed):
+        for place, copy in far.items():
+            copy.wait_recv()
+            handed.append(hand_on(ref, sems, place))
+
     gfx_copies = gather_x(g2f, gfx_sems)
 
-    for low, high in chunks(1, 15, 2):
-        x_sum = [fx[low:high, t] + fx[low + 1 : high + 1, t] for t in range(2)]
-        y_sum = [fy[low:high, t] + roll(fy[low:high, t], -1, 1) for t in range(2)]
-        z0, z1 = fz[low:high, 0], fz[low:high, 1]
-        inv[low:high, 0] = 1.0 / ((x_sum[0] + y_sum[0]) + (z0 + z1))
-        inv[low:high, 1] = 1.0 / ((x_sum[1] + y_sum[1]) + (z1 + roll(z0, -1, 2)))
+    def inverse_0(low):
+        here, after = pl.ds(low, 2), pl.ds(low + 1, 2)
+        x_sum = [fx[here, t] + fx[after, t] for t in range(2)]
+        y_sum = [fy[here, t] + roll(fy[here, t], -1, 1) for t in range(2)]
+        z0, z1 = fz[here, 0], fz[here, 1]
+        inv[here, 0] = 1.0 / ((x_sum[0] + y_sum[0]) + (z0 + z1))
+        inv[here, 1] = 1.0 / ((x_sum[1] + y_sum[1]) + (z1 + roll(z0, -1, 2)))
+
+    each(1, 15, 2, inverse_0)
 
     place_y(1, y_copies[1])
-    for low, high in chunks(1, 15, 4):
-        for t in range(2):
-            d = inv[low:high, t] * source[low:high, t] * (1.0 / CENTER)
-            dd[low:high, t] = d
-            xa[low:high, t] = d
-
-    def step_0(old, new, low, high, step, target=None):
+
+    def first_0(low):
+        here = pl.ds(low, 2)
+        d = inv[here] * source[here] * (1.0 / CENTER)
+        dd[here] = d
+        xa[here] = d
+
+    each(1, 15, 2, first_0)
+
+    def step_0(old, new, low, high, size, step, target=None):
         keep_old, keep_new = STEPS[step]
-        for lo, hi in chunks(low, high, 2):
-            applied = operator_0(old, faces0, lo, hi)
+
+        def one(lo):
+            here = pl.ds(lo, size)
+            applied = operator_0(old, faces0, lo, size)
             for t in range(2):
-                r = source[lo:hi, t] - applied[t]
-                d = keep_old * dd[lo:hi, t] + keep_new * (inv[lo:hi, t] * r)
+                r = source[here, t] - applied[t]
+                d = keep_old * dd[here, t] + keep_new * (inv[here, t] * r)
                 if target is None:
-                    dd[lo:hi, t] = d
-                    new[lo:hi, t] = old[lo:hi, t] + d
+                    dd[here, t] = d
+                    new[here, t] = old[here, t] + d
                 else:
-                    target(lo, hi, t, old[lo:hi, t] + d)
-
-    step_0(xa, xb, 2, 14, 0)
+                    target(lo, t, old[here, t] + d)
+
+        each(low, high, size, one)
+
+    step_0(xa, xb, 2, 14, 4, 0)
 
     for copy in f1x_copies:
         copy.wait_recv()
@@ -418,14 +459,20 @@
         )
         for slot, step in enumerate((-1, 1))
     ]
-    step_0(xb, xa, 3, 13, 1)
+    step_0(xb, xa, 3, 13, 5, 1)
     best[4:12, :, 0:16, :] = xa[4:12, :, 0:16, :]
-    for i in range(4):
-        applied = operator_0(xa, faces0, 4 + 2 * i, 6 + 2 * i)
-        r = (source[4 + 2 * i : 6 + 2 * i, 0, 0:16, :] - applied[0][:, :16]) + (
-            source[4 + 2 * i : 6 + 2 * i, 1, 0:16, :] - applied[1][:, :16]
-        )
-        tmp0[0, i] = r[0] + r[1]
+
+    def residual_0(low):
+        here = pl.ds(low, 4)
+        applied = operator_0(xa, faces0, low, 4)
+        r = (source[here, 0, 0:16, :] - applied[0][:, :16]) + (
+            source[here, 1, 0:16, :] - applied[1][:, :16]
+        )
+        half = (low - 4) // 2
+        tmp0[0, pl.ds(half, 1)] = r[0:1] + r[1:2]
+        tmp0[0, pl.ds(half + 1, 1)] = r[2:3] + r[3:4]
+
+    each(4, 12, 4, residual_0)
     b1[8:12, 8:16, :] = 0.125 * (tmp0[0, :, first, :] + tmp0[0, :, second, :])
     b1x_copies = [
         send(
@@ -437,18 +484,17 @@
         )
         for slot, step in enumerate((-1, 1, -2, 2))
     ]
-    x_copies.append(send_x(2))
-    for copy in gfx_copies:
-        copy.wait_recv()
-    gfy_copies = gather_y(g2f, gfy_sems)
 
     for copy in f1y_copies:
         copy.wait_recv()
-    for low, high in chunks(1, 19, 6):
-        x_sum = f1[low:high, 0] + f1[low + 1 : high + 1, 0]
-        y_term, z_term = f1[low:high, 1], f1[low:high, 2]
+    def inverse_1(low):
+        here = pl.ds(low, 6)
+        x_sum = f1[here, 0] + f1[pl.ds(low + 1, 6), 0]
+        y_term, z_term = f1[here, 1], f1[here, 2]
         y_sum = y_term + roll(y_term, -1, 1)
-        inv1[low:high] = 1.0 / ((x_sum + y_sum) + (z_term + roll(z_term, -1, 2)))
+        inv1[here] = 1.0 / ((x_sum + y_sum) + (z_term + roll(z_term, -1, 2)))
+
+    each(1, 19, 6, inverse_1)
 
     for copy in b1x_copies:
         copy.wait_recv()
@@ -462,28 +508,38 @@
         )
         for slot, step in enumerate((-1, 1))
     ]
-    for copy in x_copies[2]:
+    x_copies.append(send_x(2))
+    for copy in gfx_copies:
         copy.wait_recv()
-    y_copies.append(send_y(2))
+    gfy_far, gfy_copies = gather_y_shared(g2f, gfy_sems)
     for copy in b1y_copies:
         copy.wait_recv()
 
-    for low, high in chunks(1, 19, 6):
-        d = inv1[low:high] * b1[low:high] * (1.0 / CENTER)
-        d1[low:high] = d
-        x1a[low:high] = d
-
-    def step_1(old, new, low, high, step):
+
+    def first_1(low):
+        here = pl.ds(low, 6)
+        d = inv1[here] * b1[here] * (1.0 / CENTER)
+        d1[here] = d
+        x1a[here] = d
+
+    each(1, 19, 6, first_1)
+
+    def step_1(old, new, low, high, size, step):
         keep_old, keep_new = STEPS[step]
-        for lo, hi in chunks(low, high, 4):
-            r = b1[lo:hi] - operator_1(old, f1, lo, hi)
-            d = keep_old * d1[lo:hi] + keep_new * (inv1[lo:hi] * r)
-            d1[lo:hi] = d
-            new[lo:hi] = old[lo:hi] + d
-
-    step_1(x1a, x1b, 2, 18, 0)
-    step_1(x1b, x1a, 3, 17, 1)
-    r = (b1[8:12] - operator_1(x1a, f1, 8, 12))[:, 8:16]
+
+        def one(lo):
+            here = pl.ds(lo, size)
+            r = b1[here] - operator_1(old, f1, lo, size)
+            d = keep_old * d1[here] + keep_new * (inv1[here] * r)
+            d1[here] = d
+            new[here] = old[here] + d
+
+        each(low, high, size, one)
+
+    step_1(x1a, x1b, 2, 18, 4, 0)
+    hand_on_all(g2f, gfy_sems, gfy_far, gfy_copies)
+    step_1(x1b, x1a, 3, 17, 7, 1)
+    r = (b1[8:12] - operator_1(x1a, f1, 8, 4))[:, 8:16]
     tmp1[0] = dot(r[0] + r[1], pack[0]) + dot(r[2] + r[3], pack[1])
     g2b[1, 2] = 0.125 * (tmp1[0, first4, :] + tmp1[0, second4, :])
     gbx_copies = gather_x(g2b, gbx_sems)
@@ -494,92 +550,118 @@
         for s in range(count_y):
             f2[f, :, 4 * s : 4 * s + 4, :] = g2f[s, :, f]
     faces2 = (f2.at[0], f2.at[1], f2.at[2])
-    for low, high in chunks(0, 16, 4):
-        terms = rows(faces2[0], low, high + 1)
+
+    def inverse_2(low):
+        here = pl.ds(low, 4)
+        terms = rows(faces2[0], low, 5)
         turned = roll(terms, 64, 2)
         half = lane_of(terms[1:].shape) < 64
         x_sum = terms[:-1] + jnp.where(half, turned[:-1], turned[1:])
-        y_term, z_term = f2[1, low:high], f2[2, low:high]
+        y_term, z_term = f2[1, here], f2[2, here]
         y_sum = y_term + roll(y_term, -1, 1)
-        inv2[low:high] = 1.0 / ((x_sum + y_sum) + (z_term + roll(z_term, -1, 2)))
-
-        x_low = f2[0, low:high]
-        x_low = jnp.where(half, x_low, roll(x_low, 64, 2))
-        tmp2[0, low:high] = x_low + roll(x_low, -1, 2)
+        inv2[here] = 1.0 / ((x_sum + y_sum) + (z_term + roll(z_term, -1, 2)))
+
+        x_low = jnp.where(half, terms[:-1], turned[:-1])
+        tmp2[0, here] = x_low + roll(x_low, -1, 2)
         y_both = y_term + roll(y_term, 64, 2)
-        tmp2[1, low:high] = y_both + roll(y_both, -1, 2)
-        tmp2[2, low:high] = z_term + roll(z_term, 64, 2)
+        tmp2[1, here] = y_both + roll(y_both, -1, 2)
+        tmp2[2, here] = z_term + roll(z_term, 64, 2)
+
+    each(0, 16, 4, inverse_2)
     first16, second16 = pl.ds(0, 16, stride=2), pl.ds(1, 16, stride=2)
     f3[0] = 0.125 * (tmp2[0, :, first16, :] + tmp2[0, :, second16, :])
     f3[1] = 0.125 * tmp2[1, :, first16, :]
     f3[2] = 0.125 * (tmp2[2, :, first16, :] + tmp2[2, :, second16, :])
     faces3 = (f3.at[0], f3.at[1], f3.at[2])
-    for low, high in chunks(0, 16, 8):
-        terms = rows(faces3[0], low, high + 1)
-        y_term, z_term = f3[1, low:high], f3[2, low:high]
-        inv3[low:high] = 1.0 / (
+
+    def inverse_3(low):
+        here = pl.ds(low, 8)
+        terms = rows(faces3[0], low, 9)
+        y_term, z_term = f3[1, here], f3[2, here]
+        inv3[here] = 1.0 / (
             (terms[:-1] + terms[1:] + (y_term + roll(y_term, -1, 1)))
             + (z_term + roll(z_term, -2, 2))
         )
+
+    each(0, 16, 8, inverse_3)
 
     for copy in gbx_copies:
         copy.wait_recv()
     gby_copies = gather_y(g2b, gby_sems)
-    place_y(2, y_copies[2])
+    for copy in x_copies[2]:
+        copy.wait_recv()
+    y_copies.append(send_y(2))
     for copy in gby_copies:
         copy.wait_recv()
     for s in range(count_y):
         b2[:, 4 * s : 4 * s + 4, :] = g2b[s]
 
-    for low, high in chunks(0, 16, 4):
-        d = inv2[low:high] * b2[low:high] * (1.0 / CENTER)
-        d2[low:high] = d
-        x2a[low:high] = d
-
-    def step_2(old, new, low, high, step):
+
+    def first_2(low):
+        here = pl.ds(low, 4)
+        d = inv2[here] * b2[here] * (1.0 / CENTER)
+        d2[here] = d
+        x2a[here] = d
+
+    each(0, 16, 4, first_2)
+
+    def step_2(old, new, low, high, size, step):
         keep_old, keep_new = STEPS[step]
-        for lo, hi in chunks(low, high, 2):
-            r = rows(b2, lo, hi) - operator_2(old, faces2, lo, hi)
-            d = keep_old * rows(d2, lo, hi) + keep_new * (rows(inv2, lo, hi) * r)
-            put_rows(d2, lo, hi, d)
-            put_rows(new, lo, hi, rows(old, lo, hi) + d)
-
-    step_2(x2a, x2b, 0, 16, 0)
-    step_2(x2b, x2a, 0, 16, 1)
-    for low, high in chunks(0, 16, 2):
-        r = b2[low:high] - operator_2(x2a, faces2, low, high)
+
+        def one(lo):
+            r = rows(b2, lo, size) - operator_2(old, faces2, lo, size)
+            d = keep_old * rows(d2, lo, size) + keep_new * (rows(inv2, lo, size) * r)
+            put_rows(d2, lo, d)
+            put_rows(new, lo, rows(old, lo, size) + d)
+
+        each(low, high, size, one)
+
+    step_2(x2a, x2b, 0, 16, 4, 0)
+    step_2(x2b, x2a, 0, 16, 4, 1)
+
+    def residual_2(low):
+        here = pl.ds(low, 4)
+        r = b2[here] - operator_2(x2a, faces2, low, 4)
         r = r + roll(r, 64, 2)
-        tmp2[0, low:high] = r + roll(r, -1, 2)
+        tmp2[0, here] = r + roll(r, -1, 2)
+
+    each(0, 16, 4, residual_2)
     b3[...] = 0.125 * (tmp2[0, :, first16, :] + tmp2[0, :, second16, :])
 
     d = inv3[...] * b3[...] * (1.0 / CENTER)
     d3[...] = d
     x3a[...] = d
 
-    def step_3(old, new, low, high, step):
+    def step_3(old, new, step):
         keep_old, keep_new = STEPS[step]
-        for lo, hi in chunks(low, high, 4):
-            r = rows(b3, lo, hi) - operator_3(old, faces3, lo, hi)
-            d = keep_old * rows(d3, lo, hi) + keep_new * (rows(inv3, lo, hi) * r)
-            put_rows(d3, lo, hi, d)
-            put_rows(new, lo, hi, rows(old, lo, hi) + d)
-
-    step_3(x3a, x3b, 0, 16, 0)
-    step_3(x3b, x3a, 0, 16, 1)
+
+        def one(lo):
+            here = pl.ds(lo, 4)
+            r = b3[here] - operator_3(old, faces3, lo, 4)
+            d = keep_old * d3[here] + keep_new * (inv3[here] * r)
+            d3[here] = d
+            new[here] = old[here] + d
+
+        each(0, 16, 4, one)
+
+    step_3(x3a, x3b, 0)
+    step_3(x3b, x3a, 1)
 
     e = x3a[...]
     e = jnp.where(lane_of(e.shape) % 2 == 0, e, roll(e, 1, 2))
     dup2[:, first16, :] = e
     dup2[:, second16, :] = e
-    for low, high in chunks(-3, 8, 4):
-        put_rows(x2b, low, high, rows(x2a, low, high) + rows(dup2, low, high))
-    for low, high in chunks(-2, 7, 2):
-        r = rows(b2, low, high) - operator_2(x2b, faces2, low, high)
-        d = rows(inv2, low, high) * r * (1.0 / CENTER)
-        put_rows(d2, low, high, d)
-        put_rows(x2a, low, high, rows(x2b, low, high) + d)
-    step_2(x2a, x2b, -1, 6, 0)
-    step_2(x2b, x2a, 0, 5, 1)
+    x2b[...] = x2a[...] + dup2[...]
+
+    def first_up_2(low):
+        r = rows(b2, low, 5) - operator_2(x2b, faces2, low, 5)
+        d = rows(inv2, low, 5) * r * (1.0 / CENTER)
+        put_rows(d2, low, d)
+        put_rows(x2a, low, rows(x2b, low, 5) + d)
+
+    each(-2, 8, 5, first_up_2)
+    step_2(x2a, x2b, -1, 7, 4, 0)
+    step_2(x2b, x2a, 0, 5, 5, 1)
 
     spread = [
         jnp.where((column // 2 + 16) % 64 + 64 * p == row, 1.0, 0.0).astype(F32) for p in range(2)
@@ -589,40 +671,57 @@
         value = dot(e, spread[p]).reshape(5, 16, 128)
         dup21[p, :, first16, :] = value
         dup21[p, :, second16, :] = value
-    for i in range(3, 17):
-        x1b[i] = x1a[i] + dup21[(i // 2) % 2, i // 4, 0:24, :]
-    for low, high in chunks(4, 16, 4):
-        r = b1[low:high] - operator_1(x1b, f1, low, high)
-        d = inv1[low:high] * r * (1.0 / CENTER)
-        d1[low:high] = d
-        x1a[low:high] = x1b[low:high] + d
-    step_1(x1a, x1b, 5, 15, 0)
-    step_1(x1b, x1a, 6, 14, 1)
-
+
+    def add_1(quad):
+        for i in range(4):
+            x1b[4 * quad + i] = x1a[4 * quad + i] + dup21[i // 2, quad, 0:24, :]
+
+    each(0, 5, 1, add_1)
+
+    def first_up_1(low):
+        here = pl.ds(low, 4)
+        r = b1[here] - operator_1(x1b, f1, low, 4)
+        d = inv1[here] * r * (1.0 / CENTER)
+        d1[here] = d
+        x1a[here] = x1b[here] + d
+
+    each(4, 16, 4, first_up_1)
+    step_1(x1a, x1b, 5, 15, 5, 0)
+    step_1(x1b, x1a, 6, 14, 4, 1)
+
+    place_y(2, y_copies[2])
     e = x1a[6:14]
     dup1[:, pl.ds(0, 24, stride=2), :] = e
     dup1[:, pl.ds(1, 24, stride=2), :] = e
     lower = lax.broadcasted_iota(jnp.int32, (8, 128), 0) < 4
-    for i in range(1, 15):
-        j = i // 2
-        brick = dup1[j, 16:32, :]
-        edge = jnp.where(lower, dup1[j, 32:40, :], dup1[j, 8:16, :])
+
+    def add_0(pair):
+        brick = dup1[pair, 16:32, :]
+        edge = jnp.where(lower, dup1[pair, 32:40, :], dup1[pair, 8:16, :])
+        for k in range(2):
+            i = 2 * pair + k
+            for t in range(2):
+                xb[i, t, 0:16, :] = best[i, t, 0:16, :] + brick
+                xb[i, t, 16:24, :] = best[i, t, 16:24, :] + edge
+
+    each(0, 8, 1, add_0)
+
+    def first_up_0(low):
+        here = pl.ds(low, 4)
+        applied = operator_0(xb, faces0, low, 4)
         for t in range(2):
-            xb[i, t, 0:16, :] = best[i, t, 0:16, :] + brick
-            xb[i, t, 16:24, :] = best[i, t, 16:24, :] + edge
-    for lo, hi in chunks(2, 14, 2):
-        applied = operator_0(xb, faces0, lo, hi)
-        for t in range(2):
-            r = source[lo:hi, t] - applied[t]
-            d = inv[lo:hi, t] * r * (1.0 / CENTER)
-            dd[lo:hi, t] = d
-            xa[lo:hi, t] = xb[lo:hi, t] + d
-    step_0(xa, xb, 3, 13, 0)
-
-    def to_own(lo, hi, t, value):
-        own[t, lo - 4 : hi - 4] = value[:, 0:16, :]
-
-    step_0(xb, None, 4, 12, 1, to_own)
+            r = source[here, t] - applied[t]
+            d = inv[here, t] * r * (1.0 / CENTER)
+            dd[here, t] = d
+            xa[here, t] = xb[here, t] + d
+
+    each(2, 14, 4, first_up_0)
+    step_0(xa, xb, 3, 13, 5, 0)
+
+    def to_own(low, t, value):
+        own[t, pl.ds(low - 4, 4)] = value[:, 0:16, :]
+
+    step_0(xb, None, 4, 12, 4, 1, to_own)
     join = [
         jnp.where((column == 2 * row + t) & (row < 64), 1.0, 0.0).astype(F32) for t in range(2)
     ]
@@ -692,7 +791,7 @@
         sems(4),
         sems(2),
         sems(count_x - 1),
-        sems(count_y - 1),
+        sems(2 * count_y),
         sems(count_x - 1),
         sems(count_y - 1),
     ]
@@ -701,7 +800,7 @@
         return pl.pallas_call(
             functools.partial(kernel, sizes),
             out_shape=jax.ShapeDtypeStruct((8, 16, 128), F32),
-            in_specs=[pl.BlockSpec(memory_space=pl.ANY)] * 2,
+            in_specs=[pl.BlockSpec(memory_space=pltpu.HBM)] * 2,
             out_specs=pl.BlockSpec(memory_space=pltpu.VMEM),
             scratch_shapes=scratch,
             compiler_params=pltpu.CompilerParams(

time: 71.3 us -> 74.5 us (1.045)
  Pallas kernels: 68.8 us -> 72 us
    pallas_call x1, Pallas kernels: 68.8 us -> 72 us  [shards(): pl.pallas_call(functools.partial(kernel, sizes), out_shape=jax.ShapeDtype...]
where the time goes in v2:
time: 74.5 us; the launch traced here: 74.3 us
  Pallas kernels  72 us (97%)
  local copies, waits for them, and re-layouts  2.31 us (3%)
    pallas_call x1, Pallas kernels, shards(): pl.pallas_call(functools.partial(kernel, sizes), out_shape=jax.ShapeDtype...  72 us
    unnamed x5, local copies, waits for them, and re-layouts  2.31 us

profile of v2, /device:TPU:1, one launch (start us, length us, event | category | flops | bytes accessed | tf_op | source)
XLA Modules:
  0.0 74.3 jit_solution(11434059531352560671)
XLA Ops:
  0.0 0.0 copy-start
  0.0 0.8 %copy-done = f32[8,16,128]{2,1,0:T(8,128)S(1)} copy-done((f32[8,16,128]{2,1,0:T(8,128)S(1)}, f32[8,16,128]{2,1,0:T(8,128)}, u32[]{:S(2)}) %copy-start) | copy-done | bytes 65560
  0.8 0.0 copy-start.1
  0.8 0.8 %copy-done.1 = f32[8,16,128]{2,1,0:T(8,128)S(1)} copy-done((f32[8,16,128]{2,1,0:T(8,128)S(1)}, f32[8,16,128]{2,1,0:T(8,128)}, u32[]{:S(2)}) %copy-start.1) | copy-done | bytes 65560
  1.7 72.0 %shard_map.28 = f32[8,16,128]{2,1,0:T(8,128)S(1)} custom-call(f32[8,16,128]{2,1,0:T(8,128)S(1)} %copy-done, f32[8,16,128]{2,1,0:T(8,128)S(1)} %copy-done.1), custom_call_target="tpu_custom_call" | custom-call | tf_op jit(solution)/shard_map/pallas_call | solution.py:800
  73.6 0.6 copy.4
Async XLA Ops:
  0.0 0.8 %copy-start = (f32[8,16,128]{2,1,0:T(8,128)S(1)}, f32[8,16,128]{2,1,0:T(8,128)}, u32[]{:S(2)}) copy-start(f32[8,16,128]{2,1,0:T(8,128)} %source_hbm.1) | copy-start | bytes 196612
  0.8 0.8 %copy-start.1 = (f32[8,16,128]{2,1,0:T(8,128)S(1)}, f32[8,16,128]{2,1,0:T(8,128)}, u32[]{:S(2)}) copy-start(f32[8,16,128]{2,1,0:T(8,128)} %cond_hbm.1) | copy-start | bytes 196612

commit v3 on v1

--- a/solution.py
+++ b/solution.py
@@ -200,12 +200,17 @@
 
     barrier = pltpu.get_barrier_semaphore()
     partners = [at_z(1), at_z(-1)]
-    partners += [at_x(step) for step in range(1, count_x)]
+    partners += [at_x(sign * step) for step in (1, 2, 3, 5, 6) for sign in (1, -1)]
     partners += [at_y(step) for step in range(1, count_y)]
     for partner in partners:
         pl.semaphore_signal(barrier, inc=1, device_id=partner, device_id_type=MESH)
 
     pending = []
+
+    def drain():
+        for copy in pending:
+            copy.wait_send()
+        pending.clear()
 
     def send(source, target, sems, slot, device):
         copy = pltpu.make_async_remote_copy(
@@ -342,31 +347,10 @@
         for slot, step in enumerate((-1, 1, -2, 2))
     ]
 
-    row = lax.broadcasted_iota(jnp.int32, (128, 128), 0)
-    column = lax.broadcasted_iota(jnp.int32, (128, 128), 1)
-    pack = [
-        jnp.where((row // 2 + 16) % 64 + 64 * p == column, 1.0, 0.0).astype(F32) for p in range(2)
-    ]
-    pack_even = [
-        jnp.where((row % 2 == 0) & ((row // 2 + 16) % 64 + 64 * p == column), 1.0, 0.0).astype(F32)
-        for p in range(2)
-    ]
-    first4, second4 = pl.ds(0, 4, stride=2), pl.ds(1, 4, stride=2)
-    tmp1[0] = dot(f1[8, 0, 8:16, :], pack[0]) + dot(f1[10, 0, 8:16, :], pack[1])
-    tmp1[1] = dot(f1[8, 1, 8:16, :] + f1[9, 1, 8:16, :], pack[0]) + dot(
-        f1[10, 1, 8:16, :] + f1[11, 1, 8:16, :], pack[1]
-    )
-    tmp1[2] = dot(f1[8, 2, 8:16, :] + f1[9, 2, 8:16, :], pack_even[0]) + dot(
-        f1[10, 2, 8:16, :] + f1[11, 2, 8:16, :], pack_even[1]
-    )
-    g2f[1, 2, 0] = 0.125 * (tmp1[0, first4, :] + tmp1[0, second4, :])
-    g2f[1, 2, 1] = 0.125 * tmp1[1, first4, :]
-    g2f[1, 2, 2] = 0.125 * (tmp1[2, first4, :] + tmp1[2, second4, :])
-
-    def gather_x(ref, sems):
+    def spread_x(ref, first, last, sems, steps):
         return [
-            send(ref.at[1, 2], ref.at[1, (2 - step) % count_x], sems, step - 1, at_x(step))
-            for step in range(1, count_x)
+            send(ref.at[1, first:last], ref.at[1, first - step : last - step], sems, slot, at_x(step))
+            for slot, step in enumerate(steps)
         ]
 
     def gather_y(ref, sems):
@@ -375,7 +359,30 @@
             for step in range(1, count_y)
         ]
 
-    gfx_copies = gather_x(g2f, gfx_sems)
+    sibling = {"gy": me_y + 1 - 2 * lax.rem(me_y, 2)}
+    shift = lax.rem(me_y, 2) * 2 + (count_y - 1)
+
+    def hand_on(ref, sems, place):
+        return send(
+            ref.at[place],
+            ref.at[lax.rem(place + shift, count_y)],
+            sems,
+            count_y + place,
+            sibling,
+        )
+
+    def gather_y_shared(ref, sems):
+        places = [(1 - step) % count_y for step in range(2, count_y, 2)]
+        far = {
+            place: send(ref.at[1], ref.at[place], sems, place, at_y(1 - place + count_y))
+            for place in places
+        }
+        return far, [hand_on(ref, sems, 1)]
+
+    def hand_on_all(ref, sems, far, handed):
+        for place, copy in far.items():
+            copy.wait_recv()
+            handed.append(hand_on(ref, sems, place))
 
     for low, high in chunks(1, 15, 2):
         x_sum = [fx[low:high, t] + fx[low + 1 : high + 1, t] for t in range(2)]
@@ -437,19 +444,39 @@
         )
         for slot, step in enumerate((-1, 1, -2, 2))
     ]
-    x_copies.append(send_x(2))
-    for copy in gfx_copies:
-        copy.wait_recv()
-    gfy_copies = gather_y(g2f, gfy_sems)
-
-    for copy in f1y_copies:
-        copy.wait_recv()
-    for low, high in chunks(1, 19, 6):
-        x_sum = f1[low:high, 0] + f1[low + 1 : high + 1, 0]
-        y_term, z_term = f1[low:high, 1], f1[low:high, 2]
-        y_sum = y_term + roll(y_term, -1, 1)
-        inv1[low:high] = 1.0 / ((x_sum + y_sum) + (z_term + roll(z_term, -1, 2)))
-
+
+    row = lax.broadcasted_iota(jnp.int32, (128, 128), 0)
+    column = lax.broadcasted_iota(jnp.int32, (128, 128), 1)
+    pack = [
+        jnp.where((row // 2 + 16) % 64 + 64 * p == column, 1.0, 0.0).astype(F32) for p in range(2)
+    ]
+    pack_even = [
+        jnp.where((row % 2 == 0) & ((row // 2 + 16) % 64 + 64 * p == column), 1.0, 0.0).astype(F32)
+        for p in range(2)
+    ]
+    first4, second4 = pl.ds(0, 4, stride=2), pl.ds(1, 4, stride=2)
+
+    def packed(pieces, matrices):
+        whole = [jnp.concatenate(piece, axis=0) for piece in pieces]
+        result = dot(whole[0], matrices[0]) + dot(whole[1], matrices[1])
+        return result.reshape(len(pieces[0]), 8, 128)
+
+    g2f[1, 15] = jnp.ones((3, 4, 128), F32)
+    g2b[1, 15] = jnp.zeros((4, 128), F32)
+    mine = slice(8, 16)
+    tmp1[0] = packed([[f1[4 * i + 2 * p, 0, mine, :] for i in range(5)] for p in range(2)], pack)
+    for f in (1, 2):
+        pieces = [
+            [f1[4 * i + 2 * p, f, mine, :] + f1[4 * i + 2 * p + 1, f, mine, :] for i in range(5)]
+            for p in range(2)
+        ]
+        tmp1[f] = packed(pieces, (None, pack, pack_even)[f])
+    g2f[1, 5:10, 0] = 0.125 * (tmp1[0, :, first4, :] + tmp1[0, :, second4, :])
+    g2f[1, 5:10, 1] = 0.125 * tmp1[1, :, first4, :]
+    g2f[1, 5:10, 2] = 0.125 * (tmp1[2, :, first4, :] + tmp1[2, :, second4, :])
+    gfx_copies = spread_x(g2f, 5, 10, gfx_sems, (5, -5))
+
+    drain()
     for copy in b1x_copies:
         copy.wait_recv()
     b1y_copies = [
@@ -462,9 +489,14 @@
         )
         for slot, step in enumerate((-1, 1))
     ]
-    for copy in x_copies[2]:
-        copy.wait_recv()
-    y_copies.append(send_y(2))
+    for copy in f1y_copies:
+        copy.wait_recv()
+    for low, high in chunks(1, 19, 6):
+        x_sum = f1[low:high, 0] + f1[low + 1 : high + 1, 0]
+        y_term, z_term = f1[low:high, 1], f1[low:high, 2]
+        y_sum = y_term + roll(y_term, -1, 1)
+        inv1[low:high] = 1.0 / ((x_sum + y_sum) + (z_term + roll(z_term, -1, 2)))
+
     for copy in b1y_copies:
         copy.wait_recv()
 
@@ -482,12 +514,22 @@
             new[lo:hi] = old[lo:hi] + d
 
     step_1(x1a, x1b, 2, 18, 0)
+    for copy in gfx_copies:
+        copy.wait_recv()
+    gfy_far, gfy_copies = gather_y_shared(g2f, gfy_sems)
     step_1(x1b, x1a, 3, 17, 1)
-    r = (b1[8:12] - operator_1(x1a, f1, 8, 12))[:, 8:16]
-    tmp1[0] = dot(r[0] + r[1], pack[0]) + dot(r[2] + r[3], pack[1])
-    g2b[1, 2] = 0.125 * (tmp1[0, first4, :] + tmp1[0, second4, :])
-    gbx_copies = gather_x(g2b, gbx_sems)
-
+    r = (b1[4:16] - operator_1(x1a, f1, 4, 16))[:, 8:16]
+    tmp1[0, 0:3] = packed(
+        [[r[4 * i + 2 * p] + r[4 * i + 2 * p + 1] for i in range(3)] for p in range(2)], pack
+    )
+    g2b[1, 6:9] = 0.125 * (tmp1[0, 0:3, first4, :] + tmp1[0, 0:3, second4, :])
+    gbx_copies = spread_x(g2b, 6, 9, gbx_sems, (3, -3, 6, -6))
+    x_copies.append(send_x(2))
+    for copy in gbx_copies:
+        copy.wait_recv()
+    gby_copies = gather_y(g2b, gby_sems)
+
+    hand_on_all(g2f, gfy_sems, gfy_far, gfy_copies)
     for copy in gfy_copies:
         copy.wait_recv()
     for f in range(3):
@@ -522,10 +564,9 @@
             + (z_term + roll(z_term, -2, 2))
         )
 
-    for copy in gbx_copies:
-        copy.wait_recv()
-    gby_copies = gather_y(g2b, gby_sems)
-    place_y(2, y_copies[2])
+    for copy in x_copies[2]:
+        copy.wait_recv()
+    y_copies.append(send_y(2))
     for copy in gby_copies:
         copy.wait_recv()
     for s in range(count_y):
@@ -571,20 +612,20 @@
     e = jnp.where(lane_of(e.shape) % 2 == 0, e, roll(e, 1, 2))
     dup2[:, first16, :] = e
     dup2[:, second16, :] = e
-    for low, high in chunks(-3, 8, 4):
+    for low, high in chunks(2, 13, 4):
         put_rows(x2b, low, high, rows(x2a, low, high) + rows(dup2, low, high))
-    for low, high in chunks(-2, 7, 2):
+    for low, high in chunks(3, 12, 2):
         r = rows(b2, low, high) - operator_2(x2b, faces2, low, high)
         d = rows(inv2, low, high) * r * (1.0 / CENTER)
         put_rows(d2, low, high, d)
         put_rows(x2a, low, high, rows(x2b, low, high) + d)
-    step_2(x2a, x2b, -1, 6, 0)
-    step_2(x2b, x2a, 0, 5, 1)
+    step_2(x2a, x2b, 4, 11, 0)
+    step_2(x2b, x2a, 5, 10, 1)
 
     spread = [
         jnp.where((column // 2 + 16) % 64 + 64 * p == row, 1.0, 0.0).astype(F32) for p in range(2)
     ]
-    e = x2a[0:5, 0:16, :].reshape(80, 128)
+    e = x2a[5:10, 0:16, :].reshape(80, 128)
     for p in range(2):
         value = dot(e, spread[p]).reshape(5, 16, 128)
         dup21[p, :, first16, :] = value
@@ -599,6 +640,8 @@
     step_1(x1a, x1b, 5, 15, 0)
     step_1(x1b, x1a, 6, 14, 1)
 
+    drain()
+    place_y(2, y_copies[2])
     e = x1a[6:14]
     dup1[:, pl.ds(0, 24, stride=2), :] = e
     dup1[:, pl.ds(1, 24, stride=2), :] = e
@@ -628,9 +671,6 @@
     ]
     result = dot(own[0].reshape(128, 128), join[0]) + dot(own[1].reshape(128, 128), join[1])
     out_ref[...] = result.reshape(8, 16, 128)
-
-    for copy in pending:
-        copy.wait_send()
 
 
 def solution(mesh):
@@ -664,7 +704,7 @@
         vmem(*level1),
         vmem(*level1),
         vmem(*level1),
-        vmem(3, 8, 128),
+        vmem(3, 5, 8, 128),
         vmem(8, 48, 128),
         vmem(count_y, count_x, 3, 4, 128),
         vmem(count_y, count_x, 4, 128),
@@ -691,9 +731,9 @@
         sems(2),
         sems(4),
         sems(2),
-        sems(count_x - 1),
-        sems(count_y - 1),
-        sems(count_x - 1),
+        sems(2),
+        sems(2 * count_y),
+        sems(4),
         sems(count_y - 1),
     ]
 
@@ -701,11 +741,11 @@
         return pl.pallas_call(
             functools.partial(kernel, sizes),
             out_shape=jax.ShapeDtypeStruct((8, 16, 128), F32),
-            in_specs=[pl.BlockSpec(memory_space=pl.ANY)] * 2,
+            in_specs=[pl.BlockSpec(memory_space=pltpu.HBM)] * 2,
             out_specs=pl.BlockSpec(memory_space=pltpu.VMEM),
             scratch_shapes=scratch,
             compiler_params=pltpu.CompilerParams(
-                collective_id=0, has_side_effects=True, vmem_limit_bytes=48 * 1024 * 1024
+                collective_id=0, has_side_effects=True, vmem_limit_bytes=62 * 1024 * 1024
             ),
         )(pressure_source, conductivity)
 

time: 71.3 us -> 62.2 us (0.87)
  Pallas kernels: 68.8 us -> 60.5 us
  local copies, waits for them, and re-layouts: 2.31 us -> 1.47 us
    pallas_call x1, Pallas kernels: 68.8 us -> 60.5 us  [shards(): pl.pallas_call(functools.partial(kernel, sizes), out_shape=jax.ShapeDtype...]
    unnamed x5 -> x1, local copies, waits for them, and re-layouts: 2.31 us -> 1.47 us
where the time goes in v3:
time: 62.2 us; the launch traced here: 62 us
  Pallas kernels  60.5 us (97%)
  local copies, waits for them, and re-layouts  1.47 us (2%)
    pallas_call x1, Pallas kernels, shards(): pl.pallas_call(functools.partial(kernel, sizes), out_shape=jax.ShapeDtype...  60.5 us
    unnamed x1, local copies, waits for them, and re-layouts  1.47 us

profile of v3, /device:TPU:1, one launch (start us, length us, event | category | flops | bytes accessed | tf_op | source)
XLA Modules:
  0.0 62.0 jit_solution(5245354109409129555)
XLA Ops:
  0.0 60.5 %shard_map.28 = f32[8,16,128]{2,1,0:T(8,128)} custom-call(f32[8,16,128]{2,1,0:T(8,128)} %source_hbm.1, f32[8,16,128]{2,1,0:T(8,128)} %cond_hbm.1), custom_call_target="tpu_custom_call" | custom-call | tf_op jit(solution)/shard_map/pallas_call | solution.py:741
  60.5 1.5 %copy.4 = f32[8,16,128]{2,1,0:T(8,128)} copy(f32[8,16,128]{2,1,0:T(8,128)} %shard_map.28) | data formatting | bytes 131072

commit v4 on v3

--- a/solution.py
+++ b/solution.py
@@ -27,14 +27,23 @@
     return lax.broadcasted_iota(jnp.int32, shape, len(shape) - 1)
 
 
-def select_matrix(target):
-    row = lax.broadcasted_iota(jnp.int32, (128, 128), 0)
-    column = lax.broadcasted_iota(jnp.int32, (128, 128), 1)
-    return jnp.where(row == target(column), 1.0, 0.0).astype(F32)
-
-
-def dot(a, b):
-    return jnp.dot(a, b, precision=lax.Precision.HIGHEST, preferred_element_type=F32)
+def select_matrix(shape, holds):
+    row = lax.broadcasted_iota(jnp.int32, shape, 0)
+    column = lax.broadcasted_iota(jnp.int32, shape, 1)
+    return jnp.where(holds(row, column), 1.0, 0.0).astype(jnp.bfloat16)
+
+
+def dot(a, ones):
+    high = a.astype(jnp.bfloat16)
+    rest = a - high.astype(F32)
+    middle = rest.astype(jnp.bfloat16)
+    low = (rest - middle.astype(F32)).astype(jnp.bfloat16)
+    parts = [jnp.dot(part, ones, preferred_element_type=F32) for part in (low, middle, high)]
+    return (parts[0] + parts[1]) + parts[2]
+
+
+def side_by_side(a, b):
+    return jnp.concatenate([a, b], axis=1)
 
 
 def harmonic(one_side, other_side):
@@ -45,80 +54,67 @@
     return [(start, min(start + size, high)) for start in range(low, high, size)]
 
 
-def operator_0(field, faces, low, high):
+def sweep_0(field, faces, low, high, emit):
     face_x, face_y, face_z = faces
-    result = []
-    cells = []
-    for t in range(2):
-        v = field[low - 1 : high + 1, t]
-        flux = face_x[low : high + 1, t] * (v[1:] - v[:-1])
-        c = v[1:-1]
-        g = flux[:-1] - flux[1:]
-        flux = face_y[low:high, t] * (c - roll(c, 1, 1))
-        g = g + (flux - roll(flux, -1, 1))
-        cells.append(c)
-        result.append(g)
-    even = face_z[low:high, 0] * (cells[0] - roll(cells[1], 1, 2))
-    odd = face_z[low:high, 1] * (cells[1] - cells[0])
-    return [result[0] + (even - odd), result[1] + (odd - roll(even, -1, 2))]
-
-
-def operator_1(field, faces, low, high):
-    v = field[low - 1 : high + 1]
-    flux = faces[low : high + 1, 0] * (v[1:] - v[:-1])
-    c = v[1:-1]
-    g = flux[:-1] - flux[1:]
-    flux = faces[low:high, 1] * (c - roll(c, 1, 1))
-    g = g + (flux - roll(flux, -1, 1))
-    flux = faces[low:high, 2] * (c - roll(c, 1, 2))
-    return g + (flux - roll(flux, -1, 2))
-
-
-def rows(ref, low, high):
-    pieces = []
-    at = low
-    while at < high:
-        start = at % 16
-        stop = min(16, start + high - at)
-        pieces.append(ref[start:stop])
-        at += stop - start
-    return pieces[0] if len(pieces) == 1 else jnp.concatenate(pieces, axis=0)
-
-
-def put_rows(ref, low, high, value):
-    at = low
-    while at < high:
-        start = at % 16
-        stop = min(16, start + high - at)
-        ref[start:stop] = value[at - low : at - low + stop - start]
-        at += stop - start
-
-
-def operator_2(field, faces, low, high):
-    face_x, face_y, face_z = faces
-    v = rows(field, low - 1, high + 1)
-    half = lane_of(v[:-1].shape) < 64
-    turned = roll(v, 64, 2)
-    flux = rows(face_x, low, high + 1) * (v[1:] - jnp.where(half, turned[:-1], turned[1:]))
-    turned = roll(flux, 64, 2)
-    g = flux[:-1] - jnp.where(half[1:], turned[:-1], turned[1:])
-    c = v[1:-1]
-    flux = rows(face_y, low, high) * (c - roll(c, 1, 1))
-    g = g + (flux - roll(flux, -1, 1))
-    flux = rows(face_z, low, high) * (c - roll(c, 1, 2))
-    return g + (flux - roll(flux, -1, 2))
-
-
-def operator_3(field, faces, low, high):
-    face_x, face_y, face_z = faces
-    v = rows(field, low - 1, high + 1)
-    flux = rows(face_x, low, high + 1) * (v[1:] - v[:-1])
-    g = flux[:-1] - flux[1:]
-    c = v[1:-1]
-    flux = rows(face_y, low, high) * (c - roll(c, 1, 1))
-    g = g + (flux - roll(flux, -1, 1))
-    flux = rows(face_z, low, high) * (c - roll(c, 2, 2))
-    return g + (flux - roll(flux, -2, 2))
+    both = range(2)
+    here = [field[low, t] for t in both]
+    flux = [face_x[low, t] * (here[t] - field[low - 1, t]) for t in both]
+    for i in range(low, high):
+        after = [field[i + 1, t] for t in both]
+        upper = [face_x[i + 1, t] * (after[t] - here[t]) for t in both]
+        result = []
+        for t in both:
+            side = face_y[i, t] * (here[t] - roll(here[t], 1, 0))
+            result.append((flux[t] - upper[t]) + (side - roll(side, -1, 0)))
+        even = face_z[i, 0] * (here[0] - roll(here[1], 1, 1))
+        odd = face_z[i, 1] * (here[1] - here[0])
+        emit(i, [result[0] + (even - odd), result[1] + (odd - roll(even, -1, 1))], here)
+        here, flux = after, upper
+
+
+def sweep_1(field, faces, low, high, emit):
+    here = field[low]
+    flux = faces[low, 0] * (here - field[low - 1])
+    for i in range(low, high):
+        after = field[i + 1]
+        upper = faces[i + 1, 0] * (after - here)
+        side = faces[i, 1] * (here - roll(here, 1, 0))
+        result = (flux - upper) + (side - roll(side, -1, 0))
+        side = faces[i, 2] * (here - roll(here, 1, 1))
+        emit(i, result + (side - roll(side, -1, 1)), here)
+        here, flux = after, upper
+
+
+def sweep_2(field, faces, low, high, emit):
+    half = lane_of(field.shape[1:]) < 64
+    before, here = roll(field[low - 1], 64, 1), field[low]
+    turned = roll(here, 64, 1)
+    flux = faces[0, low] * (here - jnp.where(half, before, turned))
+    flux_turned = roll(flux, 64, 1)
+    for i in range(low, high):
+        after = field[i + 1]
+        after_turned = roll(after, 64, 1)
+        upper = faces[0, i + 1] * (after - jnp.where(half, turned, after_turned))
+        upper_turned = roll(upper, 64, 1)
+        result = flux - jnp.where(half, flux_turned, upper_turned)
+        side = faces[1, i] * (here - roll(here, 1, 0))
+        result = result + (side - roll(side, -1, 0))
+        side = faces[2, i] * (here - roll(here, 1, 1))
+        emit(i, result + (side - roll(side, -1, 1)), here)
+        here, turned, flux, flux_turned = after, after_turned, upper, upper_turned
+
+
+def sweep_3(field, faces, low, high, emit):
+    here = field[low]
+    flux = faces[0, low] * (here - field[low - 1])
+    for i in range(low, high):
+        after = field[i + 1]
+        upper = faces[0, i + 1] * (after - here)
+        side = faces[1, i] * (here - roll(here, 1, 0))
+        result = (flux - upper) + (side - roll(side, -1, 0))
+        side = faces[2, i] * (here - roll(here, 2, 1))
+        emit(i, result + (side - roll(side, -2, 1)), here)
+        here, flux = after, upper
 
 
 def kernel(
@@ -225,25 +221,23 @@
         pending.append(copy)
         return copy
 
-    keep = select_matrix(lambda l: jnp.where(l < 64, 2 * l, 2 * (l - 64) + 1))
-    down_a = select_matrix(
-        lambda l: jnp.where(l < 64, -1, jnp.where(l < 96, 2 * (l - 64), 2 * (l - 96) + 1))
-    )
-    down_b = select_matrix(
-        lambda l: jnp.where(l >= 64, -1, jnp.where(l < 32, 2 * l, 2 * (l - 32) + 1))
-    )
-    up_a = select_matrix(
-        lambda l: jnp.where(l < 64, -1, jnp.where(l >= 96, 64 + 2 * (l - 96), 64 + 2 * (l - 64) + 1))
-    )
-    up_b = select_matrix(
-        lambda l: jnp.where(l >= 64, -1, jnp.where(l >= 32, 64 + 2 * (l - 32), 64 + 2 * l + 1))
-    )
+    def kept(row, l):
+        return row == jnp.where(l < 64, 2 * l, 2 * (l - 64) + 1)
+
+    def sent(row, l):
+        half, q = l // 128, (l % 128) // 32
+        z = 2 * (l % 32) + 64 * half + jnp.where(q % 2 == 0, half, 1 - half)
+        return row == jnp.where(q >= 2, z, z + 128)
+
+    keep = select_matrix((128, 128), kept)
+    pass_on = select_matrix((256, 256), sent)
     z_copies = []
     for f in range(2):
         loads[f].wait()
         cells = staged[f].reshape(128, 128)
-        z_send[f, 0] = (dot(cells[:64], down_a) + dot(cells[64:], down_b)).reshape(4, 16, 128)
-        z_send[f, 1] = (dot(cells[:64], up_a) + dot(cells[64:], up_b)).reshape(4, 16, 128)
+        halos = dot(side_by_side(cells[:64], cells[64:]), pass_on)
+        z_send[f, 0] = halos[:, :128].reshape(4, 16, 128)
+        z_send[f, 1] = halos[:, 128:].reshape(4, 16, 128)
         if f == 0:
             pl.semaphore_wait(barrier, len(partners))
         z_copies.append(
@@ -392,26 +386,27 @@
         inv[low:high, 1] = 1.0 / ((x_sum[1] + y_sum[1]) + (z1 + roll(z0, -1, 2)))
 
     place_y(1, y_copies[1])
-    for low, high in chunks(1, 15, 4):
+    for i in range(1, 15):
         for t in range(2):
-            d = inv[low:high, t] * source[low:high, t] * (1.0 / CENTER)
-            dd[low:high, t] = d
-            xa[low:high, t] = d
-
-    def step_0(old, new, low, high, step, target=None):
+            xa[i, t] = inv[i, t] * source[i, t] * (1.0 / CENTER)
+
+    def step_0(old, new, low, high, step, before, after=None, target=None):
         keep_old, keep_new = STEPS[step]
-        for lo, hi in chunks(low, high, 2):
-            applied = operator_0(old, faces0, lo, hi)
+
+        def emit(i, applied, here):
             for t in range(2):
-                r = source[lo:hi, t] - applied[t]
-                d = keep_old * dd[lo:hi, t] + keep_new * (inv[lo:hi, t] * r)
+                r = source[i, t] - applied[t]
+                d = keep_old * before[i, t] + keep_new * (inv[i, t] * r)
+                if after is not None:
+                    after[i, t] = d
                 if target is None:
-                    dd[lo:hi, t] = d
-                    new[lo:hi, t] = old[lo:hi, t] + d
+                    new[i, t] = here[t] + d
                 else:
-                    target(lo, hi, t, old[lo:hi, t] + d)
-
-    step_0(xa, xb, 2, 14, 0)
+                    target(i, t, here[t] + d)
+
+        sweep_0(old, faces0, low, high, emit)
+
+    step_0(xa, xb, 2, 14, 0, xa, dd)
 
     for copy in f1x_copies:
         copy.wait_recv()
@@ -425,14 +420,17 @@
         )
         for slot, step in enumerate((-1, 1))
     ]
-    step_0(xb, xa, 3, 13, 1)
+    step_0(xb, xa, 3, 13, 1, dd)
     best[4:12, :, 0:16, :] = xa[4:12, :, 0:16, :]
-    for i in range(4):
-        applied = operator_0(xa, faces0, 4 + 2 * i, 6 + 2 * i)
-        r = (source[4 + 2 * i : 6 + 2 * i, 0, 0:16, :] - applied[0][:, :16]) + (
-            source[4 + 2 * i : 6 + 2 * i, 1, 0:16, :] - applied[1][:, :16]
-        )
-        tmp0[0, i] = r[0] + r[1]
+    sums = []
+
+    def residual_0(i, applied, here):
+        r = [source[i, t, 0:16, :] - applied[t][:16] for t in range(2)]
+        sums.append(r[0] + r[1])
+        if i % 2 == 1:
+            tmp0[0, (i - 4) // 2] = sums[-2] + sums[-1]
+
+    sweep_0(xa, faces0, 4, 12, residual_0)
     b1[8:12, 8:16, :] = 0.125 * (tmp0[0, :, first, :] + tmp0[0, :, second, :])
     b1x_copies = [
         send(
@@ -445,20 +443,16 @@
         for slot, step in enumerate((-1, 1, -2, 2))
     ]
 
-    row = lax.broadcasted_iota(jnp.int32, (128, 128), 0)
-    column = lax.broadcasted_iota(jnp.int32, (128, 128), 1)
-    pack = [
-        jnp.where((row // 2 + 16) % 64 + 64 * p == column, 1.0, 0.0).astype(F32) for p in range(2)
-    ]
-    pack_even = [
-        jnp.where((row % 2 == 0) & ((row // 2 + 16) % 64 + 64 * p == column), 1.0, 0.0).astype(F32)
-        for p in range(2)
-    ]
+    def in_pack(row, column):
+        return ((row % 128) // 2 + 16) % 64 + 64 * (row // 128) == column
+
+    pack = select_matrix((256, 128), in_pack)
+    pack_even = select_matrix((256, 128), lambda row, l: (row % 2 == 0) & in_pack(row, l))
     first4, second4 = pl.ds(0, 4, stride=2), pl.ds(1, 4, stride=2)
 
-    def packed(pieces, matrices):
+    def packed(pieces, matrix):
         whole = [jnp.concatenate(piece, axis=0) for piece in pieces]
-        result = dot(whole[0], matrices[0]) + dot(whole[1], matrices[1])
+        result = dot(side_by_side(*whole), matrix)
         return result.reshape(len(pieces[0]), 8, 128)
 
     g2f[1, 15] = jnp.ones((3, 4, 128), F32)
@@ -500,25 +494,32 @@
     for copy in b1y_copies:
         copy.wait_recv()
 
-    for low, high in chunks(1, 19, 6):
-        d = inv1[low:high] * b1[low:high] * (1.0 / CENTER)
-        d1[low:high] = d
-        x1a[low:high] = d
-
-    def step_1(old, new, low, high, step):
+    for i in range(1, 19):
+        x1a[i] = inv1[i] * b1[i] * (1.0 / CENTER)
+
+    def step_1(old, new, low, high, step, before, after=None):
         keep_old, keep_new = STEPS[step]
-        for lo, hi in chunks(low, high, 4):
-            r = b1[lo:hi] - operator_1(old, f1, lo, hi)
-            d = keep_old * d1[lo:hi] + keep_new * (inv1[lo:hi] * r)
-            d1[lo:hi] = d
-            new[lo:hi] = old[lo:hi] + d
-
-    step_1(x1a, x1b, 2, 18, 0)
+
+        def emit(i, applied, here):
+            r = b1[i] - applied
+            d = keep_old * before[i] + keep_new * (inv1[i] * r)
+            if after is not None:
+                after[i] = d
+            new[i] = here + d
+
+        sweep_1(old, f1, low, high, emit)
+
+    step_1(x1a, x1b, 2, 18, 0, x1a, d1)
     for copy in gfx_copies:
         copy.wait_recv()
     gfy_far, gfy_copies = gather_y_shared(g2f, gfy_sems)
-    step_1(x1b, x1a, 3, 17, 1)
-    r = (b1[4:16] - operator_1(x1a, f1, 4, 16))[:, 8:16]
+    step_1(x1b, x1a, 3, 17, 1, d1)
+    r = {}
+
+    def residual_1(i, applied, here):
+        r[i - 4] = (b1[i] - applied)[8:16]
+
+    sweep_1(x1a, f1, 4, 16, residual_1)
     tmp1[0, 0:3] = packed(
         [[r[4 * i + 2 * p] + r[4 * i + 2 * p + 1] for i in range(3)] for p in range(2)], pack
     )
@@ -535,9 +536,8 @@
     for f in range(3):
         for s in range(count_y):
             f2[f, :, 4 * s : 4 * s + 4, :] = g2f[s, :, f]
-    faces2 = (f2.at[0], f2.at[1], f2.at[2])
-    for low, high in chunks(0, 16, 4):
-        terms = rows(faces2[0], low, high + 1)
+    for low, high in chunks(0, 15, 3):
+        terms = f2[0, low : high + 1]
         turned = roll(terms, 64, 2)
         half = lane_of(terms[1:].shape) < 64
         x_sum = terms[:-1] + jnp.where(half, turned[:-1], turned[1:])
@@ -555,9 +555,8 @@
     f3[0] = 0.125 * (tmp2[0, :, first16, :] + tmp2[0, :, second16, :])
     f3[1] = 0.125 * tmp2[1, :, first16, :]
     f3[2] = 0.125 * (tmp2[2, :, first16, :] + tmp2[2, :, second16, :])
-    faces3 = (f3.at[0], f3.at[1], f3.at[2])
-    for low, high in chunks(0, 16, 8):
-        terms = rows(faces3[0], low, high + 1)
+    for low, high in chunks(2, 13, 6):
+        terms = f3[0, low : high + 1]
         y_term, z_term = f3[1, low:high], f3[2, low:high]
         inv3[low:high] = 1.0 / (
             (terms[:-1] + terms[1:] + (y_term + roll(y_term, -1, 1)))
@@ -572,73 +571,89 @@
     for s in range(count_y):
         b2[:, 4 * s : 4 * s + 4, :] = g2b[s]
 
-    for low, high in chunks(0, 16, 4):
-        d = inv2[low:high] * b2[low:high] * (1.0 / CENTER)
-        d2[low:high] = d
-        x2a[low:high] = d
-
-    def step_2(old, new, low, high, step):
+    for i in range(15):
+        x2a[i] = inv2[i] * b2[i] * (1.0 / CENTER)
+
+    def step_2(old, new, low, high, step, before, after=None):
         keep_old, keep_new = STEPS[step]
-        for lo, hi in chunks(low, high, 2):
-            r = rows(b2, lo, hi) - operator_2(old, faces2, lo, hi)
-            d = keep_old * rows(d2, lo, hi) + keep_new * (rows(inv2, lo, hi) * r)
-            put_rows(d2, lo, hi, d)
-            put_rows(new, lo, hi, rows(old, lo, hi) + d)
-
-    step_2(x2a, x2b, 0, 16, 0)
-    step_2(x2b, x2a, 0, 16, 1)
-    for low, high in chunks(0, 16, 2):
-        r = b2[low:high] - operator_2(x2a, faces2, low, high)
-        r = r + roll(r, 64, 2)
-        tmp2[0, low:high] = r + roll(r, -1, 2)
-    b3[...] = 0.125 * (tmp2[0, :, first16, :] + tmp2[0, :, second16, :])
-
-    d = inv3[...] * b3[...] * (1.0 / CENTER)
-    d3[...] = d
-    x3a[...] = d
-
-    def step_3(old, new, low, high, step):
+
+        def emit(i, applied, here):
+            r = b2[i] - applied
+            d = keep_old * before[i] + keep_new * (inv2[i] * r)
+            if after is not None:
+                after[i] = d
+            new[i] = here + d
+
+        sweep_2(old, f2, low, high, emit)
+
+    step_2(x2a, x2b, 1, 14, 0, x2a, d2)
+    step_2(x2b, x2a, 1, 14, 1, d2)
+
+    def residual_2(i, applied, here):
+        r = b2[i] - applied
+        r = r + roll(r, 64, 1)
+        tmp2[0, i] = r + roll(r, -1, 1)
+
+    sweep_2(x2a, f2, 2, 13, residual_2)
+    b3[2:13] = 0.125 * (tmp2[0, 2:13, first16, :] + tmp2[0, 2:13, second16, :])
+
+    for i in range(2, 13):
+        x3a[i] = inv3[i] * b3[i] * (1.0 / CENTER)
+
+    def step_3(old, new, low, high, step, before, after=None):
         keep_old, keep_new = STEPS[step]
-        for lo, hi in chunks(low, high, 4):
-            r = rows(b3, lo, hi) - operator_3(old, faces3, lo, hi)
-            d = keep_old * rows(d3, lo, hi) + keep_new * (rows(inv3, lo, hi) * r)
-            put_rows(d3, lo, hi, d)
-            put_rows(new, lo, hi, rows(old, lo, hi) + d)
-
-    step_3(x3a, x3b, 0, 16, 0)
-    step_3(x3b, x3a, 0, 16, 1)
-
-    e = x3a[...]
+
+        def emit(i, applied, here):
+            r = b3[i] - applied
+            d = keep_old * before[i] + keep_new * (inv3[i] * r)
+            if after is not None:
+                after[i] = d
+            new[i] = here + d
+
+        sweep_3(old, f3, low, high, emit)
+
+    step_3(x3a, x3b, 3, 12, 0, x3a, d3)
+    step_3(x3b, x3a, 4, 11, 1, d3)
+
+    e = x3a[4:11]
     e = jnp.where(lane_of(e.shape) % 2 == 0, e, roll(e, 1, 2))
-    dup2[:, first16, :] = e
-    dup2[:, second16, :] = e
-    for low, high in chunks(2, 13, 4):
-        put_rows(x2b, low, high, rows(x2a, low, high) + rows(dup2, low, high))
-    for low, high in chunks(3, 12, 2):
-        r = rows(b2, low, high) - operator_2(x2b, faces2, low, high)
-        d = rows(inv2, low, high) * r * (1.0 / CENTER)
-        put_rows(d2, low, high, d)
-        put_rows(x2a, low, high, rows(x2b, low, high) + d)
-    step_2(x2a, x2b, 4, 11, 0)
-    step_2(x2b, x2a, 5, 10, 1)
-
-    spread = [
-        jnp.where((column // 2 + 16) % 64 + 64 * p == row, 1.0, 0.0).astype(F32) for p in range(2)
-    ]
-    e = x2a[5:10, 0:16, :].reshape(80, 128)
+    dup2[4:11, first16, :] = e
+    dup2[4:11, second16, :] = e
+    for i in range(4, 11):
+        x2b[i] = x2a[i] + dup2[i]
+    x2b[3] = x2a[3]
+    x2b[11] = x2a[11]
+
+    def first_up_2(i, applied, here):
+        d = inv2[i] * (b2[i] - applied) * (1.0 / CENTER)
+        d2[i] = d
+        x2a[i] = here + d
+
+    sweep_2(x2b, f2, 4, 11, first_up_2)
+    step_2(x2a, x2b, 5, 10, 0, d2, d2)
+    x2b[4] = x2a[4]
+    x2b[10] = x2a[10]
+    step_2(x2b, x2a, 5, 10, 1, d2)
+
+    def in_spread(row, column):
+        return ((column % 128) // 2 + 16) % 64 + 64 * (column // 128) == row
+
+    e = dot(x2a[5:10, 0:16, :].reshape(80, 128), select_matrix((128, 256), in_spread))
     for p in range(2):
-        value = dot(e, spread[p]).reshape(5, 16, 128)
+        value = e[:, 128 * p : 128 * p + 128].reshape(5, 16, 128)
         dup21[p, :, first16, :] = value
         dup21[p, :, second16, :] = value
     for i in range(3, 17):
         x1b[i] = x1a[i] + dup21[(i // 2) % 2, i // 4, 0:24, :]
-    for low, high in chunks(4, 16, 4):
-        r = b1[low:high] - operator_1(x1b, f1, low, high)
-        d = inv1[low:high] * r * (1.0 / CENTER)
-        d1[low:high] = d
-        x1a[low:high] = x1b[low:high] + d
-    step_1(x1a, x1b, 5, 15, 0)
-    step_1(x1b, x1a, 6, 14, 1)
+
+    def first_up_1(i, applied, here):
+        d = inv1[i] * (b1[i] - applied) * (1.0 / CENTER)
+        d1[i] = d
+        x1a[i] = here + d
+
+    sweep_1(x1b, f1, 4, 16, first_up_1)
+    step_1(x1a, x1b, 5, 15, 0, d1, d1)
+    step_1(x1b, x1a, 6, 14, 1, d1)
 
     drain()
     place_y(2, y_copies[2])
@@ -653,23 +668,26 @@
         for t in range(2):
             xb[i, t, 0:16, :] = best[i, t, 0:16, :] + brick
             xb[i, t, 16:24, :] = best[i, t, 16:24, :] + edge
-    for lo, hi in chunks(2, 14, 2):
-        applied = operator_0(xb, faces0, lo, hi)
+
+    def first_up_0(i, applied, here):
         for t in range(2):
-            r = source[lo:hi, t] - applied[t]
-            d = inv[lo:hi, t] * r * (1.0 / CENTER)
-            dd[lo:hi, t] = d
-            xa[lo:hi, t] = xb[lo:hi, t] + d
-    step_0(xa, xb, 3, 13, 0)
-
-    def to_own(lo, hi, t, value):
-        own[t, lo - 4 : hi - 4] = value[:, 0:16, :]
-
-    step_0(xb, None, 4, 12, 1, to_own)
-    join = [
-        jnp.where((column == 2 * row + t) & (row < 64), 1.0, 0.0).astype(F32) for t in range(2)
-    ]
-    result = dot(own[0].reshape(128, 128), join[0]) + dot(own[1].reshape(128, 128), join[1])
+            d = inv[i, t] * (source[i, t] - applied[t]) * (1.0 / CENTER)
+            dd[i, t] = d
+            xa[i, t] = here[t] + d
+
+    sweep_0(xb, faces0, 2, 14, first_up_0)
+    step_0(xa, xb, 3, 13, 0, dd, dd)
+
+    def to_own(i, t, value):
+        own[t, i - 4] = value[0:16]
+
+    step_0(xb, None, 4, 12, 1, dd, None, to_own)
+
+    def joined(row, column):
+        return (row % 128 < 64) & (column == 2 * (row % 128) + row // 128)
+
+    cells = side_by_side(own[0].reshape(128, 128), own[1].reshape(128, 128))
+    result = dot(cells, select_matrix((256, 128), joined))
     out_ref[...] = result.reshape(8, 16, 128)
 
 

time: 62.2 us -> 59.3 us (0.953); the launches traced: 62 us -> 58.5 us
  Pallas kernels: 60.5 us -> 57 us
    pallas_call x1, Pallas kernels: 60.5 us -> 57 us  [shards(): pl.pallas_call(functools.partial(kernel, sizes), out_shape=jax.ShapeDtype...]
where the time goes in v4:
time: 59.3 us; the launch traced here: 58.5 us
  Pallas kernels  57 us (96%)
  local copies, waits for them, and re-layouts  1.47 us (2%)
    pallas_call x1, Pallas kernels, shards(): pl.pallas_call(functools.partial(kernel, sizes), out_shape=jax.ShapeDtype...  57 us
    unnamed x1, local copies, waits for them, and re-layouts  1.47 us

profile of v4, /device:TPU:1, one launch (start us, length us, event | category | flops | bytes accessed | tf_op | source)
XLA Modules:
  0.0 58.5 jit_solution(8731227710379753265)
XLA Ops:
  0.0 57.0 %shard_map.28 = f32[8,16,128]{2,1,0:T(8,128)} custom-call(f32[8,16,128]{2,1,0:T(8,128)} %source_hbm.1, f32[8,16,128]{2,1,0:T(8,128)} %cond_hbm.1), custom_call_target="tpu_custom_call" | custom-call | tf_op jit(solution)/shard_map/pallas_call | solution.py:759
  57.0 1.5 %copy.4 = f32[8,16,128]{2,1,0:T(8,128)} copy(f32[8,16,128]{2,1,0:T(8,128)} %shard_map.28) | data formatting | bytes 131072

commit v5 on v4

--- a/solution.py
+++ b/solution.py
@@ -166,6 +166,7 @@
     z_sems,
     x_sems,
     y_sems,
+    xy_sems,
     f1x_sems,
     f1y_sems,
     b1x_sems,
@@ -198,6 +199,7 @@
     partners = [at_z(1), at_z(-1)]
     partners += [at_x(sign * step) for step in (1, 2, 3, 5, 6) for sign in (1, -1)]
     partners += [at_y(step) for step in range(1, count_y)]
+    partners += [at_x(dx) | at_y(dy) for dx in (-1, 1) for dy in (-1, 1)]
     for partner in partners:
         pl.semaphore_signal(barrier, inc=1, device_id=partner, device_id_type=MESH)
 
@@ -274,13 +276,30 @@
             for way in range(2)
         ]
 
+    def send_xy(f):
+        copies = send_x(f)
+        y_send[f, 0, 4:12] = win[f, 4:12, :, 0:4, :]
+        y_send[f, 1, 4:12] = win[f, 4:12, :, 12:16, :]
+        for way in range(2):
+            for slot, (dx, first, last) in enumerate(((0, 4, 12), (1, 8, 12), (-1, 4, 8))):
+                copies.append(
+                    send(
+                        y_send.at[f, way, first:last],
+                        y_recv.at[f, way, first - 8 * dx : last - 8 * dx],
+                        xy_sems,
+                        6 * f + 3 * way + slot,
+                        at_y((-1, 1)[way]) | (at_x(dx) if dx else {}),
+                    )
+                )
+        return copies
+
     def place_y(f, copies):
         for copy in copies:
             copy.wait_recv()
         win[f, :, :, 16:20, :] = y_recv[f, 0]
         win[f, :, :, 20:24, :] = y_recv[f, 1]
 
-    x_copies = []
+    xy_copies = []
     for f in range(2):
         for copy in z_copies[f]:
             copy.wait_recv()
@@ -299,26 +318,31 @@
                 win[f, 4 + 4 * part : 8 + 4 * part, t, 0:16, :] = jnp.where(
                     lane < 64, roll(mine, 64, 2) if t else mine, halo
                 )
-        x_copies.append(send_x(f))
-    y_copies = []
-    for f in range(2):
-        for copy in x_copies[f]:
-            copy.wait_recv()
-        y_copies.append(send_y(f))
-    place_y(0, y_copies[0])
+        xy_copies.append(send_xy(f))
 
     cond, source, best = win.at[0], win.at[1], win.at[2]
     faces0 = (fx, fy, fz)
-    for low, high in chunks(1, 16, 4):
+    brick = slice(0, 16)
+    for i in range(4, 12):
+        k0, k1 = cond[i, 0, brick, :], cond[i, 1, brick, :]
+        fz[i, 0, brick, :] = harmonic(k0, roll(k1, 1, 1))
+        fz[i, 1, brick, :] = harmonic(k1, k0)
+        if i > 4:
+            fx[i, 0, brick, :] = harmonic(k0, cond[i - 1, 0, brick, :])
+            fx[i, 1, brick, :] = harmonic(k1, cond[i - 1, 1, brick, :])
+    place_y(0, xy_copies[0])
+    for i in range(1, 16):
+        rest = slice(16, 24) if 4 < i < 12 else slice(0, 24)
         for t in range(2):
-            k = cond[low - 1 : high, t]
-            fx[low:high, t] = harmonic(k[1:], k[:-1])
-    for low, high in chunks(1, 15, 4):
-        k0, k1 = cond[low:high, 0], cond[low:high, 1]
-        fy[low:high, 0] = harmonic(k0, roll(k0, 1, 1))
-        fy[low:high, 1] = harmonic(k1, roll(k1, 1, 1))
-        fz[low:high, 0] = harmonic(k0, roll(k1, 1, 2))
-        fz[low:high, 1] = harmonic(k1, k0)
+            fx[i, t, rest, :] = harmonic(cond[i, t, rest, :], cond[i - 1, t, rest, :])
+    for i in range(1, 15):
+        k0, k1 = cond[i, 0], cond[i, 1]
+        fy[i, 0] = harmonic(k0, roll(k0, 1, 0))
+        fy[i, 1] = harmonic(k1, roll(k1, 1, 0))
+        rest = slice(16, 24) if 4 <= i < 12 else slice(0, 24)
+        k0, k1 = k0[rest], k1[rest]
+        fz[i, 0, rest, :] = harmonic(k0, roll(k1, 1, 1))
+        fz[i, 1, rest, :] = harmonic(k1, k0)
 
     for i in range(4):
         tmp0[0, i] = fx[4 + 2 * i, 0, 0:16, :] + fx[4 + 2 * i, 1, 0:16, :]
@@ -385,7 +409,7 @@
         inv[low:high, 0] = 1.0 / ((x_sum[0] + y_sum[0]) + (z0 + z1))
         inv[low:high, 1] = 1.0 / ((x_sum[1] + y_sum[1]) + (z1 + roll(z0, -1, 2)))
 
-    place_y(1, y_copies[1])
+    place_y(1, xy_copies[1])
     for i in range(1, 15):
         for t in range(2):
             xa[i, t] = inv[i, t] * source[i, t] * (1.0 / CENTER)
@@ -434,13 +458,15 @@
     b1[8:12, 8:16, :] = 0.125 * (tmp0[0, :, first, :] + tmp0[0, :, second, :])
     b1x_copies = [
         send(
-            b1.at[8:12, 8:16, :],
-            b1.at[8 - 4 * step : 12 - 4 * step, 8:16, :],
+            b1.at[first:last, 8:16, :],
+            b1.at[first - 4 * step : last - 4 * step, 8:16, :],
             b1x_sems,
             slot,
             at_x(step),
         )
-        for slot, step in enumerate((-1, 1, -2, 2))
+        for slot, (step, first, last) in enumerate(
+            ((-1, 8, 12), (1, 8, 12), (-2, 8, 11), (2, 9, 12))
+        )
     ]
 
     def in_pack(row, column):
@@ -525,7 +551,7 @@
     )
     g2b[1, 6:9] = 0.125 * (tmp1[0, 0:3, first4, :] + tmp1[0, 0:3, second4, :])
     gbx_copies = spread_x(g2b, 6, 9, gbx_sems, (3, -3, 6, -6))
-    x_copies.append(send_x(2))
+    x0_copies = send_x(2)
     for copy in gbx_copies:
         copy.wait_recv()
     gby_copies = gather_y(g2b, gby_sems)
@@ -563,9 +589,9 @@
             + (z_term + roll(z_term, -2, 2))
         )
 
-    for copy in x_copies[2]:
+    for copy in x0_copies:
         copy.wait_recv()
-    y_copies.append(send_y(2))
+    y0_copies = send_y(2)
     for copy in gby_copies:
         copy.wait_recv()
     for s in range(count_y):
@@ -656,7 +682,7 @@
     step_1(x1b, x1a, 6, 14, 1, d1)
 
     drain()
-    place_y(2, y_copies[2])
+    place_y(2, y0_copies)
     e = x1a[6:14]
     dup1[:, pl.ds(0, 24, stride=2), :] = e
     dup1[:, pl.ds(1, 24, stride=2), :] = e
@@ -745,6 +771,7 @@
         sems(4),
         sems(6),
         sems(6),
+        sems(12),
         sems(4),
         sems(2),
         sems(4),
@@ -763,7 +790,7 @@
             out_specs=pl.BlockSpec(memory_space=pltpu.VMEM),
             scratch_shapes=scratch,
             compiler_params=pltpu.CompilerParams(
-                collective_id=0, has_side_effects=True, vmem_limit_bytes=62 * 1024 * 1024
+                collective_id=0, has_side_effects=True, vmem_limit_bytes=55136 * 1024
             ),
         )(pressure_source, conductivity)
 

time: 59.3 us -> 56.9 us (0.960); the launches traced: 58.5 us -> 56.7 us
  Pallas kernels: 57 us -> 56.1 us
  local copies, waits for them, and re-layouts: 1.47 us -> 0.63 us
    pallas_call x1, Pallas kernels: 57 us -> 56.1 us  [shards(): pl.pallas_call(functools.partial(kernel, sizes), out_shape=jax.ShapeDtype...]
    unnamed x1, local copies, waits for them, and re-layouts: 1.47 us -> 0.63 us
where the time goes in v5:
time: 56.9 us; the launch traced here: 56.7 us
  Pallas kernels  56.1 us (99%)
  local copies, waits for them, and re-layouts  0.63 us (1%)
    pallas_call x1, Pallas kernels, shards(): pl.pallas_call(functools.partial(kernel, sizes), out_shape=jax.ShapeDtype...  56.1 us

profile of v5, /device:TPU:1, one launch (start us, length us, event | category | flops | bytes accessed | tf_op | source)
XLA Modules:
  0.0 56.7 jit_solution(12464673042543350225)
XLA Ops:
  0.0 56.1 %shard_map.28 = f32[8,16,128]{2,1,0:T(8,128)S(1)} custom-call(f32[8,16,128]{2,1,0:T(8,128)} %source_hbm.1, f32[8,16,128]{2,1,0:T(8,128)} %cond_hbm.1), custom_call_target="tpu_custom_call" | custom-call | tf_op jit(solution)/shard_map/pallas_call | solution.py:786
  56.1 0.6 %copy.4 = f32[8,16,128]{2,1,0:T(8,128)} copy(f32[8,16,128]{2,1,0:T(8,128)S(1)} %shard_map.28) | data formatting | bytes 131072

commit v6 on v5

--- a/solution.py
+++ b/solution.py
@@ -331,18 +331,12 @@
             fx[i, 0, brick, :] = harmonic(k0, cond[i - 1, 0, brick, :])
             fx[i, 1, brick, :] = harmonic(k1, cond[i - 1, 1, brick, :])
     place_y(0, xy_copies[0])
-    for i in range(1, 16):
-        rest = slice(16, 24) if 4 < i < 12 else slice(0, 24)
+    for t in range(2):
+        fx[4, t, brick, :] = harmonic(cond[4, t, brick, :], cond[3, t, brick, :])
+    for i in range(4, 12):
         for t in range(2):
-            fx[i, t, rest, :] = harmonic(cond[i, t, rest, :], cond[i - 1, t, rest, :])
-    for i in range(1, 15):
-        k0, k1 = cond[i, 0], cond[i, 1]
-        fy[i, 0] = harmonic(k0, roll(k0, 1, 0))
-        fy[i, 1] = harmonic(k1, roll(k1, 1, 0))
-        rest = slice(16, 24) if 4 <= i < 12 else slice(0, 24)
-        k0, k1 = k0[rest], k1[rest]
-        fz[i, 0, rest, :] = harmonic(k0, roll(k1, 1, 1))
-        fz[i, 1, rest, :] = harmonic(k1, k0)
+            k = cond[i, t]
+            fy[i, t] = harmonic(k, roll(k, 1, 0))
 
     for i in range(4):
         tmp0[0, i] = fx[4 + 2 * i, 0, 0:16, :] + fx[4 + 2 * i, 1, 0:16, :]
@@ -377,6 +371,20 @@
             for step in range(1, count_y)
         ]
 
+    for i in range(1, 16):
+        part = slice(16, 24) if 4 <= i < 12 else slice(0, 24)
+        for t in range(2):
+            fx[i, t, part, :] = harmonic(cond[i, t, part, :], cond[i - 1, t, part, :])
+        if i == 15:
+            break
+        k0, k1 = cond[i, 0], cond[i, 1]
+        if not 4 <= i < 12:
+            fy[i, 0] = harmonic(k0, roll(k0, 1, 0))
+            fy[i, 1] = harmonic(k1, roll(k1, 1, 0))
+        k0, k1 = k0[part], k1[part]
+        fz[i, 0, part, :] = harmonic(k0, roll(k1, 1, 1))
+        fz[i, 1, part, :] = harmonic(k1, k0)
+
     sibling = {"gy": me_y + 1 - 2 * lax.rem(me_y, 2)}
     shift = lax.rem(me_y, 2) * 2 + (count_y - 1)
 
@@ -432,6 +440,32 @@
 
     step_0(xa, xb, 2, 14, 0, xa, dd)
 
+    step_0(xb, xa, 3, 13, 1, dd)
+    best[4:12, :, 0:16, :] = xa[4:12, :, 0:16, :]
+    sums = []
+
+    def residual_0(i, applied, here):
+        r = [source[i, t, 0:16, :] - applied[t][:16] for t in range(2)]
+        sums.append(r[0] + r[1])
+        if i % 2 == 1:
+            tmp0[0, (i - 4) // 2] = sums[-2] + sums[-1]
+
+    sweep_0(xa, faces0, 4, 12, residual_0)
+    b1[8:12, 8:16, :] = 0.125 * (tmp0[0, :, first, :] + tmp0[0, :, second, :])
+    b1x_copies = [
+        send(
+            b1.at[first:last, 8:16, :],
+            b1.at[first - 4 * step : last - 4 * step, 8:16, :],
+            b1x_sems,
+            slot,
+            at_x(step),
+        )
+        for slot, (step, first, last) in enumerate(
+            ((-1, 8, 12), (1, 8, 12), (-2, 8, 11), (2, 9, 12))
+        )
+    ]
+
+
     for copy in f1x_copies:
         copy.wait_recv()
     f1y_copies = [
@@ -443,30 +477,6 @@
             at_y(step),
         )
         for slot, step in enumerate((-1, 1))
-    ]
-    step_0(xb, xa, 3, 13, 1, dd)
-    best[4:12, :, 0:16, :] = xa[4:12, :, 0:16, :]
-    sums = []
-
-    def residual_0(i, applied, here):
-        r = [source[i, t, 0:16, :] - applied[t][:16] for t in range(2)]
-        sums.append(r[0] + r[1])
-        if i % 2 == 1:
-            tmp0[0, (i - 4) // 2] = sums[-2] + sums[-1]
-
-    sweep_0(xa, faces0, 4, 12, residual_0)
-    b1[8:12, 8:16, :] = 0.125 * (tmp0[0, :, first, :] + tmp0[0, :, second, :])
-    b1x_copies = [
-        send(
-            b1.at[first:last, 8:16, :],
-            b1.at[first - 4 * step : last - 4 * step, 8:16, :],
-            b1x_sems,
-            slot,
-            at_x(step),
-        )
-        for slot, (step, first, last) in enumerate(
-            ((-1, 8, 12), (1, 8, 12), (-2, 8, 11), (2, 9, 12))
-        )
     ]
 
     def in_pack(row, column):

time: 56.9 us -> 55.8 us (0.981)
  Pallas kernels: 56.1 us -> 55 us
    pallas_call x1, Pallas kernels: 56.1 us -> 55 us  [shards(): pl.pallas_call(functools.partial(kernel, sizes), out_shape=jax.ShapeDtype...]
where the time goes in v6:
time: 55.8 us; the launch traced here: 55.7 us
  Pallas kernels  55 us (99%)
  local copies, waits for them, and re-layouts  0.63 us (1%)
    pallas_call x1, Pallas kernels, shards(): pl.pallas_call(functools.partial(kernel, sizes), out_shape=jax.ShapeDtype...  55 us

profile of v6, /device:TPU:1, one launch (start us, length us, event | category | flops | bytes accessed | tf_op | source)
XLA Modules:
  0.0 55.7 jit_solution(13691055020588364174)
XLA Ops:
  0.0 55.0 %shard_map.28 = f32[8,16,128]{2,1,0:T(8,128)S(1)} custom-call(f32[8,16,128]{2,1,0:T(8,128)} %source_hbm.1, f32[8,16,128]{2,1,0:T(8,128)} %cond_hbm.1), custom_call_target="tpu_custom_call" | custom-call | tf_op jit(solution)/shard_map/pallas_call | solution.py:796
  55.0 0.6 %copy.4 = f32[8,16,128]{2,1,0:T(8,128)} copy(f32[8,16,128]{2,1,0:T(8,128)S(1)} %shard_map.28) | data formatting | bytes 131072

commit v7 on v6

--- a/solution.py
+++ b/solution.py
@@ -224,11 +224,11 @@
         return copy
 
     def kept(row, l):
-        return row == jnp.where(l < 64, 2 * l, 2 * (l - 64) + 1)
+        return row == jnp.where(l < 64, 2 * l, 2 * l - 127)
 
     def sent(row, l):
-        half, q = l // 128, (l % 128) // 32
-        z = 2 * (l % 32) + 64 * half + jnp.where(q % 2 == 0, half, 1 - half)
+        half, q = l >> 7, (l >> 5) & 3
+        z = 2 * (l & 31) + 64 * half + jnp.where((q & 1) == 0, half, 1 - half)
         return row == jnp.where(q >= 2, z, z + 128)
 
     keep = select_matrix((128, 128), kept)
@@ -356,7 +356,7 @@
             slot,
             at_x(step),
         )
-        for slot, step in enumerate((-1, 1, -2, 2))
+        for slot, step in enumerate((-2, 2, -1, 1))
     ]
 
     def spread_x(ref, first, last, sems, steps):
@@ -368,7 +368,7 @@
     def gather_y(ref, sems):
         return [
             send(ref.at[1], ref.at[(1 - step) % count_y], sems, step - 1, at_y(step))
-            for step in range(1, count_y)
+            for step in sorted(range(1, count_y), key=lambda step: abs(step - count_y // 2))
         ]
 
     for i in range(1, 16):
@@ -461,7 +461,7 @@
             at_x(step),
         )
         for slot, (step, first, last) in enumerate(
-            ((-1, 8, 12), (1, 8, 12), (-2, 8, 11), (2, 9, 12))
+            ((-2, 8, 11), (2, 9, 12), (-1, 8, 12), (1, 8, 12))
         )
     ]
 
@@ -480,10 +480,10 @@
     ]
 
     def in_pack(row, column):
-        return ((row % 128) // 2 + 16) % 64 + 64 * (row // 128) == column
+        return ((((row & 127) >> 1) + 16) & 63) + 64 * (row >> 7) == column
 
     pack = select_matrix((256, 128), in_pack)
-    pack_even = select_matrix((256, 128), lambda row, l: (row % 2 == 0) & in_pack(row, l))
+    pack_even = select_matrix((256, 128), lambda row, l: ((row & 1) == 0) & in_pack(row, l))
     first4, second4 = pl.ds(0, 4, stride=2), pl.ds(1, 4, stride=2)
 
     def packed(pieces, matrix):
@@ -560,7 +560,7 @@
         [[r[4 * i + 2 * p] + r[4 * i + 2 * p + 1] for i in range(3)] for p in range(2)], pack
     )
     g2b[1, 6:9] = 0.125 * (tmp1[0, 0:3, first4, :] + tmp1[0, 0:3, second4, :])
-    gbx_copies = spread_x(g2b, 6, 9, gbx_sems, (3, -3, 6, -6))
+    gbx_copies = spread_x(g2b, 6, 9, gbx_sems, (6, -6, 3, -3))
     x0_copies = send_x(2)
     for copy in gbx_copies:
         copy.wait_recv()
@@ -652,7 +652,7 @@
     step_3(x3b, x3a, 4, 11, 1, d3)
 
     e = x3a[4:11]
-    e = jnp.where(lane_of(e.shape) % 2 == 0, e, roll(e, 1, 2))
+    e = jnp.where((lane_of(e.shape) & 1) == 0, e, roll(e, 1, 2))
     dup2[4:11, first16, :] = e
     dup2[4:11, second16, :] = e
     for i in range(4, 11):
@@ -672,7 +672,7 @@
     step_2(x2b, x2a, 5, 10, 1, d2)
 
     def in_spread(row, column):
-        return ((column % 128) // 2 + 16) % 64 + 64 * (column // 128) == row
+        return ((((column & 127) >> 1) + 16) & 63) + 64 * (column >> 7) == row
 
     e = dot(x2a[5:10, 0:16, :].reshape(80, 128), select_matrix((128, 256), in_spread))
     for p in range(2):
@@ -720,7 +720,7 @@
     step_0(xb, None, 4, 12, 1, dd, None, to_own)
 
     def joined(row, column):
-        return (row % 128 < 64) & (column == 2 * (row % 128) + row // 128)
+        return ((row & 127) < 64) & (column == 2 * (row & 127) + (row >> 7))
 
     cells = side_by_side(own[0].reshape(128, 128), own[1].reshape(128, 128))
     result = dot(cells, select_matrix((256, 128), joined))

time: 55.8 us -> 54.4 us (0.975)
  Pallas kernels: 55 us -> 53.6 us
    pallas_call x1, Pallas kernels: 55 us -> 53.6 us  [shards(): pl.pallas_call(functools.partial(kernel, sizes), out_shape=jax.ShapeDtype...]
where the time goes in v7:
time: 54.4 us; the launch traced here: 54.2 us
  Pallas kernels  53.6 us (99%)
  local copies, waits for them, and re-layouts  0.63 us (1%)
    pallas_call x1, Pallas kernels, shards(): pl.pallas_call(functools.partial(kernel, sizes), out_shape=jax.ShapeDtype...  53.6 us

profile of v7, /device:TPU:1, one launch (start us, length us, event | category | flops | bytes accessed | tf_op | source)
XLA Modules:
  0.0 54.2 jit_solution(2952058324258776193)
XLA Ops:
  0.0 53.6 %shard_map.28 = f32[8,16,128]{2,1,0:T(8,128)S(1)} custom-call(f32[8,16,128]{2,1,0:T(8,128)} %source_hbm.1, f32[8,16,128]{2,1,0:T(8,128)} %cond_hbm.1), custom_call_target="tpu_custom_call" | custom-call | tf_op jit(solution)/shard_map/pallas_call | solution.py:796
  53.6 0.6 %copy.4 = f32[8,16,128]{2,1,0:T(8,128)} copy(f32[8,16,128]{2,1,0:T(8,128)S(1)} %shard_map.28) | data formatting | bytes 131072

commit v8 on v7

--- a/solution.py
+++ b/solution.py
@@ -147,6 +147,7 @@
     dup1,
     g2f,
     g2b,
+    last_y,
     f2,
     b2,
     inv2,
@@ -155,6 +156,10 @@
     d2,
     tmp2,
     f3,
+    f3_send,
+    f3_recv,
+    b3_send,
+    b3_recv,
     b3,
     inv3,
     x3a,
@@ -175,6 +180,8 @@
     gfy_sems,
     gbx_sems,
     gby_sems,
+    f3_sems,
+    b3_sems,
 ):
     count_x, count_y, count_z = sizes
     me_x, me_y, me_z = lax.axis_index("gx"), lax.axis_index("gy"), lax.axis_index("gz")
@@ -198,7 +205,7 @@
     barrier = pltpu.get_barrier_semaphore()
     partners = [at_z(1), at_z(-1)]
     partners += [at_x(sign * step) for step in (1, 2, 3, 5, 6) for sign in (1, -1)]
-    partners += [at_y(step) for step in range(1, count_y)]
+    partners += [at_y(sign * step) for step in (1, 2, 3) for sign in (1, -1)]
     partners += [at_x(dx) | at_y(dy) for dx in (-1, 1) for dy in (-1, 1)]
     for partner in partners:
         pl.semaphore_signal(barrier, inc=1, device_id=partner, device_id_type=MESH)
@@ -361,14 +368,19 @@
 
     def spread_x(ref, first, last, sems, steps):
         return [
-            send(ref.at[1, first:last], ref.at[1, first - step : last - step], sems, slot, at_x(step))
+            send(ref.at[2, first:last], ref.at[2, first - step : last - step], sems, slot, at_x(step))
             for slot, step in enumerate(steps)
         ]
 
-    def gather_y(ref, sems):
+    def spread_y(ref, sems):
         return [
-            send(ref.at[1], ref.at[(1 - step) % count_y], sems, step - 1, at_y(step))
-            for step in sorted(range(1, count_y), key=lambda step: abs(step - count_y // 2))
+            send(ref.at[2], ref.at[2 - step], sems, slot, at_y(step))
+            for slot, step in enumerate((2, -2, 1, -1))
+        ]
+
+    def pass_rows_3(out, into, sems):
+        return [
+            send(out.at[way], into.at[way], sems, way, at_y((2, -2)[way])) for way in range(2)
         ]
 
     for i in range(1, 16):
@@ -384,31 +396,6 @@
         k0, k1 = k0[part], k1[part]
         fz[i, 0, part, :] = harmonic(k0, roll(k1, 1, 1))
         fz[i, 1, part, :] = harmonic(k1, k0)
-
-    sibling = {"gy": me_y + 1 - 2 * lax.rem(me_y, 2)}
-    shift = lax.rem(me_y, 2) * 2 + (count_y - 1)
-
-    def hand_on(ref, sems, place):
-        return send(
-            ref.at[place],
-            ref.at[lax.rem(place + shift, count_y)],
-            sems,
-            count_y + place,
-            sibling,
-        )
-
-    def gather_y_shared(ref, sems):
-        places = [(1 - step) % count_y for step in range(2, count_y, 2)]
-        far = {
-            place: send(ref.at[1], ref.at[place], sems, place, at_y(1 - place + count_y))
-            for place in places
-        }
-        return far, [hand_on(ref, sems, 1)]
-
-    def hand_on_all(ref, sems, far, handed):
-        for place, copy in far.items():
-            copy.wait_recv()
-            handed.append(hand_on(ref, sems, place))
 
     for low, high in chunks(1, 15, 2):
         x_sum = [fx[low:high, t] + fx[low + 1 : high + 1, t] for t in range(2)]
@@ -491,8 +478,8 @@
         result = dot(side_by_side(*whole), matrix)
         return result.reshape(len(pieces[0]), 8, 128)
 
-    g2f[1, 15] = jnp.ones((3, 4, 128), F32)
-    g2b[1, 15] = jnp.zeros((4, 128), F32)
+    g2f[2, 15] = jnp.ones((3, 4, 128), F32)
+    g2b[2, 15] = jnp.zeros((4, 128), F32)
     mine = slice(8, 16)
     tmp1[0] = packed([[f1[4 * i + 2 * p, 0, mine, :] for i in range(5)] for p in range(2)], pack)
     for f in (1, 2):
@@ -501,9 +488,9 @@
             for p in range(2)
         ]
         tmp1[f] = packed(pieces, (None, pack, pack_even)[f])
-    g2f[1, 5:10, 0] = 0.125 * (tmp1[0, :, first4, :] + tmp1[0, :, second4, :])
-    g2f[1, 5:10, 1] = 0.125 * tmp1[1, :, first4, :]
-    g2f[1, 5:10, 2] = 0.125 * (tmp1[2, :, first4, :] + tmp1[2, :, second4, :])
+    g2f[2, 5:10, 0] = 0.125 * (tmp1[0, :, first4, :] + tmp1[0, :, second4, :])
+    g2f[2, 5:10, 1] = 0.125 * tmp1[1, :, first4, :]
+    g2f[2, 5:10, 2] = 0.125 * (tmp1[2, :, first4, :] + tmp1[2, :, second4, :])
     gfx_copies = spread_x(g2f, 5, 10, gfx_sems, (5, -5))
 
     drain()
@@ -548,7 +535,8 @@
     step_1(x1a, x1b, 2, 18, 0, x1a, d1)
     for copy in gfx_copies:
         copy.wait_recv()
-    gfy_far, gfy_copies = gather_y_shared(g2f, gfy_sems)
+    gfy_copies = spread_y(g2f, gfy_sems)
+    gfy_copies.append(send(g2f.at[2, :, 1], last_y, gfy_sems, 4, at_y(-3)))
     step_1(x1b, x1a, 3, 17, 1, d1)
     r = {}
 
@@ -559,19 +547,19 @@
     tmp1[0, 0:3] = packed(
         [[r[4 * i + 2 * p] + r[4 * i + 2 * p + 1] for i in range(3)] for p in range(2)], pack
     )
-    g2b[1, 6:9] = 0.125 * (tmp1[0, 0:3, first4, :] + tmp1[0, 0:3, second4, :])
+    g2b[2, 6:9] = 0.125 * (tmp1[0, 0:3, first4, :] + tmp1[0, 0:3, second4, :])
     gbx_copies = spread_x(g2b, 6, 9, gbx_sems, (6, -6, 3, -3))
     x0_copies = send_x(2)
     for copy in gbx_copies:
         copy.wait_recv()
-    gby_copies = gather_y(g2b, gby_sems)
-
-    hand_on_all(g2f, gfy_sems, gfy_far, gfy_copies)
+    gby_copies = spread_y(g2b, gby_sems)
+
     for copy in gfy_copies:
         copy.wait_recv()
     for f in range(3):
-        for s in range(count_y):
+        for s in range(5):
             f2[f, :, 4 * s : 4 * s + 4, :] = g2f[s, :, f]
+        f2[f, :, 20:24, :] = last_y[...] if f == 1 else jnp.ones((16, 4, 128), F32)
     for low, high in chunks(0, 15, 3):
         terms = f2[0, low : high + 1]
         turned = roll(terms, 64, 2)
@@ -587,10 +575,59 @@
         y_both = y_term + roll(y_term, 64, 2)
         tmp2[1, low:high] = y_both + roll(y_both, -1, 2)
         tmp2[2, low:high] = z_term + roll(z_term, 64, 2)
-    first16, second16 = pl.ds(0, 16, stride=2), pl.ds(1, 16, stride=2)
-    f3[0] = 0.125 * (tmp2[0, :, first16, :] + tmp2[0, :, second16, :])
-    f3[1] = 0.125 * tmp2[1, :, first16, :]
-    f3[2] = 0.125 * (tmp2[2, :, first16, :] + tmp2[2, :, second16, :])
+    first_8, second_8 = pl.ds(4, 8, stride=2), pl.ds(5, 8, stride=2)
+    f3[:, :, 8:16, :] = jnp.ones((3, 16, 8, 128), F32)
+    f3[0, :, 0:8, :] = 0.125 * (tmp2[0, :, first_8, :] + tmp2[0, :, second_8, :])
+    f3[1, :, 0:8, :] = 0.125 * tmp2[1, :, first_8, :]
+    f3[2, :, 0:8, :] = 0.125 * (tmp2[2, :, first_8, :] + tmp2[2, :, second_8, :])
+    f3_send[0] = f3[:, 2:14, 0:4, :]
+    f3_send[1] = f3[:, 2:14, 2:6, :]
+    f3_copies = pass_rows_3(f3_send, f3_recv, f3_sems)
+
+    for copy in gby_copies:
+        copy.wait_recv()
+    for s in range(5):
+        b2[:, 4 * s : 4 * s + 4, :] = g2b[s]
+    b2[:, 20:24, :] = jnp.zeros((16, 4, 128), F32)
+
+    for i in range(15):
+        x2a[i] = inv2[i] * b2[i] * (1.0 / CENTER)
+
+    def step_2(old, new, low, high, step, before, after=None):
+        keep_old, keep_new = STEPS[step]
+
+        def emit(i, applied, here):
+            r = b2[i] - applied
+            d = keep_old * before[i] + keep_new * (inv2[i] * r)
+            if after is not None:
+                after[i] = d
+            new[i] = here + d
+
+        sweep_2(old, f2, low, high, emit)
+
+    step_2(x2a, x2b, 1, 14, 0, x2a, d2)
+    step_2(x2b, x2a, 1, 14, 1, d2)
+
+    def residual_2(i, applied, here):
+        r = b2[i] - applied
+        r = r + roll(r, 64, 1)
+        tmp2[0, i] = r + roll(r, -1, 1)
+
+    sweep_2(x2a, f2, 2, 13, residual_2)
+    restricted = 0.125 * (tmp2[0, 2:13, first_8, :] + tmp2[0, 2:13, second_8, :])
+    b3[2:13, 0:8, :] = restricted
+    b3[2:13, 8:16, :] = jnp.zeros((11, 8, 128), F32)
+    b3_send[0] = restricted[:, 0:4]
+    b3_send[1] = b3[2:13, 2:6, :]
+    b3_copies = pass_rows_3(b3_send, b3_recv, b3_sems)
+
+    for copy in x0_copies:
+        copy.wait_recv()
+    y0_copies = send_y(2)
+    for copy in f3_copies:
+        copy.wait_recv()
+    f3[:, 2:14, 12:16, :] = f3_recv[0]
+    f3[:, 2:14, 6:10, :] = f3_recv[1]
     for low, high in chunks(2, 13, 6):
         terms = f3[0, low : high + 1]
         y_term, z_term = f3[1, low:high], f3[2, low:high]
@@ -599,39 +636,10 @@
             + (z_term + roll(z_term, -2, 2))
         )
 
-    for copy in x0_copies:
-        copy.wait_recv()
-    y0_copies = send_y(2)
-    for copy in gby_copies:
-        copy.wait_recv()
-    for s in range(count_y):
-        b2[:, 4 * s : 4 * s + 4, :] = g2b[s]
-
-    for i in range(15):
-        x2a[i] = inv2[i] * b2[i] * (1.0 / CENTER)
-
-    def step_2(old, new, low, high, step, before, after=None):
-        keep_old, keep_new = STEPS[step]
-
-        def emit(i, applied, here):
-            r = b2[i] - applied
-            d = keep_old * before[i] + keep_new * (inv2[i] * r)
-            if after is not None:
-                after[i] = d
-            new[i] = here + d
-
-        sweep_2(old, f2, low, high, emit)
-
-    step_2(x2a, x2b, 1, 14, 0, x2a, d2)
-    step_2(x2b, x2a, 1, 14, 1, d2)
-
-    def residual_2(i, applied, here):
-        r = b2[i] - applied
-        r = r + roll(r, 64, 1)
-        tmp2[0, i] = r + roll(r, -1, 1)
-
-    sweep_2(x2a, f2, 2, 13, residual_2)
-    b3[2:13] = 0.125 * (tmp2[0, 2:13, first16, :] + tmp2[0, 2:13, second16, :])
+    for copy in b3_copies:
+        copy.wait_recv()
+    b3[2:13, 12:16, :] = b3_recv[0]
+    b3[2:13, 6:10, :] = b3_recv[1]
 
     for i in range(2, 13):
         x3a[i] = inv3[i] * b3[i] * (1.0 / CENTER)
@@ -653,8 +661,9 @@
 
     e = x3a[4:11]
     e = jnp.where((lane_of(e.shape) & 1) == 0, e, roll(e, 1, 2))
-    dup2[4:11, first16, :] = e
-    dup2[4:11, second16, :] = e
+    e = roll(e, 2, 1)[:, 0:12]
+    dup2[4:11, pl.ds(0, 12, stride=2), :] = e
+    dup2[4:11, pl.ds(1, 12, stride=2), :] = e
     for i in range(4, 11):
         x2b[i] = x2a[i] + dup2[i]
     x2b[3] = x2a[3]
@@ -674,13 +683,13 @@
     def in_spread(row, column):
         return ((((column & 127) >> 1) + 16) & 63) + 64 * (column >> 7) == row
 
-    e = dot(x2a[5:10, 0:16, :].reshape(80, 128), select_matrix((128, 256), in_spread))
+    e = dot(x2a[5:10].reshape(120, 128), select_matrix((128, 256), in_spread))
     for p in range(2):
-        value = e[:, 128 * p : 128 * p + 128].reshape(5, 16, 128)
-        dup21[p, :, first16, :] = value
-        dup21[p, :, second16, :] = value
+        value = e[:, 128 * p : 128 * p + 128].reshape(5, 24, 128)
+        dup21[p, :, pl.ds(0, 24, stride=2), :] = value
+        dup21[p, :, pl.ds(1, 24, stride=2), :] = value
     for i in range(3, 17):
-        x1b[i] = x1a[i] + dup21[(i // 2) % 2, i // 4, 0:24, :]
+        x1b[i] = x1a[i] + dup21[(i // 2) % 2, i // 4, 8:32, :]
 
     def first_up_1(i, applied, here):
         d = inv1[i] * (b1[i] - applied) * (1.0 / CENTER)
@@ -729,12 +738,12 @@
 
 def solution(mesh):
     sizes = (mesh.shape["gx"], mesh.shape["gy"], mesh.shape["gz"])
-    count_x, count_y, _ = sizes
+    count_x = sizes[0]
     vmem = lambda *shape: pltpu.VMEM(shape, F32)
     sems = lambda count: pltpu.SemaphoreType.DMA((2, count))
     fine = (16, 2, 24, 128)
     level1 = (20, 24, 128)
-    level2 = (16, 32, 128)
+    level2 = (16, 24, 128)
     level3 = (16, 16, 128)
     scratch = [
         vmem(2, 8, 16, 128),
@@ -760,8 +769,9 @@
         vmem(*level1),
         vmem(3, 5, 8, 128),
         vmem(8, 48, 128),
-        vmem(count_y, count_x, 3, 4, 128),
-        vmem(count_y, count_x, 4, 128),
+        vmem(5, count_x, 3, 4, 128),
+        vmem(5, count_x, 4, 128),
+        vmem(count_x, 4, 128),
         vmem(3, *level2),
         vmem(*level2),
         vmem(*level2),
@@ -770,13 +780,17 @@
         vmem(*level2),
         vmem(3, *level2),
         vmem(3, *level3),
+        vmem(2, 3, 12, 4, 128),
+        vmem(2, 3, 12, 4, 128),
+        vmem(2, 11, 4, 128),
+        vmem(2, 11, 4, 128),
         vmem(*level3),
         vmem(*level3),
         vmem(*level3),
         vmem(*level3),
         vmem(*level3),
         vmem(*level2),
-        vmem(2, 5, 32, 128),
+        vmem(2, 5, 48, 128),
         pltpu.SemaphoreType.DMA((2,)),
         sems(4),
         sems(6),
@@ -787,9 +801,11 @@
         sems(4),
         sems(2),
         sems(2),
-        sems(2 * count_y),
+        sems(5),
         sems(4),
-        sems(count_y - 1),
+        sems(4),
+        sems(2),
+        sems(2),
     ]
 
     def shards(pressure_source, conductivity):

time: 54.4 us -> 58 us (1.066)
  Pallas kernels: 53.6 us -> 57.2 us
    pallas_call x1, Pallas kernels: 53.6 us -> 57.2 us  [shards(): pl.pallas_call(functools.partial(kernel, sizes), out_shape=jax.ShapeDtype...]
where the time goes in v8:
time: 58 us; the launch traced here: 57.9 us
  Pallas kernels  57.2 us (99%)
  local copies, waits for them, and re-layouts  0.63 us (1%)
    pallas_call x1, Pallas kernels, shards(): pl.pallas_call(functools.partial(kernel, sizes), out_shape=jax.ShapeDtype...  57.2 us

profile of v8, /device:TPU:1, one launch (start us, length us, event | category | flops | bytes accessed | tf_op | source)
XLA Modules:
  0.0 57.9 jit_solution(122437249898912407)
XLA Ops:
  0.0 57.2 %shard_map.28 = f32[8,16,128]{2,1,0:T(8,128)S(1)} custom-call(f32[8,16,128]{2,1,0:T(8,128)} %source_hbm.1, f32[8,16,128]{2,1,0:T(8,128)} %cond_hbm.1), custom_call_target="tpu_custom_call" | custom-call | tf_op jit(solution)/shard_map/pallas_call | solution.py:812
  57.2 0.6 %copy.4 = f32[8,16,128]{2,1,0:T(8,128)} copy(f32[8,16,128]{2,1,0:T(8,128)S(1)} %shard_map.28) | data formatting | bytes 131072

commit v9 on v7

--- a/solution.py
+++ b/solution.py
@@ -169,8 +169,7 @@
     xy_sems,
     f1x_sems,
     f1y_sems,
-    b1x_sems,
-    b1y_sems,
+    b1_sems,
     gfx_sems,
     gfy_sems,
     gbx_sems,
@@ -199,16 +198,16 @@
     partners = [at_z(1), at_z(-1)]
     partners += [at_x(sign * step) for step in (1, 2, 3, 5, 6) for sign in (1, -1)]
     partners += [at_y(step) for step in range(1, count_y)]
-    partners += [at_x(dx) | at_y(dy) for dx in (-1, 1) for dy in (-1, 1)]
+    partners += [at_x(dx) | at_y(dy) for dx in (-2, -1, 1, 2) for dy in (-1, 1)]
     for partner in partners:
         pl.semaphore_signal(barrier, inc=1, device_id=partner, device_id_type=MESH)
 
     pending = []
 
-    def drain():
-        for copy in pending:
+    def drain(count):
+        for copy in pending[:count]:
             copy.wait_send()
-        pending.clear()
+        del pending[:count]
 
     def send(source, target, sems, slot, device):
         copy = pltpu.make_async_remote_copy(
@@ -319,6 +318,7 @@
                     lane < 64, roll(mine, 64, 2) if t else mine, halo
                 )
         xy_copies.append(send_xy(f))
+    level_0_sends = len(pending)
 
     cond, source, best = win.at[0], win.at[1], win.at[2]
     faces0 = (fx, fy, fz)
@@ -359,6 +359,26 @@
         for slot, step in enumerate((-2, 2, -1, 1))
     ]
 
+    def send_f1_y(first, last, part):
+        return [
+            send(
+                f1.at[first:last, :, 8:16, :],
+                f1.at[first:last, :, 8 - 8 * step : 16 - 8 * step, :],
+                f1y_sems,
+                2 * part + slot,
+                at_y(step),
+            )
+            for slot, step in enumerate((-1, 1))
+        ]
+
+    f1y_copies = send_f1_y(8, 12, 0)
+    for i in (0, 19):
+        for tile in (slice(0, 8), slice(16, 24)):
+            f1[i, :, tile, :] = jnp.ones((3, 8, 128), F32)
+    for i in (1, 18):
+        for tile in (slice(0, 8), slice(16, 24)):
+            b1[i, tile, :] = jnp.zeros((8, 128), F32)
+
     def spread_x(ref, first, last, sems, steps):
         return [
             send(ref.at[1, first:last], ref.at[1, first - step : last - step], sems, slot, at_x(step))
@@ -452,32 +472,38 @@
 
     sweep_0(xa, faces0, 4, 12, residual_0)
     b1[8:12, 8:16, :] = 0.125 * (tmp0[0, :, first, :] + tmp0[0, :, second, :])
-    b1x_copies = [
+    b1_copies = [
         send(
             b1.at[first:last, 8:16, :],
-            b1.at[first - 4 * step : last - 4 * step, 8:16, :],
-            b1x_sems,
+            b1.at[first - 4 * dx : last - 4 * dx, 8 - 8 * dy : 16 - 8 * dy, :],
+            b1_sems,
             slot,
-            at_x(step),
+            (at_x(dx) if dx else {}) | (at_y(dy) if dy else {}),
         )
-        for slot, (step, first, last) in enumerate(
-            ((-2, 8, 11), (2, 9, 12), (-1, 8, 12), (1, 8, 12))
+        for slot, (dx, dy, first, last) in enumerate(
+            (
+                (-2, 0, 8, 11),
+                (2, 0, 9, 12),
+                (-2, -1, 8, 10),
+                (-2, 1, 8, 10),
+                (2, -1, 10, 12),
+                (2, 1, 10, 12),
+                (-1, 0, 8, 12),
+                (1, 0, 8, 12),
+                (-1, -1, 8, 12),
+                (-1, 1, 8, 12),
+                (1, -1, 8, 12),
+                (1, 1, 8, 12),
+                (0, -1, 8, 12),
+                (0, 1, 8, 12),
+            )
         )
     ]
 
 
     for copy in f1x_copies:
         copy.wait_recv()
-    f1y_copies = [
-        send(
-            f1.at[:, :, 8:16, :],
-            f1.at[:, :, 8 - 8 * step : 16 - 8 * step, :],
-            f1y_sems,
-            slot,
-            at_y(step),
-        )
-        for slot, step in enumerate((-1, 1))
-    ]
+    f1y_copies += send_f1_y(1, 8, 1) + send_f1_y(12, 19, 2)
 
     def in_pack(row, column):
         return ((((row & 127) >> 1) + 16) & 63) + 64 * (row >> 7) == column
@@ -506,19 +532,8 @@
     g2f[1, 5:10, 2] = 0.125 * (tmp1[2, :, first4, :] + tmp1[2, :, second4, :])
     gfx_copies = spread_x(g2f, 5, 10, gfx_sems, (5, -5))
 
-    drain()
-    for copy in b1x_copies:
-        copy.wait_recv()
-    b1y_copies = [
-        send(
-            b1.at[:, 8:16, :],
-            b1.at[:, 8 - 8 * step : 16 - 8 * step, :],
-            b1y_sems,
-            slot,
-            at_y(step),
-        )
-        for slot, step in enumerate((-1, 1))
-    ]
+    drain(level_0_sends)
+    level_1_sends = len(pending)
     for copy in f1y_copies:
         copy.wait_recv()
     for low, high in chunks(1, 19, 6):
@@ -527,7 +542,7 @@
         y_sum = y_term + roll(y_term, -1, 1)
         inv1[low:high] = 1.0 / ((x_sum + y_sum) + (z_term + roll(z_term, -1, 2)))
 
-    for copy in b1y_copies:
+    for copy in b1_copies:
         copy.wait_recv()
 
     for i in range(1, 19):
@@ -602,6 +617,7 @@
     for copy in x0_copies:
         copy.wait_recv()
     y0_copies = send_y(2)
+    drain(level_1_sends)
     for copy in gby_copies:
         copy.wait_recv()
     for s in range(count_y):
@@ -691,7 +707,7 @@
     step_1(x1a, x1b, 5, 15, 0, d1, d1)
     step_1(x1b, x1a, 6, 14, 1, d1)
 
-    drain()
+    drain(len(pending))
     place_y(2, y0_copies)
     e = x1a[6:14]
     dup1[:, pl.ds(0, 24, stride=2), :] = e
@@ -783,9 +799,8 @@
         sems(6),
         sems(12),
         sems(4),
-        sems(2),
-        sems(4),
-        sems(2),
+        sems(6),
+        sems(14),
         sems(2),
         sems(2 * count_y),
         sems(4),

time: 54.4 us -> 54.5 us (level)
  no operation moved by 1% of the time
where the time goes in v9:
time: 54.5 us; the launch traced here: 54.3 us
  Pallas kernels  53.7 us (99%)
  local copies, waits for them, and re-layouts  0.63 us (1%)
    pallas_call x1, Pallas kernels, shards(): pl.pallas_call(functools.partial(kernel, sizes), out_shape=jax.ShapeDtype...  53.7 us

profile of v9, /device:TPU:1, one launch (start us, length us, event | category | flops | bytes accessed | tf_op | source)
XLA Modules:
  0.0 54.3 jit_solution(6024598759500200263)
XLA Ops:
  0.0 53.7 %shard_map.28 = f32[8,16,128]{2,1,0:T(8,128)S(1)} custom-call(f32[8,16,128]{2,1,0:T(8,128)} %source_hbm.1, f32[8,16,128]{2,1,0:T(8,128)} %cond_hbm.1), custom_call_target="tpu_custom_call" | custom-call | tf_op jit(solution)/shard_map/pallas_call | solution.py:811
  53.7 0.6 %copy.4 = f32[8,16,128]{2,1,0:T(8,128)} copy(f32[8,16,128]{2,1,0:T(8,128)S(1)} %shard_map.28) | data formatting | bytes 131072

commit v10 on v7

--- a/solution.py
+++ b/solution.py
@@ -205,10 +205,10 @@
 
     pending = []
 
-    def drain():
-        for copy in pending:
+    def drain(count):
+        for copy in pending[:count]:
             copy.wait_send()
-        pending.clear()
+        del pending[:count]
 
     def send(source, target, sems, slot, device):
         copy = pltpu.make_async_remote_copy(
@@ -250,18 +250,25 @@
         )
         own[f] = dot(cells, keep).reshape(8, 16, 128)
 
+    for way in range(2):
+        for i in (0, 1, 14, 15):
+            y_recv[1, way, i] = jnp.zeros((2, 4, 128), F32)
+            if i in (0, 15):
+                y_recv[0, way, i] = jnp.ones((2, 4, 128), F32)
+
     def send_x(f):
+        depth = 4 if f == 0 else 3
         return [
             send(
-                win.at[f, 4:8, :, 0:16, :],
-                win.at[f, 12:16, :, 0:16, :],
+                win.at[f, 4 : 4 + depth, :, 0:16, :],
+                win.at[f, 12 : 12 + depth, :, 0:16, :],
                 x_sems,
                 2 * f,
                 at_x(-1),
             ),
             send(
-                win.at[f, 8:12, :, 0:16, :],
-                win.at[f, 0:4, :, 0:16, :],
+                win.at[f, 12 - depth : 12, :, 0:16, :],
+                win.at[f, 4 - depth : 4, :, 0:16, :],
                 x_sems,
                 2 * f + 1,
                 at_x(1),
@@ -272,16 +279,25 @@
         y_send[f, 0] = win[f, :, :, 0:4, :]
         y_send[f, 1] = win[f, :, :, 12:16, :]
         return [
-            send(y_send.at[f, way], y_recv.at[f, way], y_sems, 2 * f + way, at_y((-1, 1)[way]))
+            send(
+                y_send.at[f, way, 1:15],
+                y_recv.at[f, way, 1:15],
+                y_sems,
+                2 * f + way,
+                at_y((-1, 1)[way]),
+            )
             for way in range(2)
         ]
 
     def send_xy(f):
+        depth = 3 - f
         copies = send_x(f)
         y_send[f, 0, 4:12] = win[f, 4:12, :, 0:4, :]
         y_send[f, 1, 4:12] = win[f, 4:12, :, 12:16, :]
         for way in range(2):
-            for slot, (dx, first, last) in enumerate(((0, 4, 12), (1, 8, 12), (-1, 4, 8))):
+            for slot, (dx, first, last) in enumerate(
+                ((1, 12 - depth, 12), (-1, 4, 4 + depth), (0, 4, 12))
+            ):
                 copies.append(
                     send(
                         y_send.at[f, way, first:last],
@@ -319,6 +335,7 @@
                     lane < 64, roll(mine, 64, 2) if t else mine, halo
                 )
         xy_copies.append(send_xy(f))
+    level_0_sends = len(pending)
 
     cond, source, best = win.at[0], win.at[1], win.at[2]
     faces0 = (fx, fy, fz)
@@ -359,6 +376,23 @@
         for slot, step in enumerate((-2, 2, -1, 1))
     ]
 
+    def send_f1_y(first, last, part):
+        return [
+            send(
+                f1.at[first:last, :, 8:16, :],
+                f1.at[first:last, :, 8 - 8 * step : 16 - 8 * step, :],
+                f1y_sems,
+                2 * part + slot,
+                at_y(step),
+            )
+            for slot, step in enumerate((-1, 1))
+        ]
+
+    f1y_copies = send_f1_y(8, 12, 0)
+    for i in (0, 19):
+        for tile in (slice(0, 8), slice(16, 24)):
+            f1[i, :, tile, :] = jnp.ones((3, 8, 128), F32)
+
     def spread_x(ref, first, last, sems, steps):
         return [
             send(ref.at[1, first:last], ref.at[1, first - step : last - step], sems, slot, at_x(step))
@@ -405,10 +439,15 @@
         }
         return far, [hand_on(ref, sems, 1)]
 
+    def put_faces_2(place):
+        for f in range(3):
+            f2[f, :, 4 * place : 4 * place + 4, :] = g2f[place, :, f]
+
     def hand_on_all(ref, sems, far, handed):
         for place, copy in far.items():
             copy.wait_recv()
             handed.append(hand_on(ref, sems, place))
+            put_faces_2(place)
 
     for low, high in chunks(1, 15, 2):
         x_sum = [fx[low:high, t] + fx[low + 1 : high + 1, t] for t in range(2)]
@@ -465,19 +504,9 @@
         )
     ]
 
-
     for copy in f1x_copies:
         copy.wait_recv()
-    f1y_copies = [
-        send(
-            f1.at[:, :, 8:16, :],
-            f1.at[:, :, 8 - 8 * step : 16 - 8 * step, :],
-            f1y_sems,
-            slot,
-            at_y(step),
-        )
-        for slot, step in enumerate((-1, 1))
-    ]
+    f1y_copies += send_f1_y(1, 8, 1) + send_f1_y(12, 19, 2)
 
     def in_pack(row, column):
         return ((((row & 127) >> 1) + 16) & 63) + 64 * (row >> 7) == column
@@ -506,13 +535,14 @@
     g2f[1, 5:10, 2] = 0.125 * (tmp1[2, :, first4, :] + tmp1[2, :, second4, :])
     gfx_copies = spread_x(g2f, 5, 10, gfx_sems, (5, -5))
 
-    drain()
+    drain(level_0_sends)
+    level_1_sends = len(pending)
     for copy in b1x_copies:
         copy.wait_recv()
     b1y_copies = [
         send(
-            b1.at[:, 8:16, :],
-            b1.at[:, 8 - 8 * step : 16 - 8 * step, :],
+            b1.at[1:19, 8:16, :],
+            b1.at[1:19, 8 - 8 * step : 16 - 8 * step, :],
             b1y_sems,
             slot,
             at_y(step),
@@ -566,12 +596,12 @@
         copy.wait_recv()
     gby_copies = gather_y(g2b, gby_sems)
 
+    put_faces_2(1)
     hand_on_all(g2f, gfy_sems, gfy_far, gfy_copies)
     for copy in gfy_copies:
         copy.wait_recv()
-    for f in range(3):
-        for s in range(count_y):
-            f2[f, :, 4 * s : 4 * s + 4, :] = g2f[s, :, f]
+    for s in range(0, count_y, 2):
+        put_faces_2(s)
     for low, high in chunks(0, 15, 3):
         terms = f2[0, low : high + 1]
         turned = roll(terms, 64, 2)
@@ -602,6 +632,7 @@
     for copy in x0_copies:
         copy.wait_recv()
     y0_copies = send_y(2)
+    drain(level_1_sends)
     for copy in gby_copies:
         copy.wait_recv()
     for s in range(count_y):
@@ -691,7 +722,7 @@
     step_1(x1a, x1b, 5, 15, 0, d1, d1)
     step_1(x1b, x1a, 6, 14, 1, d1)
 
-    drain()
+    drain(len(pending))
     place_y(2, y0_copies)
     e = x1a[6:14]
     dup1[:, pl.ds(0, 24, stride=2), :] = e
@@ -783,7 +814,7 @@
         sems(6),
         sems(12),
         sems(4),
-        sems(2),
+        sems(6),
         sems(4),
         sems(2),
         sems(2),

time: 54.4 us -> 54.3 us (level)
  no operation moved by 1% of the time
where the time goes in v10:
time: 54.3 us; the launch traced here: 54.1 us
  Pallas kernels  53.5 us (99%)
  local copies, waits for them, and re-layouts  0.63 us (1%)
    pallas_call x1, Pallas kernels, shards(): pl.pallas_call(functools.partial(kernel, sizes), out_shape=jax.ShapeDtype...  53.5 us

profile of v10, /device:TPU:1, one launch (start us, length us, event | category | flops | bytes accessed | tf_op | source)
XLA Modules:
  0.0 54.1 jit_solution(2008957077240080490)
XLA Ops:
  0.0 53.5 %shard_map.28 = f32[8,16,128]{2,1,0:T(8,128)S(1)} custom-call(f32[8,16,128]{2,1,0:T(8,128)} %source_hbm.1, f32[8,16,128]{2,1,0:T(8,128)} %cond_hbm.1), custom_call_target="tpu_custom_call" | custom-call | tf_op jit(solution)/shard_map/pallas_call | solution.py:827
  53.5 0.6 %copy.4 = f32[8,16,128]{2,1,0:T(8,128)} copy(f32[8,16,128]{2,1,0:T(8,128)S(1)} %shard_map.28) | data formatting | bytes 131072

commit v11 on v10

--- a/solution.py
+++ b/solution.py
@@ -197,7 +197,7 @@
 
     barrier = pltpu.get_barrier_semaphore()
     partners = [at_z(1), at_z(-1)]
-    partners += [at_x(sign * step) for step in (1, 2, 3, 5, 6) for sign in (1, -1)]
+    partners += [at_x(sign * step) for step in (1, 2, 3, 6) for sign in (1, -1)]
     partners += [at_y(step) for step in range(1, count_y)]
     partners += [at_x(dx) | at_y(dy) for dx in (-1, 1) for dy in (-1, 1)]
     for partner in partners:
@@ -367,13 +367,15 @@
     f1[8:12, 2, 8:16, :] = 0.125 * (tmp0[2, :, first, :] + tmp0[2, :, second, :])
     f1x_copies = [
         send(
-            f1.at[8:12, :, 8:16, :],
-            f1.at[8 - 4 * step : 12 - 4 * step, :, 8:16, :],
+            f1.at[first:last, :, 8:16, :],
+            f1.at[first - 4 * step : last - 4 * step, :, 8:16, :],
             f1x_sems,
             slot,
             at_x(step),
         )
-        for slot, step in enumerate((-2, 2, -1, 1))
+        for slot, (step, first, last) in enumerate(
+            ((-1, 8, 12), (1, 8, 12), (-2, 8, 12), (2, 9, 12))
+        )
     ]
 
     def send_f1_y(first, last, part):
@@ -479,6 +481,9 @@
 
     step_0(xa, xb, 2, 14, 0, xa, dd)
 
+    for copy in f1x_copies[:2]:
+        copy.wait_recv()
+    f1y_copies += send_f1_y(4, 8, 1) + send_f1_y(12, 16, 2)
     step_0(xb, xa, 3, 13, 1, dd)
     best[4:12, :, 0:16, :] = xa[4:12, :, 0:16, :]
     sums = []
@@ -504,10 +509,6 @@
         )
     ]
 
-    for copy in f1x_copies:
-        copy.wait_recv()
-    f1y_copies += send_f1_y(1, 8, 1) + send_f1_y(12, 19, 2)
-
     def in_pack(row, column):
         return ((((row & 127) >> 1) + 16) & 63) + 64 * (row >> 7) == column
 
@@ -523,17 +524,20 @@
     g2f[1, 15] = jnp.ones((3, 4, 128), F32)
     g2b[1, 15] = jnp.zeros((4, 128), F32)
     mine = slice(8, 16)
-    tmp1[0] = packed([[f1[4 * i + 2 * p, 0, mine, :] for i in range(5)] for p in range(2)], pack)
+    tmp1[0] = packed([[f1[4 * i + 2 * p, 0, mine, :] for i in (1, 2, 3)] for p in range(2)], pack)
     for f in (1, 2):
         pieces = [
-            [f1[4 * i + 2 * p, f, mine, :] + f1[4 * i + 2 * p + 1, f, mine, :] for i in range(5)]
+            [f1[4 * i + 2 * p, f, mine, :] + f1[4 * i + 2 * p + 1, f, mine, :] for i in (1, 2, 3)]
             for p in range(2)
         ]
         tmp1[f] = packed(pieces, (None, pack, pack_even)[f])
-    g2f[1, 5:10, 0] = 0.125 * (tmp1[0, :, first4, :] + tmp1[0, :, second4, :])
-    g2f[1, 5:10, 1] = 0.125 * tmp1[1, :, first4, :]
-    g2f[1, 5:10, 2] = 0.125 * (tmp1[2, :, first4, :] + tmp1[2, :, second4, :])
-    gfx_copies = spread_x(g2f, 5, 10, gfx_sems, (5, -5))
+    g2f[1, 6:9, 0] = 0.125 * (tmp1[0, :, first4, :] + tmp1[0, :, second4, :])
+    g2f[1, 6:9, 1] = 0.125 * tmp1[1, :, first4, :]
+    g2f[1, 6:9, 2] = 0.125 * (tmp1[2, :, first4, :] + tmp1[2, :, second4, :])
+    gfx_copies = spread_x(g2f, 6, 9, gfx_sems, (6, -6, 3, -3))
+    for copy in f1x_copies[2:]:
+        copy.wait_recv()
+    f1y_copies += send_f1_y(1, 4, 3) + send_f1_y(16, 19, 4)
 
     drain(level_0_sends)
     level_1_sends = len(pending)
@@ -586,10 +590,10 @@
         r[i - 4] = (b1[i] - applied)[8:16]
 
     sweep_1(x1a, f1, 4, 16, residual_1)
-    tmp1[0, 0:3] = packed(
+    tmp1[0] = packed(
         [[r[4 * i + 2 * p] + r[4 * i + 2 * p + 1] for i in range(3)] for p in range(2)], pack
     )
-    g2b[1, 6:9] = 0.125 * (tmp1[0, 0:3, first4, :] + tmp1[0, 0:3, second4, :])
+    g2b[1, 6:9] = 0.125 * (tmp1[0, :, first4, :] + tmp1[0, :, second4, :])
     gbx_copies = spread_x(g2b, 6, 9, gbx_sems, (6, -6, 3, -3))
     x0_copies = send_x(2)
     for copy in gbx_copies:
@@ -789,7 +793,7 @@
         vmem(*level1),
         vmem(*level1),
         vmem(*level1),
-        vmem(3, 5, 8, 128),
+        vmem(3, 3, 8, 128),
         vmem(8, 48, 128),
         vmem(count_y, count_x, 3, 4, 128),
         vmem(count_y, count_x, 4, 128),
@@ -814,10 +818,10 @@
         sems(6),
         sems(12),
         sems(4),
-        sems(6),
+        sems(10),
         sems(4),
         sems(2),
-        sems(2),
+        sems(4),
         sems(2 * count_y),
         sems(4),
         sems(count_y - 1),

time: 54.3 us -> 55 us (1.013)
  Pallas kernels: 53.5 us -> 54.2 us
    pallas_call x1, Pallas kernels: 53.5 us -> 54.2 us  [shards(): pl.pallas_call(functools.partial(kernel, sizes), out_shape=jax.ShapeDtype...]
where the time goes in v11:
time: 55 us; the launch traced here: 54.8 us
  Pallas kernels  54.2 us (99%)
  local copies, waits for them, and re-layouts  0.63 us (1%)
    pallas_call x1, Pallas kernels, shards(): pl.pallas_call(functools.partial(kernel, sizes), out_shape=jax.ShapeDtype...  54.2 us

profile of v11, /device:TPU:1, one launch (start us, length us, event | category | flops | bytes accessed | tf_op | source)
XLA Modules:
  0.0 54.8 jit_solution(7071528039082749829)
XLA Ops:
  0.0 54.2 %shard_map.28 = f32[8,16,128]{2,1,0:T(8,128)S(1)} custom-call(f32[8,16,128]{2,1,0:T(8,128)} %source_hbm.1, f32[8,16,128]{2,1,0:T(8,128)} %cond_hbm.1), custom_call_target="tpu_custom_call" | custom-call | tf_op jit(solution)/shard_map/pallas_call | solution.py:831
  54.2 0.6 %copy.4 = f32[8,16,128]{2,1,0:T(8,128)} copy(f32[8,16,128]{2,1,0:T(8,128)S(1)} %shard_map.28) | data formatting | bytes 131072

commit v12 on v10

--- a/solution.py
+++ b/solution.py
@@ -251,10 +251,9 @@
         own[f] = dot(cells, keep).reshape(8, 16, 128)
 
     for way in range(2):
-        for i in (0, 1, 14, 15):
+        for i in (0, 15):
+            y_recv[0, way, i] = jnp.ones((2, 4, 128), F32)
             y_recv[1, way, i] = jnp.zeros((2, 4, 128), F32)
-            if i in (0, 15):
-                y_recv[0, way, i] = jnp.ones((2, 4, 128), F32)
 
     def send_x(f):
         depth = 4 if f == 0 else 3
@@ -290,30 +289,37 @@
         ]
 
     def send_xy(f):
-        depth = 3 - f
         copies = send_x(f)
         y_send[f, 0, 4:12] = win[f, 4:12, :, 0:4, :]
         y_send[f, 1, 4:12] = win[f, 4:12, :, 12:16, :]
         for way in range(2):
-            for slot, (dx, first, last) in enumerate(
-                ((1, 12 - depth, 12), (-1, 4, 4 + depth), (0, 4, 12))
-            ):
-                copies.append(
-                    send(
-                        y_send.at[f, way, first:last],
-                        y_recv.at[f, way, first - 8 * dx : last - 8 * dx],
-                        xy_sems,
-                        6 * f + 3 * way + slot,
-                        at_y((-1, 1)[way]) | (at_x(dx) if dx else {}),
-                    )
+            copies.append(
+                send(
+                    y_send.at[f, way, 4:12],
+                    y_recv.at[f, way, 4:12],
+                    xy_sems,
+                    2 * f + way,
+                    at_y((-1, 1)[way]),
                 )
+            )
         return copies
 
-    def place_y(f, copies):
-        for copy in copies:
-            copy.wait_recv()
-        win[f, :, :, 16:20, :] = y_recv[f, 0]
-        win[f, :, :, 20:24, :] = y_recv[f, 1]
+    def send_corners():
+        return [
+            send(
+                y_send.at[0:2, way, first:last],
+                y_recv.at[0:2, way, first - 8 * dx : last - 8 * dx],
+                xy_sems,
+                4 + 2 * way + slot,
+                at_y((-1, 1)[way]) | at_x(dx),
+            )
+            for way in range(2)
+            for slot, (dx, first, last) in enumerate(((1, 9, 12), (-1, 4, 7)))
+        ]
+
+    def place_y(f, first, last):
+        win[f, first:last, :, 16:20, :] = y_recv[f, 0, first:last]
+        win[f, first:last, :, 20:24, :] = y_recv[f, 1, first:last]
 
     xy_copies = []
     for f in range(2):
@@ -335,6 +341,7 @@
                     lane < 64, roll(mine, 64, 2) if t else mine, halo
                 )
         xy_copies.append(send_xy(f))
+    corners = send_corners()
     level_0_sends = len(pending)
 
     cond, source, best = win.at[0], win.at[1], win.at[2]
@@ -347,7 +354,9 @@
         if i > 4:
             fx[i, 0, brick, :] = harmonic(k0, cond[i - 1, 0, brick, :])
             fx[i, 1, brick, :] = harmonic(k1, cond[i - 1, 1, brick, :])
-    place_y(0, xy_copies[0])
+    for copy in xy_copies[0]:
+        copy.wait_recv()
+    place_y(0, 4, 12)
     for t in range(2):
         fx[4, t, brick, :] = harmonic(cond[4, t, brick, :], cond[3, t, brick, :])
     for i in range(4, 12):
@@ -376,19 +385,6 @@
         for slot, step in enumerate((-2, 2, -1, 1))
     ]
 
-    def send_f1_y(first, last, part):
-        return [
-            send(
-                f1.at[first:last, :, 8:16, :],
-                f1.at[first:last, :, 8 - 8 * step : 16 - 8 * step, :],
-                f1y_sems,
-                2 * part + slot,
-                at_y(step),
-            )
-            for slot, step in enumerate((-1, 1))
-        ]
-
-    f1y_copies = send_f1_y(8, 12, 0)
     for i in (0, 19):
         for tile in (slice(0, 8), slice(16, 24)):
             f1[i, :, tile, :] = jnp.ones((3, 8, 128), F32)
@@ -405,6 +401,10 @@
             for step in sorted(range(1, count_y), key=lambda step: abs(step - count_y // 2))
         ]
 
+    for copy in corners:
+        copy.wait_recv()
+    place_y(0, 0, 4)
+    place_y(0, 12, 16)
     for i in range(1, 16):
         part = slice(16, 24) if 4 <= i < 12 else slice(0, 24)
         for t in range(2):
@@ -456,7 +456,9 @@
         inv[low:high, 0] = 1.0 / ((x_sum[0] + y_sum[0]) + (z0 + z1))
         inv[low:high, 1] = 1.0 / ((x_sum[1] + y_sum[1]) + (z1 + roll(z0, -1, 2)))
 
-    place_y(1, xy_copies[1])
+    for copy in xy_copies[1]:
+        copy.wait_recv()
+    place_y(1, 0, 16)
     for i in range(1, 15):
         for t in range(2):
             xa[i, t] = inv[i, t] * source[i, t] * (1.0 / CENTER)
@@ -506,7 +508,16 @@
 
     for copy in f1x_copies:
         copy.wait_recv()
-    f1y_copies += send_f1_y(1, 8, 1) + send_f1_y(12, 19, 2)
+    f1y_copies = [
+        send(
+            f1.at[1:19, :, 8:16, :],
+            f1.at[1:19, :, 8 - 8 * step : 16 - 8 * step, :],
+            f1y_sems,
+            slot,
+            at_y(step),
+        )
+        for slot, step in enumerate((-1, 1))
+    ]
 
     def in_pack(row, column):
         return ((((row & 127) >> 1) + 16) & 63) + 64 * (row >> 7) == column
@@ -723,7 +734,9 @@
     step_1(x1b, x1a, 6, 14, 1, d1)
 
     drain(len(pending))
-    place_y(2, y0_copies)
+    for copy in y0_copies:
+        copy.wait_recv()
+    place_y(2, 0, 16)
     e = x1a[6:14]
     dup1[:, pl.ds(0, 24, stride=2), :] = e
     dup1[:, pl.ds(1, 24, stride=2), :] = e
@@ -812,9 +825,9 @@
         sems(4),
         sems(6),
         sems(6),
-        sems(12),
+        sems(8),
         sems(4),
-        sems(6),
+        sems(2),
         sems(4),
         sems(2),
         sems(2),

time: 54.3 us -> 54.1 us (level)
  no operation moved by 1% of the time
where the time goes in v12:
time: 54.1 us; the launch traced here: 54 us
  Pallas kernels  53.3 us (99%)
  local copies, waits for them, and re-layouts  0.63 us (1%)
    pallas_call x1, Pallas kernels, shards(): pl.pallas_call(functools.partial(kernel, sizes), out_shape=jax.ShapeDtype...  53.3 us

profile of v12, /device:TPU:1, one launch (start us, length us, event | category | flops | bytes accessed | tf_op | source)
XLA Modules:
  0.0 54.0 jit_solution(224989106993462999)
XLA Ops:
  0.0 53.3 %shard_map.28 = f32[8,16,128]{2,1,0:T(8,128)S(1)} custom-call(f32[8,16,128]{2,1,0:T(8,128)} %source_hbm.1, f32[8,16,128]{2,1,0:T(8,128)} %cond_hbm.1), custom_call_target="tpu_custom_call" | custom-call | tf_op jit(solution)/shard_map/pallas_call | solution.py:840
  53.3 0.6 %copy.4 = f32[8,16,128]{2,1,0:T(8,128)} copy(f32[8,16,128]{2,1,0:T(8,128)S(1)} %shard_map.28) | data formatting | bytes 131072

commit v13 on v12

--- a/solution.py
+++ b/solution.py
@@ -248,7 +248,9 @@
                 for way in range(2)
             ]
         )
-        own[f] = dot(cells, keep).reshape(8, 16, 128)
+
+    for f in range(2):
+        own[f] = dot(staged[f].reshape(128, 128), keep).reshape(8, 16, 128)
 
     for way in range(2):
         for i in (0, 15):

time: 54.1 us -> 54.1 us (level)
  no operation moved by 1% of the time
where the time goes in v13:
time: 54.1 us; the launch traced here: 54 us
  Pallas kernels  53.3 us (99%)
  local copies, waits for them, and re-layouts  0.63 us (1%)
    pallas_call x1, Pallas kernels, shards(): pl.pallas_call(functools.partial(kernel, sizes), out_shape=jax.ShapeDtype...  53.3 us

profile of v13, /device:TPU:1, one launch (start us, length us, event | category | flops | bytes accessed | tf_op | source)
XLA Modules:
  0.0 54.0 jit_solution(1530709329405963897)
XLA Ops:
  0.0 53.3 %shard_map.28 = f32[8,16,128]{2,1,0:T(8,128)S(1)} custom-call(f32[8,16,128]{2,1,0:T(8,128)} %source_hbm.1, f32[8,16,128]{2,1,0:T(8,128)} %cond_hbm.1), custom_call_target="tpu_custom_call" | custom-call | tf_op jit(solution)/shard_map/pallas_call | solution.py:842
  53.3 0.6 %copy.4 = f32[8,16,128]{2,1,0:T(8,128)} copy(f32[8,16,128]{2,1,0:T(8,128)S(1)} %shard_map.28) | data formatting | bytes 131072
